TPU v7x, 128 devices: a whole 4x4x4 slice. The times are simulated.
128 devices in a mesh: lon: 16 (over x, z_lo, core), mem: 8 (over z_hi, y).
Axes of the slice: x: 4, y: 4, z: 4 (z_hi: 2, z_lo: 2; z = z_hi * 2 + z_lo), core: 2. Of those that a mesh axis runs over, the one named last changes fastest.
Arguments:
- inputs: bfloat16 [8, 2, 96, 192, 192], P('mem', None, None, 'lon'), may hold values from -6 to 6
- target: bfloat16 [2, 96, 192, 192], P(None, None, 'lon'), may hold values from -8 to 8
- norm_gain_vector: float32 [192], replicated, may hold values from 0.1 to 1.9
- w_qkv: bfloat16 [192, 576], replicated, may hold values from -0.4375 to 0.4375
- w_proj: bfloat16 [192, 192], replicated, may hold values from -0.4375 to 0.4375
- lat_region: int32 [96], replicated, may hold values from 0 to 31, never falling along the last dimension, each value on 1 to 6 neighbouring positions
- lat_valid: int32 [96], replicated, may hold values 0 or 1
Outputs:
- grad_inputs: bfloat16 [8, 2, 96, 192, 192], P('mem', None, None, 'lon')
- grad_qkv: float32 [192, 576], replicated
- grad_proj: float32 [192, 192], replicated
- grad_gain: float32 [192], replicated
- loss: float32 [], replicated
Inputs may be any that keep to these rules, and one draw needn't show every extreme that they name: `lat_region`: never falls along the rows; each value covers 1 to 6 consecutive rows, and every value of the range occurs.
All inputs are finite; a program needn't handle non-finite values.
Results may differ from a plain program's by a relative error of at most 0.015.
Values may be sent and summed in bfloat16 or wider, within the bound.
No kernel may reach another device: no remote copies, remote signals or barrier semaphores. Data moves between devices by JAX's collectives and lax.ppermute only.
A program may use at most 128 MiB of HBM per device.

v0:
```python
import jax
import jax.numpy as jnp
from jax import lax
from jax.sharding import PartitionSpec as P

HEADS = 6
SHIFT = 6


EPS = 1e-05
DELTA_SQ = 0.0625


def from_behind(array, axis, by):
    devices = lax.axis_size(axis)
    return lax.ppermute(array, axis, [(i, (i + by) % devices) for i in range(devices)])


def to_windows(field):
    levels, rows, columns, width = field.shape
    field = field.reshape(levels // 2, 2, rows // 6, 6, columns // 12, 12, width)
    field = field.transpose(0, 2, 4, 1, 3, 5, 6)
    return field.reshape(levels // 2, rows // 6, columns // 12, 144, width)


def from_windows(field, levels, rows, columns):
    width = field.shape[-1]
    field = field.reshape(levels // 2, rows // 6, columns // 12, 2, 6, 12, width)
    field = field.transpose(0, 3, 1, 4, 2, 5, 6)
    return field.reshape(levels, rows, columns, width)


def window_mask(lat_region, lat_valid):
    blocks = lat_region.shape[0] // 6
    region = jnp.broadcast_to(lat_region.reshape(blocks, 1, 6, 1), (blocks, 2, 6, 12)).reshape(
        blocks, 144
    )
    valid = jnp.broadcast_to(lat_valid.reshape(blocks, 1, 6, 1), (blocks, 2, 6, 12)).reshape(
        blocks, 144
    )
    same = region[:, :, None] == region[:, None, :]
    itself = jnp.arange(144)[:, None] == jnp.arange(144)[None, :]
    return same & ((valid[:, None, :] == 1) | itself[None])


def batched(spec, left, right):
    return jnp.einsum(spec, left, right, preferred_element_type=jnp.float32)


def split_heads(field):
    first, second, cells, width = field.shape
    return field.reshape(first, second, cells, HEADS, width // HEADS).transpose(0, 1, 3, 2, 4)


def merge_heads(field):
    first, second, heads, cells, size = field.shape
    return field.transpose(0, 1, 3, 2, 4).reshape(first, second, cells, heads * size)


def weights_of(query, keys, mask):
    scale = query.shape[-1] ** (-0.5)
    scores = batched("abhqd,abhkd->abhqk", query, keys) * scale
    scores = jnp.where(mask[:, None, None], scores, -1e30)
    expo = jnp.exp(scores)
    return expo / jnp.sum(expo, axis=-1, keepdims=True)


def forward_block(block, w_qkv, mask):
    width = block.shape[-1]
    qkv = jnp.dot(block, w_qkv, preferred_element_type=jnp.float32).astype(jnp.bfloat16)
    query = split_heads(qkv[..., :width])
    keys = split_heads(qkv[..., width : 2 * width])
    value_rows = split_heads(qkv[..., 2 * width :])
    probs = weights_of(query, keys, mask).astype(jnp.bfloat16)
    attended = batched("abhqk,abhkd->abhqd", probs, value_rows).astype(jnp.bfloat16)
    return (qkv, merge_heads(attended))


def backward_block(block, qkv, attended, grad_rows, w_qkv, w_proj, mask):
    width = block.shape[-1]
    query = split_heads(qkv[..., :width])
    keys = split_heads(qkv[..., width : 2 * width])
    value_rows = split_heads(qkv[..., 2 * width :])
    scale = query.shape[-1] ** (-0.5)
    weights = weights_of(query, keys, mask)
    probs = weights.astype(jnp.bfloat16)
    grad_att = split_heads(
        jnp.dot(grad_rows, w_proj.T, preferred_element_type=jnp.float32).astype(jnp.bfloat16)
    )
    grad_probs = batched("abhqd,abhkd->abhqk", grad_att, value_rows)
    total = jnp.sum(weights * grad_probs, axis=-1, keepdims=True)
    grad_scores = (weights * (grad_probs - total) * scale).astype(jnp.bfloat16)
    grad_query = batched("abhqk,abhkd->abhqd", grad_scores, keys)
    grad_keys = batched("abhqk,abhqd->abhkd", grad_scores, query)
    grad_values = batched("abhqk,abhqd->abhkd", probs, grad_att)
    grad_qkv = jnp.concatenate(
        [merge_heads(grad_query), merge_heads(grad_keys), merge_heads(grad_values)], axis=-1
    ).astype(jnp.bfloat16)
    qkv_part = jnp.dot(
        block.reshape(-1, width).T,
        grad_qkv.reshape(-1, 3 * width),
        preferred_element_type=jnp.float32,
    )
    proj_part = jnp.dot(
        attended.reshape(-1, width).T,
        grad_rows.reshape(-1, width),
        preferred_element_type=jnp.float32,
    )
    grad_block = jnp.dot(grad_qkv, w_qkv.T, preferred_element_type=jnp.float32).astype(jnp.bfloat16)
    return (grad_block, qkv_part, proj_part)


def layer_normalize(inputs, gain_vector):
    value_rows = inputs.astype(jnp.float32)
    mean_removed = value_rows - jnp.mean(value_rows, axis=-1, keepdims=True)
    inverse_deviation = lax.rsqrt(
        jnp.mean(mean_removed * mean_removed, axis=-1, keepdims=True) + EPS
    )
    standardized_input = mean_removed * inverse_deviation
    return (
        value_rows,
        standardized_input,
        inverse_deviation,
        (standardized_input * gain_vector).astype(jnp.bfloat16),
    )


def attend_grid(rolled, w_qkv, w_proj, mask):
    levels, rows, columns, width = rolled.shape
    windows = to_windows(rolled)
    qkv, attended = lax.map(lambda block: forward_block(block, w_qkv, mask), windows)
    proj = jnp.dot(attended, w_proj, preferred_element_type=jnp.float32).astype(jnp.bfloat16)
    return (windows, qkv, attended, from_windows(proj, levels, rows, columns))


def backward_grid(windows, qkv, attended, grad_rolled, w_qkv, w_proj, mask):
    levels, rows, columns, width = grad_rolled.shape
    grad_windows = to_windows(grad_rolled)
    grad_blocks, qkv_parts, proj_parts = lax.map(
        lambda items: backward_block(items[0], items[1], items[2], items[3], w_qkv, w_proj, mask),
        (windows, qkv, attended, grad_windows),
    )
    return (
        from_windows(grad_blocks, levels, rows, columns),
        jnp.sum(qkv_parts, axis=0),
        jnp.sum(proj_parts, axis=0),
    )


def smooth(diff):
    return jnp.sqrt(diff * diff + DELTA_SQ)


def lead_roll(field):
    arriving = from_behind(field[:, :, :SHIFT], "lon", -1)
    return jnp.concatenate([field[:, :, SHIFT:], arriving], axis=2)


def trail_roll(field):
    arriving = from_behind(field[:, :, -SHIFT:], "lon", 1)
    return jnp.concatenate([arriving, field[:, :, :-SHIFT]], axis=2)


def body(inputs, target, norm_gain_vector, w_qkv, w_proj, lat_region, lat_valid):
    members = lax.axis_size("mem")
    strips = lax.axis_size("lon")
    local_piece = inputs[0]
    levels, rows, columns, width = local_piece.shape
    mask = window_mask(lat_region, lat_valid)
    value_rows, standardized_input, inverse_deviation, normalized_rows = layer_normalize(
        local_piece, norm_gain_vector
    )
    rolled = lead_roll(normalized_rows)
    windows, qkv, attended, proj = attend_grid(rolled, w_qkv, w_proj, mask)
    mixed = value_rows + trail_roll(proj).astype(jnp.float32)
    rounded = lax.optimization_barrier(mixed.astype(jnp.bfloat16))
    own = rounded.astype(jnp.float32)
    valid = lat_valid.astype(jnp.float32).reshape(1, rows, 1, 1)
    zeros = jnp.zeros_like(own)

    def step(inner, other):
        diff = own - other.astype(jnp.float32)
        size = smooth(diff)
        return ((inner[0] + size, inner[1] + diff / size), None)

    result, unused = lax.scan(
        step, (zeros, zeros), lax.all_gather(rounded[None], "mem", axis=0, tiled=True)
    )
    pairs, slopes = result
    pair_score = jnp.sum(valid * pairs)
    diff = mixed - target.astype(jnp.float32)
    size = smooth(diff)
    grad_mixed = valid * (diff / size - slopes / members)
    score = jnp.sum(valid * size) - pair_score / (2.0 * members)
    grad_rolled = lead_roll(grad_mixed.astype(jnp.bfloat16))
    grad_back, qkv_part, proj_part = backward_grid(
        windows, qkv, attended, grad_rolled, w_qkv, w_proj, mask
    )
    gradient_normalized = trail_roll(grad_back).astype(jnp.float32)
    gain_partial = jnp.sum(gradient_normalized * standardized_input, axis=(0, 1, 2))
    scaled_rows = gradient_normalized * norm_gain_vector
    gradient_input = inverse_deviation * (
        scaled_rows
        - jnp.mean(scaled_rows, axis=-1, keepdims=True)
        - standardized_input * jnp.mean(scaled_rows * standardized_input, axis=-1, keepdims=True)
    )
    grad_inputs = (grad_mixed + gradient_input).astype(jnp.bfloat16)[None]
    qkv_sum, proj_sum, gain_sum, score_sum = lax.psum(
        (qkv_part, proj_part, gain_partial, score), ("lon", "mem")
    )
    count = members * levels * rows * columns * strips
    scale = count ** (-0.5)
    loss = score_sum / (count * width)
    return (grad_inputs, qkv_sum * scale, proj_sum * scale, gain_sum * scale, loss)


def solution(mesh):
    in_specs = (
        P("mem", None, None, "lon", None),
        P(None, None, "lon", None),
        P(),
        P(),
        P(),
        P(),
        P(),
    )
    out_specs = (P("mem", None, None, "lon", None), P(), P(), P(), P())
    return jax.shard_map(body, mesh=mesh, in_specs=in_specs, out_specs=out_specs, check_vma=False)
```

profile of v0, /device:TPU:0, one launch (start us, length us, event | category | flops | bytes accessed | tf_op | source)
XLA Modules:
  0.0 644.3 jit_solution(11454291910575370867)
XLA Ops:
  7.2 2.7 convert_reduce_fusion
  10.1 3.9 fusion.35
  15.0 3.1 multiply_convert_fusion.1
  18.9 3.9 collective-permute-start
  23.5 2.0 or_and_fusion
  25.5 4.8 collective-permute-done
  34.4 2.1 fusion.82
  38.2 1.8 copy.70
  40.0 3.1 copy.68
  43.1 5.8 fusion.5
  49.0 4.1 fusion.46
  57.5 11.6 %collective-permute-done.1 = bf16[2,96,6,192]{3,0,2,1:T(2,128)(2,1)S(1)} collective-permute-done((bf16[2,96,6,192]{3,0,2,1:T(2,128)(2,1)S(1)}, bf16[2,96,6,192]{3,0,2,1:T(2,128)(2,1)S(1)}, u32[]{:S(2)}, u32[]{:S(2)}) %collective-permute-start.1) | collective-permute-done | bytes 442400 | tf_op jit(solution)/shard_map/ppermute | solution.py:16
  69.1 4.7 fusion.45
  77.9 116.5 %all-gather.3.cloned.1.call-done = bf16[16,96,12,192]{3,1,2,0:T(8,128)(2,1)} async-done(((bf16[2,96,12,192]{3,1,2,0:T(8,128)(2,1)}), bf16[16,96,12,192]{3,1,2,0:T(8,128)(2,1)}) %all-gather.3.cloned.1.call-update) | async-done | bytes 7077904 | tf_op jit(solution)/shard_map/all_gather | solution.py:187
  194.4 69.6 %while.3 = (s32[]{:T(128)}, f32[2,96,12,192]{3,2,1,0:T(8,128)}, f32[2,96,12,192]{3,2,1,0:T(8,128)}, bf16[8,2,96,12,192]{4,2,3,1,0:T(8,128)(2,1)}, f32[2,96,12,192]{3,2,1,0:T(8,128)S(1)}, /*index=5*/s32[]{:T(128)}, s32[]{:T(128)}) while((s32[]{:T(128)}, f32[2,96,12,192]{3,2,1,0:T(8,128)}, f32[2,96,12,192]{3,2,1,0:T(8,128)}, ...), condition=%wide.region_4.5_spmd.clone, body=%wide.region_3.4_spmd.clone.sunk | while | flops 3981315 | bytes 11501667 | solution.py:186
  195.7 4.9 select_add_fusion.3
  202.0 7.7 %select_add_fusion.3 = (f32[2,96,12,192]{3,2,1,0:T(8,128)}, f32[2,96,12,192]{3,2,1,0:T(8,128)}) fusion(f32[2,96,12,192]{3,2,1,0:T(8,128)} %get-tuple-element.211, f32[2,96,12,192]{3,2,1,0:T(8,128)S(1)} %get-tuple-element.220, bf16[1,2,96,12,192]{4,2,3,1,0:T(8,128)(2,1)S(1)} %constant_dynamic-slice_fusion.2, pred[]{:T(512)S(6)} %compare.3, ...), kind=kLoop, calls=%fused_computation.1.clone.1 | loop fusion | flops 3981312 | bytes 9732097 | tf_op jit(solution)/shard_map/while/body/eval_jaxpr/add | solution.py:184
  211.0 7.7 %select_add_fusion.3 = (f32[2,96,12,192]{3,2,1,0:T(8,128)}, f32[2,96,12,192]{3,2,1,0:T(8,128)}) fusion(f32[2,96,12,192]{3,2,1,0:T(8,128)} %get-tuple-element.211, f32[2,96,12,192]{3,2,1,0:T(8,128)S(1)} %get-tuple-element.220, bf16[1,2,96,12,192]{4,2,3,1,0:T(8,128)(2,1)S(1)} %constant_dynamic-slice_fusion.2, pred[]{:T(512)S(6)} %compare.3, ...), kind=kLoop, calls=%fused_computation.1.clone.1 | loop fusion | flops 3981312 | bytes 9732097 | tf_op jit(solution)/shard_map/while/body/eval_jaxpr/add | solution.py:184
  220.1 7.7 %select_add_fusion.3 = (f32[2,96,12,192]{3,2,1,0:T(8,128)}, f32[2,96,12,192]{3,2,1,0:T(8,128)}) fusion(f32[2,96,12,192]{3,2,1,0:T(8,128)} %get-tuple-element.211, f32[2,96,12,192]{3,2,1,0:T(8,128)S(1)} %get-tuple-element.220, bf16[1,2,96,12,192]{4,2,3,1,0:T(8,128)(2,1)S(1)} %constant_dynamic-slice_fusion.2, pred[]{:T(512)S(6)} %compare.3, ...), kind=kLoop, calls=%fused_computation.1.clone.1 | loop fusion | flops 3981312 | bytes 9732097 | tf_op jit(solution)/shard_map/while/body/eval_jaxpr/add | solution.py:184
  229.1 7.7 %select_add_fusion.3 = (f32[2,96,12,192]{3,2,1,0:T(8,128)}, f32[2,96,12,192]{3,2,1,0:T(8,128)}) fusion(f32[2,96,12,192]{3,2,1,0:T(8,128)} %get-tuple-element.211, f32[2,96,12,192]{3,2,1,0:T(8,128)S(1)} %get-tuple-element.220, bf16[1,2,96,12,192]{4,2,3,1,0:T(8,128)(2,1)S(1)} %constant_dynamic-slice_fusion.2, pred[]{:T(512)S(6)} %compare.3, ...), kind=kLoop, calls=%fused_computation.1.clone.1 | loop fusion | flops 3981312 | bytes 9732097 | tf_op jit(solution)/shard_map/while/body/eval_jaxpr/add | solution.py:184
  238.2 7.7 %select_add_fusion.3 = (f32[2,96,12,192]{3,2,1,0:T(8,128)}, f32[2,96,12,192]{3,2,1,0:T(8,128)}) fusion(f32[2,96,12,192]{3,2,1,0:T(8,128)} %get-tuple-element.211, f32[2,96,12,192]{3,2,1,0:T(8,128)S(1)} %get-tuple-element.220, bf16[1,2,96,12,192]{4,2,3,1,0:T(8,128)(2,1)S(1)} %constant_dynamic-slice_fusion.2, pred[]{:T(512)S(6)} %compare.3, ...), kind=kLoop, calls=%fused_computation.1.clone.1 | loop fusion | flops 3981312 | bytes 9732097 | tf_op jit(solution)/shard_map/while/body/eval_jaxpr/add | solution.py:184
  247.2 7.7 %select_add_fusion.3 = (f32[2,96,12,192]{3,2,1,0:T(8,128)}, f32[2,96,12,192]{3,2,1,0:T(8,128)}) fusion(f32[2,96,12,192]{3,2,1,0:T(8,128)} %get-tuple-element.211, f32[2,96,12,192]{3,2,1,0:T(8,128)S(1)} %get-tuple-element.220, bf16[1,2,96,12,192]{4,2,3,1,0:T(8,128)(2,1)S(1)} %constant_dynamic-slice_fusion.2, pred[]{:T(512)S(6)} %compare.3, ...), kind=kLoop, calls=%fused_computation.1.clone.1 | loop fusion | flops 3981312 | bytes 9732097 | tf_op jit(solution)/shard_map/while/body/eval_jaxpr/add | solution.py:184
  256.3 7.7 %select_add_fusion.3 = (f32[2,96,12,192]{3,2,1,0:T(8,128)}, f32[2,96,12,192]{3,2,1,0:T(8,128)}) fusion(f32[2,96,12,192]{3,2,1,0:T(8,128)} %get-tuple-element.211, f32[2,96,12,192]{3,2,1,0:T(8,128)S(1)} %get-tuple-element.220, bf16[1,2,96,12,192]{4,2,3,1,0:T(8,128)(2,1)S(1)} %constant_dynamic-slice_fusion.2, pred[]{:T(512)S(6)} %compare.3, ...), kind=kLoop, calls=%fused_computation.1.clone.1 | loop fusion | flops 3981312 | bytes 9732097 | tf_op jit(solution)/shard_map/while/body/eval_jaxpr/add | solution.py:184
  264.0 10.7 %fusion.80 = (bf16[2,96,12,192]{3,0,2,1:T(2,128)(2,1)S(1)}, f32[2,96,12,192]{3,0,2,1:T(2,128)}) fusion(f32[2,96,12,192]{3,2,1,0:T(8,128)} %get-tuple-element.73, bf16[2,96,12,192]{3,1,2,0:T(8,128)(2,1)} %param.10, bf16[2,96,6,192]{3,0,2,1:T(2,128)(2,1)} %copy-done.11, bf16[2,96,6,192]{3,0,2,1:T(2,128)(2,1)} %copy-done.15, ...), kind=kLoop, calls=%fused_computation.94 | loop fusion | flops 5750784 | bytes 7078272 | tf_op jit(solution)/shard_map/convert_element_type | solution.py:195
  275.5 1.9 collective-permute-start.2
  279.3 2.3 copy.95
  281.7 3.0 reshape.285
  284.8 2.7 pad_maximum_fusion.2
  291.0 9.3 %fusion.49 = bf16[16,6,144,32]{2,3,1,0:T(8,128)(2,1)} fusion(bf16[16,6,144,32]{2,3,1,0:T(8,128)(2,1)S(1)} %bitcast.147, f32[16,6,144,144]{2,3,1,0:T(8,128)} %copy-done.27, f32[16,6,144]{2,1,0:T(8,128)} %copy-done.28, pred[16,144,144]{1,2,0:T(8,128)(4,1)} %or_and_fusion), kind=kOutput, calls=%fused_computation.62 | convolution fusion | flops 135806976 | bytes 10119168 | tf_op jit(solution)/shard_map/while/body/eval_jaxpr/abhqk,abhqd->abhkd/dot_general | solution.py:47
  300.3 7.2 %fusion.87 = f32[16,6,144,144]{2,3,1,0:T(8,128)} fusion(bf16[16,6,144,32]{2,3,1,0:T(8,128)(2,1)S(1)} %bitcast.148, bf16[16,6,144,32]{2,3,1,0:T(8,128)(2,1)S(1)} %bitcast.146), kind=kOutput, calls=%fused_computation.100 | convolution fusion | flops 127401984 | bytes 9732096 | tf_op jit(solution)/shard_map/while/body/eval_jaxpr/abhqd,abhkd->abhqk/dot_general | solution.py:47
  307.5 26.8 %fusion.52 = bf16[16,6,144,32]{2,3,1,0:T(8,128)(2,1)} fusion(bf16[16,6,144,32]{2,3,1,0:T(8,128)(2,1)} %bitcast.165, f32[16,6,144,144]{2,3,1,0:T(8,128)} %fusion.87, f32[16,6,144,144]{2,3,1,0:T(8,128)} %copy-done.27, f32[16,6,144]{2,1,0:T(8,128)} %copy-done.28, pred[16,144,144]{1,2,0:T(8,128)(4,1)} %or_and_fusion), kind=kOutput, calls=%fused_computation.63 | convolution fusion | flops 149755536 | bytes 18081792 | tf_op jit(solution)/shard_map/while/body/eval_jaxpr/abhqk,abhkd->abhqd/dot_general | solution.py:47
  334.3 25.2 %fusion.55 = bf16[16,6,144,32]{2,3,1,0:T(8,128)(2,1)S(1)} fusion(bf16[16,6,144,32]{2,3,1,0:T(8,128)(2,1)S(1)} %bitcast.167, f32[16,6,144,144]{2,3,1,0:T(8,128)} %fusion.87, f32[16,6,144,144]{2,3,1,0:T(8,128)} %copy-done.27, f32[16,6,144]{2,1,0:T(8,128)} %copy-done.28, pred[16,144,144]{1,2,0:T(8,128)(4,1)} %or_and_fusion), kind=kOutput, calls=%fused_computation.64 | convolution fusion | flops 149755536 | bytes 18081792 | tf_op jit(solution)/shard_map/while/body/eval_jaxpr/abhqk,abhqd->abhkd/dot_general | solution.py:47
  359.6 3.5 reshape.286
  364.7 2.3 copy.94
  367.0 3.0 concatenate.46
  370.0 2.6 copy.86
  374.3 2.3 copy.92
  376.6 3.2 concatenate.44
  380.8 3.1 concatenate.45
  383.9 2.2 fusion.88
  386.1 4.2 fusion.24
  390.4 2.4 fusion.58
  394.4 1.8 fusion.83
  396.3 139.0 %all-reduce.4.cloned.1.call-done = (f32[192,576]{1,0:T(8,128)}, f32[192,192]{1,0:T(8,128)}) async-done(((f32[192,576]{1,0:T(8,128)}, f32[192,192]{1,0:T(8,128)}), (f32[192,576]{1,0:T(8,128)}, f32[192,192]{1,0:T(8,128)})) %all-reduce.4.cloned.1.call-update) | async-done | bytes 589840 | tf_op jit(solution)/shard_map/psum | solution.py:208
  536.9 1.9 broadcast_multiply_fusion.3
  538.8 19.0 %fusion.40 = (f32[192]{0:T(256)S(1)}, f32[2,96,12]{0,2,1:T(8,128)}, f32[2,96,12]{0,2,1:T(8,128)}, f32[]{:T(128)}, f32[]{:T(128)}) fusion(f32[2,96,12]{0,2,1:T(8,128)} %copy-done.6, f32[2,96,12]{0,2,1:T(8,128)} %copy-done.4, bf16[1,2,96,12,192]{4,2,3,1,0:T(8,128)(2,1)} %param.9, bf16[2,96,6,192]{3,0,2,1:T(2,128)(2,1)} %get-tuple-element.155, ...), kind=kLoop, calls=%fused_computation.48 | loop fusion | flops 9727294 | bytes 5347208 | tf_op jit(solution)/shard_map/reduce_sum | solution.py:200
  559.3 64.8 %all-reduce = (f32[192]{0:T(256)S(1)}, f32[]{:T(128)}) all-reduce(f32[192]{0:T(256)S(1)} %get-tuple-element.129, f32[]{:T(128)S(6)} %sub.53), channel_id=1, replica_groups=mesh['lon'=16,'mem'=8] {'lon','mem'}, use_global_device_ids=true, to_apply=%region_11.12 | all-reduce | flops 193 | bytes 1544 | tf_op jit(solution)/shard_map/psum | solution.py:208
  626.2 7.7 %fusion.63 = bf16[1,2,96,12,192]{4,1,3,2,0:T(2,128)(2,1)S(1)} fusion(f32[2,96,12,192]{3,0,2,1:T(2,128)} %get-tuple-element.148, f32[2,96,12]{0,2,1:T(8,128)S(1)} %get-tuple-element.165, f32[2,96,12]{0,2,1:T(8,128)S(1)} %get-tuple-element.166, f32[192]{0:T(256)S(1)} %copy-done.24, f32[2,96,12]{0,2,1:T(8,128)S(1)} %copy-done.7, f32[2,96,12]{0,2,1:T(8,128)S(1)} %copy-done.5, ...), kind=kLoop, calls=%fused_computation.74 | loop fusion | flops 5308416 | bytes 4461312 | tf_op jit(solution)/shard_map/broadcast_in_dim | solution.py:207
  (114 shorter events, 44.7 us)
Async XLA Ops:
  7.2 25.8 %copy-start = (bf16[192,576]{1,0:T(8,128)(2,1)S(1)}, bf16[192,576]{1,0:T(8,128)(2,1)}, u32[]{:S(2)}) copy-start(bf16[192,576]{1,0:T(8,128)(2,1)} %param.12) | copy-start | bytes 663556
  7.2 2.9 copy-start.2
  7.2 187.2 %all-gather.3.cloned.1.call-start = ((), (), s32[]{:S(2)}) async-start(), calls=%async_computation | async-start | bytes 10616832 | tf_op jit(solution)/shard_map/all_gather | solution.py:187
  10.1 8.1 %copy-start.4 = (f32[2,96,12]{0,2,1:T(8,128)}, f32[2,96,12]{0,2,1:T(8,128)S(1)}, u32[]{:S(2)}) copy-start(f32[2,96,12]{0,2,1:T(8,128)S(1)} %broadcast_multiply_fusion.2) | copy-start | bytes 27652
  10.1 4.9 copy-start.23
  14.1 0.9 copy-start.6
  15.0 7.9 %copy-start.26 = (s32[96]{0:T(128)S(1)}, s32[96]{0:T(128)}, u32[]{:S(2)}) copy-start(s32[96]{0:T(128)} %param.15) | copy-start | bytes 1156
  15.0 8.0 %copy-start.25 = (s32[96]{0:T(128)S(1)}, s32[96]{0:T(128)}, u32[]{:S(2)}) copy-start(s32[96]{0:T(128)} %param.14) | copy-start | bytes 1156
  18.9 11.3 %collective-permute-start = (bf16[2,96,6,192]{3,0,2,1:T(2,128)(2,1)S(1)}, bf16[2,96,6,192]{3,0,2,1:T(2,128)(2,1)S(1)}, u32[]{:S(2)}, u32[]{:S(2)}) collective-permute-start(bf16[2,96,6,192]{3,0,2,1:T(2,128)(2,1)S(1)} %get-tuple-element.161), channel_id=1, source_target_pairs={{0,120},{8,0},{16,8},{24,16},{32,24},{40,32},{48,40},{56,48},{64,5... | collective-permute-start | bytes 1327112 | tf_op jit(solution)/shard_map/ppermute | solution.py:16
  31.9 1.0 copy-start.9
  40.0 8.9 %copy-start.12 = (bf16[16,1,144,192]{2,3,0,1:T(8,128)(2,1)}, bf16[16,1,144,192]{2,3,0,1:T(8,128)(2,1)S(1)}, u32[]{:S(2)}) copy-start(bf16[16,1,144,192]{2,3,0,1:T(8,128)(2,1)S(1)} %copy.70) | copy-start | bytes 2654212
  43.1 5.9 copy-start.21
  48.9 5.1 copy-start.27
  48.9 5.3 copy-start.28
  48.9 5.3 copy-start.22
  54.2 1.1 copy-start.17
  57.4 16.4 %copy-start.11 = (bf16[2,96,6,192]{3,0,2,1:T(2,128)(2,1)}, bf16[2,96,6,192]{3,0,2,1:T(2,128)(2,1)S(1)}, u32[]{:S(2)}) copy-start(bf16[2,96,6,192]{3,0,2,1:T(2,128)(2,1)S(1)} %get-tuple-element.159) | copy-start | bytes 1327108
  57.4 11.7 %collective-permute-start.1 = (bf16[2,96,6,192]{3,0,2,1:T(2,128)(2,1)S(1)}, bf16[2,96,6,192]{3,0,2,1:T(2,128)(2,1)S(1)}, u32[]{:S(2)}, u32[]{:S(2)}) collective-permute-start(bf16[2,96,6,192]{3,0,2,1:T(2,128)(2,1)S(1)} %get-tuple-element.158), channel_id=1, source_target_pairs={{0,8},{8,16},{16,24},{24,32},{32,40},{40,48},{48,56},{56,64},{64,7... | collective-permute-start | bytes 1327112 | tf_op jit(solution)/shard_map/ppermute | solution.py:16
  69.1 4.7 copy-start.15
  73.8 1.0 copy-start.8
  76.1 459.1 %all-reduce.4.cloned.1.call-start = ((), (), s32[]{:S(2)}) async-start(), calls=%async_computation.1 | async-start | bytes 1376256 | tf_op jit(solution)/shard_map/psum | solution.py:208
  274.7 2.7 copy-start.10
  275.5 9.3 %collective-permute-start.2 = (bf16[2,96,6,192]{3,0,2,1:T(2,128)(2,1)S(1)}, bf16[2,96,6,192]{3,0,2,1:T(2,128)(2,1)}, u32[]{:S(2)}, u32[]{:S(2)}) collective-permute-start(bf16[2,96,6,192]{3,0,2,1:T(2,128)(2,1)S(1)} %get-tuple-element.157), channel_id=1, source_target_pairs={{0,120},{8,0},{16,8},{24,16},{32,24},{40,32},{48,40},{56,48},{64,5... | collective-permute-start | bytes 1327112 | tf_op jit(solution)/shard_map/ppermute | solution.py:16
  291.0 9.3 %copy-start.13 = (bf16[16,1,144,192]{2,3,0,1:T(8,128)(2,1)S(1)}, bf16[16,1,144,192]{2,3,0,1:T(8,128)(2,1)}, u32[]{:S(2)}) copy-start(bf16[16,1,144,192]{2,3,0,1:T(8,128)(2,1)} %copy-done.12) | copy-start | bytes 2654212
  307.5 26.8 %copy-start.18 = (bf16[16,1,144,192]{2,3,0,1:T(8,128)(2,1)S(1)}, bf16[16,1,144,192]{2,3,0,1:T(8,128)(2,1)}, u32[]{:S(2)}) copy-start(bf16[16,1,144,192]{2,3,0,1:T(8,128)(2,1)} %copy.68) | copy-start | bytes 2654212
  359.6 3.5 copy-start.14
  380.8 3.1 copy-start.16
  386.1 4.3 copy-start.19
  386.1 4.3 copy-start.20
  394.4 144.4 %copy-start.1 = (f32[2,96,12,192]{3,2,1,0:T(8,128)S(1)}, f32[2,96,12,192]{3,2,1,0:T(8,128)}, u32[]{:S(2)}) copy-start(f32[2,96,12,192]{3,2,1,0:T(8,128)} %get-tuple-element.74) | copy-start | bytes 5308420
  394.4 144.4 %copy-start.24 = (f32[192]{0:T(256)S(1)}, f32[192]{0:T(256)}, u32[]{:S(2)}) copy-start(f32[192]{0:T(256)} %param.11) | copy-start | bytes 2308
  396.2 142.5 %collective-permute-start.3 = (bf16[2,96,6,192]{3,0,2,1:T(2,128)(2,1)}, bf16[2,96,6,192]{3,0,2,1:T(2,128)(2,1)}, u32[]{:S(2)}, u32[]{:S(2)}) collective-permute-start(bf16[2,96,6,192]{3,0,2,1:T(2,128)(2,1)} %get-tuple-element.154), channel_id=1, source_target_pairs={{0,8},{8,16},{16,24},{24,32},{32,40},{40,48},{48,56},{56,64},{64,7... | collective-permute-start | bytes 1327112 | tf_op jit(solution)/shard_map/ppermute | solution.py:16
  557.8 68.4 %copy-start.3 = (bf16[1,2,96,12,192]{4,2,3,1,0:T(8,128)(2,1)S(1)}, bf16[1,2,96,12,192]{4,2,3,1,0:T(8,128)(2,1)}, u32[]{:S(2)}) copy-start(bf16[1,2,96,12,192]{4,2,3,1,0:T(8,128)(2,1)} %param.9) | copy-start | bytes 2654212
  557.8 68.4 %copy-start.5 = (f32[2,96,12]{0,2,1:T(8,128)S(1)}, f32[2,96,12]{0,2,1:T(8,128)}, u32[]{:S(2)}) copy-start(f32[2,96,12]{0,2,1:T(8,128)} %copy-done.4) | copy-start | bytes 27652
  557.8 68.4 %copy-start.7 = (f32[2,96,12]{0,2,1:T(8,128)S(1)}, f32[2,96,12]{0,2,1:T(8,128)}, u32[]{:S(2)}) copy-start(f32[2,96,12]{0,2,1:T(8,128)} %copy-done.6) | copy-start | bytes 27652
Sparse Core Ops, SparseCore 0:
  76.3 118.0 all-gather.2
  390.5 144.7 all-reduce.3
where the time goes:
time: 650 us; the launch traced here: 644 us
  waiting for transfers between devices  272 us (42%)
  other arithmetic  123 us (19%)
  matrix products  90.3 us (14%)
  local copies, waits for them, and re-layouts  70.1 us (11%)
  blocking collectives  64.8 us (10%)
  between operations  18.3 us (3%)
    psum x1, waiting for transfers between devices, body(): lax.psum((qkv_part, proj_part, gain_partial, score), ('lon', 'mem'))  139 us
    all_gather x1, waiting for transfers between devices, body(): lax.all_gather(rounded[None], 'mem', axis=0, tiled=True)  116 us
    dot_general x6, matrix products, batched(): return jnp.einsum(spec, left, right, preferred_element_type=jnp.float32)  78.5 us
    psum x1, blocking collectives, body(): lax.psum((qkv_part, proj_part, gain_partial, score), ('lon', 'mem'))  64.8 us
    add x8, other arithmetic, step(): return ((inner[0] + size, inner[1] + diff / size), None)  58.8 us
    reduce_sum x1, other arithmetic, body(): jnp.sum(gradient_normalized * standardized_input, axis=(0, 1, 2))  19 us
    ppermute x4, waiting for transfers between devices, from_behind(): lax.ppermute(array, axis, [(i, (i + by) % devices) for i in range(devices)])  16.4 us
    concatenate x6, local copies, waits for them, and re-layouts, backward_block(): jnp.concatenate([merge_heads(grad_query), merge_heads(grad_keys), merge_h...  15.2 us
  transfers between devices with their start and end apart: 6, of which 5 were waited for; matrix products, arithmetic and copies ran while one was open for 3% of the time, Pallas kernels for 0%

commit v1 on v0

v1 whole, which is shorter than its diff:
```python
import functools

import jax
import jax.numpy as jnp
import numpy as np
from jax import lax
from jax.experimental import pallas as pl
from jax.experimental.pallas import tpu as pltpu
from jax.sharding import PartitionSpec as P

HEADS = 6
SIZE = 32
SHIFT = 6
C = 192
CELLS = 144
HALF = 72
M = 8
EPS = 1e-05
DELTA_SQ = 0.0625
PIECE = 216
GRAD_ROWS = 160
ROWS = 2 * PIECE + GRAD_ROWS
BF = jnp.bfloat16
F32 = jnp.float32
VMEM_LIMIT = 56 * 1024 * 1024


def dot(left, right):
    return jnp.dot(left, right, preferred_element_type=F32)


def dot_t(left, right):
    return lax.dot_general(left, right, (((1,), (1,)), ((), ())), preferred_element_type=F32)


def identity(n):
    return (
        lax.broadcasted_iota(jnp.int32, (n, n), 0) == lax.broadcasted_iota(jnp.int32, (n, n), 1)
    ).astype(BF)


def pack_half(first, second):
    pad = jnp.zeros((HALF, 64), F32)
    rest = jnp.concatenate([first[:, 128:], pad], axis=1)
    other = jnp.concatenate([second[:, 128:], pad], axis=1)
    return jnp.concatenate(
        [first[:, :128], second[:, :128], rest + pltpu.roll(other, 64, 1)], axis=0
    )


def unpack_half(piece, block):
    rest = piece[2 * HALF :]
    if block == 1:
        rest = pltpu.roll(rest, 64, 1)
    return jnp.concatenate([piece[block * HALF : (block + 1) * HALF], rest[:, :64]], axis=1)


def place_matrix():
    cell = np.arange(CELLS)
    half, level, row, column = cell // 72, cell // 36 % 2, cell // 6 % 6, cell % 6
    out = np.zeros((CELLS, 12 * 16), np.float32)
    out[cell, (level * 6 + row) * 16 + half * 6 + column] = 1.0
    return out


def pack_kernel(x_ref, t_ref, place_ref, x_out, t_out, slabs):
    @pl.when(pl.program_id(0) == 0)
    def _():
        slabs[...] = jnp.zeros_like(slabs)

    def gather(ref):
        blocks = []
        for block in range(2):
            for level in range(2):
                for row in range(6):
                    at = (level * 6 + row) * 16
                    slabs[block, at : at + 12, :] = ref[level, block * 6 + row]
            blocks.append(dot(place_ref[...], slabs[block]))
        return [
            pack_half(blocks[0][half * HALF : (half + 1) * HALF], blocks[1][half * HALF : (half + 1) * HALF]).astype(BF)
            for half in range(2)
        ]

    to_west, own = gather(x_ref.at[0])
    x_out[0, 0] = to_west
    x_out[0, 1] = own

    @pl.when(pl.program_id(0) == 0)
    def _():
        to_west, own = gather(t_ref)
        t_out[0] = to_west
        t_out[1] = own


def pack(inputs, target_rows, place):
    return pl.pallas_call(
        pack_kernel,
        grid=(M,),
        in_specs=[
            pl.BlockSpec((1, 2, 12, 12, C), lambda i: (0, 0, i, 0, 0)),
            pl.BlockSpec((2, 12, 12, C), lambda i: (0, 0, 0, 0)),
            pl.BlockSpec((CELLS, 192), lambda i: (0, 0)),
        ],
        out_specs=[
            pl.BlockSpec((1, 2, PIECE, 128), lambda i: (i, 0, 0, 0)),
            pl.BlockSpec((2, PIECE, 128), lambda i: (0, 0, 0)),
        ],
        out_shape=[
            jax.ShapeDtypeStruct((M, 2, PIECE, 128), BF),
            jax.ShapeDtypeStruct((2, PIECE, 128), BF),
        ],
        scratch_shapes=[pltpu.VMEM((2, 192, C), BF)],
        name="pack_strip",
    )(inputs, target_rows, place)


def unpack_kernel(own_ref, beyond_ref, place_ref, out_ref):
    own = own_ref[0].astype(F32)
    beyond = beyond_ref[0].astype(F32)
    for block in range(2):
        cells = jnp.concatenate([unpack_half(beyond, block), unpack_half(own, block)], axis=0).astype(BF)
        slabs = dot(place_ref[...], cells).astype(BF)
        for level in range(2):
            for row in range(6):
                at = (level * 6 + row) * 16
                out_ref[0, level, block * 6 + row] = slabs[at : at + 12, :]


def unpack(own, beyond, place_t):
    return pl.pallas_call(
        unpack_kernel,
        grid=(M,),
        in_specs=[
            pl.BlockSpec((1, PIECE, 128), lambda i: (i, 0, 0)),
            pl.BlockSpec((1, PIECE, 128), lambda i: (i, 0, 0)),
            pl.BlockSpec((192, CELLS), lambda i: (0, 0)),
        ],
        out_specs=pl.BlockSpec((1, 2, 12, 12, C), lambda i: (0, 0, i, 0, 0)),
        out_shape=jax.ShapeDtypeStruct((1, 2, 96, 12, C), BF),
        name="unpack_strip",
    )(own, beyond, place_t)


def head_only(field, head):
    lane = lax.broadcasted_iota(jnp.int32, field.shape, 1)
    return jnp.where((lane >= head * SIZE) & (lane < (head + 1) * SIZE), field, jnp.zeros_like(field))


def main_kernel(
    xo_ref, xb_ref, t_ref, bias_ref, valid_ref, gain_ref, wkv_ref, wqkv_ref, wqkvt_ref, wproj_ref, wprojt_ref,
    out_ref,
    x_s, t_s, xhat_s, rstd_s, n_s, v_s, qkvt_s, att_s, w_s, mixed_s, sqkv_s, sproj_s, sgain_s,
):
    scale = SIZE ** (-0.5)
    to_exp2 = scale * 1.4426950408889634
    gain = gain_ref[...]
    eye_cells = identity(CELLS)
    eye_c = identity(C)

    for member in range(M):
        own = xo_ref[member].astype(F32)
        beyond = xb_ref[member].astype(F32)
        for block in range(2):
            x_s[block * M + member] = jnp.concatenate(
                [unpack_half(own, block), unpack_half(beyond, block)], axis=0
            )
    own = t_ref[0].astype(F32)
    beyond = t_ref[1].astype(F32)
    for block in range(2):
        t_s[block] = jnp.concatenate([unpack_half(own, block), unpack_half(beyond, block)], axis=0)

    def forward(window, carry):
        block = window // M
        x = x_s[window]
        centred = x - jnp.mean(x, axis=1, keepdims=True)
        rstd = lax.rsqrt(jnp.mean(centred * centred, axis=1, keepdims=True) + EPS)
        xhat = centred * rstd
        xhat_s[window] = xhat
        rstd_s[window] = rstd
        normed = (xhat * gain).astype(BF)
        n_s[window] = normed
        kv = dot(normed, wkv_ref[...]).astype(BF)
        keys = kv[:, :C]
        v_s[window] = kv[:, C:]
        qkvt = dot_t(wqkvt_ref[...], normed).astype(BF)
        qkvt_s[window] = qkvt
        qt = qkvt[:C]
        bias = bias_ref[block]
        parts = []
        for head in range(HEADS):
            scores = dot(head_only(keys, head), qt)
            expo = jnp.exp2(scores * to_exp2 + bias)
            weights = expo * (1.0 / jnp.sum(expo, axis=0, keepdims=True))
            w_s[window, head] = weights
            vt = qkvt[2 * C + head * SIZE : 2 * C + (head + 1) * SIZE]
            parts.append(dot(vt, weights.astype(BF)))
        attended = jnp.concatenate(parts, axis=0).astype(BF)
        att_s[window] = attended
        projt = dot(wprojt_ref[...], attended).astype(BF)
        mixed_s[window] = x + dot_t(eye_cells, projt)
        return carry

    lax.fori_loop(0, 2 * M, forward, 0)

    def crps(step, score):
        block = step // 18
        rows = pl.ds(pl.multiple_of((step % 18) * 8, 8), 8)
        valid = valid_ref[block, rows]
        target = t_s[block, rows]
        mixed = [mixed_s[block * M + m, rows] for m in range(M)]
        rounded = [value.astype(BF).astype(F32) for value in mixed]
        slopes = [None] * M
        pairs = None
        for m in range(M):
            for n in range(m + 1, M):
                diff = rounded[m] - rounded[n]
                square = diff * diff + DELTA_SQ
                inverse = lax.rsqrt(square)
                size = square * inverse
                slope = diff * inverse
                pairs = size if pairs is None else pairs + size
                slopes[m] = slope if slopes[m] is None else slopes[m] + slope
                slopes[n] = -slope if slopes[n] is None else slopes[n] - slope
        total = -(2.0 * pairs + M * DELTA_SQ**0.5) / (2.0 * M)
        for m in range(M):
            diff = mixed[m] - target
            square = diff * diff + DELTA_SQ
            inverse = lax.rsqrt(square)
            total = total + square * inverse
            mixed_s[block * M + m, rows] = valid * (diff * inverse - slopes[m] / M)
        return score + valid * total

    score = lax.fori_loop(0, 36, crps, jnp.zeros((8, C), F32))

    sqkv_s[...] = jnp.zeros_like(sqkv_s)
    sproj_s[...] = jnp.zeros_like(sproj_s)
    sgain_s[...] = jnp.zeros_like(sgain_s)

    def backward(window, carry):
        grad_mixed = mixed_s[window]
        grad_rows = grad_mixed.astype(BF)
        attended = att_s[window]
        gat = dot_t(wproj_ref[...], grad_rows).astype(BF)
        sproj_s[...] += dot(attended, grad_rows)
        values = v_s[window]
        dq, dk, dv = [], [], []
        for head in range(HEADS):
            at = slice(head * SIZE, (head + 1) * SIZE)
            weights = w_s[window, head]
            grad_probs = dot(head_only(values, head), gat)
            total = jnp.sum(weights * grad_probs, axis=0, keepdims=True)
            grad_scores = (weights * ((grad_probs - total) * scale)).astype(BF)
            qt = qkvt_s[window, head * SIZE : (head + 1) * SIZE]
            kt = qkvt_s[window, C + head * SIZE : C + (head + 1) * SIZE]
            dq.append(dot(kt, grad_scores))
            dk.append(dot_t(qt, grad_scores))
            dv.append(dot_t(gat[at], weights.astype(BF)))
        grad_qkvt = jnp.concatenate(dq + dk + dv, axis=0).astype(BF)
        sqkv_s[...] += dot(grad_qkvt, n_s[window])
        gbt = dot(wqkv_ref[...], grad_qkvt).astype(BF)
        grad_normed = dot_t(eye_cells, gbt)
        xhat = xhat_s[window]
        sgain_s[...] += jnp.sum((grad_normed * xhat).reshape(18, 8, C), axis=0)
        scaled = grad_normed * gain
        first = jnp.mean(scaled, axis=1, keepdims=True)
        second = jnp.mean(scaled * xhat, axis=1, keepdims=True)
        x_s[window] = grad_mixed + rstd_s[window] * (scaled - first - xhat * second)
        return carry

    lax.fori_loop(0, 2 * M, backward, 0)

    sqkv = dot_t(eye_c, sqkv_s[...].astype(BF))
    sproj = sproj_s[...]
    pad = jnp.zeros((C, 64), F32)
    rest = jnp.concatenate([sqkv[:, 512:], pad], axis=1)
    rest = rest[:96] + pltpu.roll(rest[96:], 64, 1)
    last = jnp.concatenate([sproj[:, 128:], pad], axis=1)
    last = last[:96] + pltpu.roll(last[96:], 64, 1)
    sgain = jnp.sum(sgain_s[...], axis=0, keepdims=True)
    total = jnp.sum(jnp.sum(score, axis=0, keepdims=True), axis=1, keepdims=True)
    high = total.astype(BF).astype(F32)
    low = (total - high).astype(BF).astype(F32)
    row = lax.broadcasted_iota(jnp.int32, (128, 128), 0)
    lane = lax.broadcasted_iota(jnp.int32, (128, 128), 1)
    extra = jnp.where(row == 0, jnp.broadcast_to(sgain[:, :128], (128, 128)), 0.0)
    wide = jnp.concatenate([sgain[:, 128:], jnp.zeros((1, 64), F32)], axis=1)
    extra = extra + jnp.where(row == 1, jnp.broadcast_to(wide, (128, 128)), 0.0)
    extra = extra + jnp.where((row == 2) & (lane == 0), jnp.broadcast_to(high, (128, 128)), 0.0)
    extra = extra + jnp.where((row == 2) & (lane == 1), jnp.broadcast_to(low, (128, 128)), 0.0)
    grads = jnp.concatenate(
        [sqkv[:, 128 * i : 128 * (i + 1)] for i in range(4)] + [rest, sproj[:, :128], last, extra], axis=0
    )
    for member in range(M):
        halves = []
        for half in range(2):
            at = slice(half * HALF, (half + 1) * HALF)
            halves.append(pack_half(x_s[member, at], x_s[M + member, at]))
        mine = grads[member * GRAD_ROWS : (member + 1) * GRAD_ROWS]
        out_ref[member] = jnp.concatenate(halves + [mine], axis=0).astype(BF)


def main(own, beyond, target, bias, valid, gain, w_qkv, w_proj):
    windows = 2 * M
    return pl.pallas_call(
        main_kernel,
        out_shape=jax.ShapeDtypeStruct((M, ROWS, 128), BF),
        scratch_shapes=[
            pltpu.VMEM((windows, CELLS, C), F32),
            pltpu.VMEM((2, CELLS, C), F32),
            pltpu.VMEM((windows, CELLS, C), F32),
            pltpu.VMEM((windows, CELLS, 1), F32),
            pltpu.VMEM((windows, CELLS, C), BF),
            pltpu.VMEM((windows, CELLS, C), BF),
            pltpu.VMEM((windows, 3 * C, CELLS), BF),
            pltpu.VMEM((windows, C, CELLS), BF),
            pltpu.VMEM((windows, HEADS, CELLS, CELLS), F32),
            pltpu.VMEM((windows, CELLS, C), F32),
            pltpu.VMEM((3 * C, C), F32),
            pltpu.VMEM((C, C), F32),
            pltpu.VMEM((8, C), F32),
        ],
        compiler_params=pltpu.CompilerParams(vmem_limit_bytes=VMEM_LIMIT),
        name="window_attention_crps",
    )(own, beyond, target, bias, valid, gain[None], w_qkv[:, C:], w_qkv, w_qkv.T, w_proj, w_proj.T)


def cell_rows(rows):
    return jnp.broadcast_to(rows.reshape(2, 1, 6, 1), (2, 4, 6, 6)).reshape(2, CELLS)


def body(inputs, target, norm_gain_vector, w_qkv, w_proj, lat_region, lat_valid):
    strips = lax.axis_size("lon")
    mine = lax.axis_index("mem")
    place = place_matrix()
    start = mine * 12
    target_rows = lax.dynamic_slice_in_dim(target, start, 12, axis=1)
    packed, target_packed = pack(inputs, target_rows, jnp.asarray(place, BF))

    region = cell_rows(lax.dynamic_slice_in_dim(lat_region, start, 12))
    valid = cell_rows(lax.dynamic_slice_in_dim(lat_valid, start, 12))
    same = region[:, :, None] == region[:, None, :]
    itself = np.eye(CELLS, dtype=bool)
    bias = jnp.where(same & ((valid[:, :, None] == 1) | itself[None]), 0.0, -1e30).astype(F32)
    valid_column = valid.astype(F32)[:, :, None]

    west = [(i, (i - 1) % strips) for i in range(strips)]
    east = [(i, (i + 1) % strips) for i in range(strips)]
    target_beyond = lax.ppermute(target_packed[0], "lon", west)
    arrived = lax.all_to_all(packed, "mem", 0, 0, tiled=False)
    beyond = lax.ppermute(arrived[:, 0], "lon", west)
    sent = main(
        arrived[:, 1], beyond, jnp.stack([target_packed[1], target_beyond]), bias, valid_column, norm_gain_vector, w_qkv, w_proj
    )
    back = lax.all_to_all(sent, "mem", 0, 0, tiled=False)
    west_half = lax.ppermute(back[:, PIECE : 2 * PIECE], "lon", east)
    part = jnp.sum(back[:, 2 * PIECE :].astype(F32), axis=0)
    bit = 1
    while bit < strips:
        part = part + lax.ppermute(part, "lon", [(i, i ^ bit) for i in range(strips)])
        bit *= 2
    high = part.astype(BF)
    low = (part - high.astype(F32))[32:48].astype(BF)
    full = jnp.concatenate([high, low], axis=0)
    shared = lax.all_to_all(
        jnp.broadcast_to(full[None], (M, GRAD_ROWS + 16, 128)), "mem", 0, 0, tiled=False
    ).astype(F32)
    grads = shared[:, :GRAD_ROWS].reshape(M * GRAD_ROWS, 128)
    extra = shared[M - 1, 32:48] + shared[M - 1, GRAD_ROWS:]
    grad_inputs = unpack(back[:, :PIECE], west_half, jnp.asarray(place.T, BF))

    count = M * 2 * 96 * 12 * strips
    scale = count ** (-0.5)
    rest = grads[768:864]
    qkv_sum = jnp.concatenate(
        [grads[i * C : (i + 1) * C] for i in range(4)]
        + [jnp.concatenate([rest[:, :64], rest[:, 64:]], axis=0)], axis=1
    )
    last = grads[1056:1152]
    proj_sum = jnp.concatenate(
        [grads[864:1056], jnp.concatenate([last[:, :64], last[:, 64:]], axis=0)], axis=1
    )
    gain_sum = extra[:2].reshape(256)[:C]
    loss = (extra[2, 0] + extra[2, 1]) / (count * C)
    return (grad_inputs, qkv_sum * scale, proj_sum * scale, gain_sum * scale, loss)


def solution(mesh):
    in_specs = (
        P("mem", None, None, "lon", None),
        P(None, None, "lon", None),
        P(),
        P(),
        P(),
        P(),
        P(),
    )
    out_specs = (P("mem", None, None, "lon", None), P(), P(), P(), P())
    return jax.shard_map(body, mesh=mesh, in_specs=in_specs, out_specs=out_specs, check_vma=False)
```

time: 650 us -> 183 us (0.28)
  waiting for transfers between devices: 272 us -> 28.2 us
  other arithmetic: 123 us -> 3.92 us
  matrix products: 90.3 us -> 0 us
  Pallas kernels: 0 us -> 87.6 us
  local copies, waits for them, and re-layouts: 70.1 us -> 16.7 us
  blocking collectives: 64.8 us -> 22 us
  between operations: 18.3 us -> 3.28 us
  starting transfers between devices: 5.96 us -> 20 us
    psum x1 -> x0, waiting for transfers between devices: 139 us -> none  [body(): lax.psum((qkv_part, proj_part, gain_partial, score), ('lon', 'mem'))]
    all_gather x1 -> x0, waiting for transfers between devices: 116 us -> none  [body(): lax.all_gather(rounded[None], 'mem', axis=0, tiled=True)]
    dot_general x12 -> x0, matrix products: 90.3 us -> none  [the longest x6 78.5 us: batched(): return jnp.einsum(spec, left, right, preferred_element_type=jnp.float32)]
    pallas_call x0 -> x3, Pallas kernels: none -> 87.6 us  [the longest x1 74.8 us: main(): pl.pallas_call(main_kernel, out_shape=jax.ShapeDtypeStruct((M, ROWS, 128)...]
    psum x1 -> x0, blocking collectives: 64.8 us -> none  [body(): lax.psum((qkv_part, proj_part, gain_partial, score), ('lon', 'mem'))]
    add x8 -> x5, other arithmetic: 58.8 us -> 0.04 us  [the longest x3 0.03 us: body(): part + lax.ppermute(part, 'lon', [(i, i ^ bit) for i in range(strips)])]
    reduce_sum x3 -> x1, other arithmetic: 25.6 us -> 0.05 us  [body(): part = jnp.sum(back[:, 2 * PIECE:].astype(F32), axis=0)]
    all_to_all x0 -> x1, blocking collectives: none -> 22 us  [body(): back = lax.all_to_all(sent, 'mem', 0, 0, tiled=False)]
  transfers between devices with their start and end apart: 6 -> 9, of which waited for: 5 -> 7; matrix products, arithmetic and copies ran while one was open for 3% -> 6% of each run, Pallas kernels for 0% -> 3%
where the time goes in v1:
time: 183 us; the launch traced here: 182 us
  Pallas kernels  87.6 us (48%)
  waiting for transfers between devices  28.2 us (15%)
  blocking collectives  22 us (12%)
  starting transfers between devices  20 us (11%)
  local copies, waits for them, and re-layouts  16.7 us (9%)
  other arithmetic  3.92 us (2%)
  between operations  3.28 us (2%)
    pallas_call x1, Pallas kernels, main(): pl.pallas_call(main_kernel, out_shape=jax.ShapeDtypeStruct((M, ROWS, 128)...  74.8 us
    all_to_all x1, blocking collectives, body(): back = lax.all_to_all(sent, 'mem', 0, 0, tiled=False)  22 us
    all_to_all x1, waiting for transfers between devices, body(): arrived = lax.all_to_all(packed, 'mem', 0, 0, tiled=False)  12.2 us
    ppermute x4, waiting for transfers between devices, body(): lax.ppermute(part, 'lon', [(i, i ^ bit) for i in range(strips)])  12 us
    unnamed x26, local copies, waits for them, and re-layouts  11.1 us
    all_to_all x1, starting transfers between devices, body(): arrived = lax.all_to_all(packed, 'mem', 0, 0, tiled=False)  8.01 us
    pallas_call x1, Pallas kernels, pack(): pl.pallas_call(pack_kernel, grid=(M,), in_specs=[pl.BlockSpec((1, 2, 12,...  6.72 us
    pallas_call x1, Pallas kernels, unpack(): pl.pallas_call(unpack_kernel, grid=(M,), in_specs=[pl.BlockSpec((1, PIECE...  6.08 us
  transfers between devices with their start and end apart: 9, of which 7 were waited for; matrix products, arithmetic and copies ran while one was open for 6% of the time, Pallas kernels for 3%

profile of v1, /device:TPU:0, one launch (start us, length us, event | category | flops | bytes accessed | tf_op | source)
XLA Modules:
  0.0 181.7 jit_solution(10271031802155987645)
XLA Ops:
  0.7 1.3 copy-done
  2.0 0.7 copy.36.t_ref
  2.7 3.1 %copy.29.x_ref = bf16[1,2,96,12,192]{4,3,2,1,0:T(8,128)(2,1)} copy(bf16[1,2,96,12,192]{4,2,3,1,0:T(8,128)(2,1)} %param.10) | data formatting | bytes 1769472 | tf_op args[0]
  5.8 6.7 %pack_strip.1 = (bf16[8,2,216,128]{3,2,1,0:T(8,128)(2,1)}, bf16[2,216,128]{2,1,0:T(8,128)(2,1)}) custom-call(bf16[1,2,96,12,192]{4,3,2,1,0:T(8,128)(2,1)} %copy.29.x_ref, bf16[2,12,12,192]{3,2,1,0:T(8,128)(2,1)} %copy.36.t_ref, bf16[144,192]{1,0:T(8,128)(2,1)} %constant.30.clone.place_ref), custom_call_target="tpu_custom_call" | custom-call | tf_op jit(solution)/shard_map/pack_strip/pallas_call | solution.py:96
  12.6 8.0 %all-to-all-start = ((bf16[8,2,216,128]{3,2,1,0:T(8,128)(2,1)}), bf16[8,2,216,128]{3,2,1,0:T(8,128)(2,1)S(1)}, u32[]{:S(2)}, u32[]{:S(2)}) async-start(bf16[8,2,216,128]{3,2,1,0:T(8,128)(2,1)} %get-tuple-element.7), calls=%async_computation | async-start | bytes 1769472 | tf_op jit(solution)/shard_map/all_to_all | solution.py:349
  20.6 2.4 %collective-permute-start.1 = (bf16[216,128]{1,0:T(8,128)(2,1)S(1)}, bf16[216,128]{1,0:T(8,128)(2,1)S(1)}, u32[]{:S(2)}, u32[]{:S(2)}) collective-permute-start(bf16[216,128]{1,0:T(8,128)(2,1)S(1)} %get-tuple-element.37), channel_id=1, source_target_pairs={{0,120},{8,0},{16,8},{24,16},{32,24},{40,32},{48,40},{56,48},{64,5... | collective-permute-start | bytes 165896 | tf_op jit(solution)/shard_map/ppermute | solution.py:348
  23.1 0.1 dynamic_slice.10
  23.2 0.1 broadcast_in_dim.32
  23.3 0.1 eq.33
  23.4 0.1 broadcast_compare_fusion
  23.5 0.1 eq.39
  23.6 0.1 broadcast_in_dim.34
  23.7 0.1 eq.40
  23.8 12.2 %all-to-all-done = bf16[8,2,216,128]{3,2,1,0:T(8,128)(2,1)S(1)} async-done(((bf16[8,2,216,128]{3,2,1,0:T(8,128)(2,1)}), bf16[8,2,216,128]{3,2,1,0:T(8,128)(2,1)S(1)}, u32[]{:S(2)}, u32[]{:S(2)}) %all-to-all-start) | async-done | bytes 884768 | tf_op jit(solution)/shard_map/all_to_all | solution.py:349
  36.0 0.8 slice_bitcast_fusion
  36.9 2.5 %collective-permute-start = (bf16[8,216,128]{2,1,0:T(8,128)(2,1)S(1)}, bf16[8,216,128]{2,1,0:T(8,128)(2,1)S(1)}, u32[]{:S(2)}, u32[]{:S(2)}) collective-permute-start(bf16[8,216,128]{2,1,0:T(8,128)(2,1)S(1)} %get-tuple-element.28), channel_id=1, source_target_pairs={{0,120},{8,0},{16,8},{24,16},{32,24},{40,32},{48,40},{56,48},{64,5... | collective-permute-start | bytes 1327112 | tf_op jit(solution)/shard_map/ppermute | solution.py:350
  39.4 0.9 and_select_fusion.bias_ref
  40.2 0.1 dynamic-slice_convert_fusion
  40.3 0.9 copy.32
  41.2 0.8 slice.87.wkv_ref
  41.9 0.1 convert_element_type.31
  42.1 0.8 convert_element_type.37.valid_ref
  42.9 0.7 copy.33
  43.6 0.6 pad_maximum_fusion.t_ref
  44.2 0.9 collective-permute-done.xb_ref
  45.2 0.8 copy-done.2
  45.9 74.8 %window_attention_crps.1 = bf16[8,592,128]{2,1,0:T(8,128)(2,1)} custom-call(bf16[8,216,128]{2,1,0:T(8,128)(2,1)} %get-tuple-element.29.xo_ref, bf16[8,216,128]{2,1,0:T(8,128)(2,1)} %copy-done.2, bf16[2,216,128]{2,1,0:T(8,128)(2,1)} %pad_maximum_fusion.t_ref, f32[2,144,144]{2,1,0:T(8,128)} %and_select_fusion.bias_ref, ...), custom_call_target="tpu_custom_call" | custom-call | tf_op jit(solution)/shard_map/window_attention_crps/pallas_call | solution.py:304
  120.7 22.0 %all_to_all.15 = bf16[8,592,128]{2,1,0:T(8,128)(2,1)S(1)} all-to-all(bf16[8,592,128]{2,1,0:T(8,128)(2,1)} %window_attention_crps.1), channel_id=1, replica_groups=mesh['lon'=16,'mem'=8] {'mem'}, dimensions={0} | all-to-all | bytes 2424832 | tf_op jit(solution)/shard_map/all_to_all | solution.py:354
  142.7 0.1 collective-permute-start.3
  142.8 1.3 collective-permute-done.3
  144.1 0.2 collective-permute-start.4
  144.3 4.3 %collective-permute-done.4 = f32[160,128]{1,0:T(8,128)S(1)} collective-permute-done((f32[160,128]{1,0:T(8,128)S(1)}, f32[160,128]{1,0:T(8,128)S(1)}, u32[]{:S(2)}, u32[]{:S(2)}) %collective-permute-start.4) | collective-permute-done | bytes 81952 | tf_op jit(solution)/shard_map/ppermute | solution.py:359
  148.7 0.9 collective-permute-start.5
  149.6 3.6 %collective-permute-done.5 = f32[160,128]{1,0:T(8,128)S(1)} collective-permute-done((f32[160,128]{1,0:T(8,128)S(1)}, f32[160,128]{1,0:T(8,128)S(1)}, u32[]{:S(2)}, u32[]{:S(2)}) %collective-permute-start.5) | collective-permute-done | bytes 81952 | tf_op jit(solution)/shard_map/ppermute | solution.py:359
  153.2 2.4 %collective-permute-start.6 = (f32[160,128]{1,0:T(8,128)S(1)}, f32[160,128]{1,0:T(8,128)S(1)}, u32[]{:S(2)}, u32[]{:S(2)}) collective-permute-start(f32[160,128]{1,0:T(8,128)S(1)} %add.30), channel_id=1, source_target_pairs={{0,64},{8,72},{16,80},{24,88},{32,96},{40,104},{48,112},{56,120},{... | collective-permute-start | bytes 245768 | tf_op jit(solution)/shard_map/ppermute | solution.py:359
  155.6 0.8 fusion.2
  156.5 2.8 %collective-permute-done.6 = f32[160,128]{1,0:T(8,128)S(1)} collective-permute-done((f32[160,128]{1,0:T(8,128)S(1)}, f32[160,128]{1,0:T(8,128)S(1)}, u32[]{:S(2)}, u32[]{:S(2)}) %collective-permute-start.6) | collective-permute-done | bytes 81952 | tf_op jit(solution)/shard_map/ppermute | solution.py:359
  159.3 0.8 broadcast_in_dim.39
  160.1 3.4 %all-to-all-start.2 = ((bf16[8,176,128]{2,1,0:T(8,128)(2,1)}), bf16[8,176,128]{2,1,0:T(8,128)(2,1)S(1)}, u32[]{:S(2)}, u32[]{:S(2)}) async-start(bf16[8,176,128]{2,1,0:T(8,128)(2,1)} %broadcast_in_dim.39), calls=%async_computation.2 | async-start | bytes 720896 | tf_op jit(solution)/shard_map/all_to_all | solution.py:364
  163.5 3.0 %collective-permute-done.2.beyond_ref = bf16[8,216,128]{2,1,0:T(8,128)(2,1)S(1)} collective-permute-done((bf16[8,216,128]{2,1,0:T(8,128)(2,1)S(1)}, bf16[8,216,128]{2,1,0:T(8,128)(2,1)S(1)}, u32[]{:S(2)}, u32[]{:S(2)}) %collective-permute-start.2) | collective-permute-done | bytes 442400 | tf_op jit(solution)/shard_map/ppermute | solution.py:355
  166.6 0.8 copy-done.3
  167.3 6.1 %unpack_strip.1 = bf16[1,2,96,12,192]{4,3,2,1,0:T(8,128)(2,1)} custom-call(bf16[8,216,128]{2,1,0:T(8,128)(2,1)} %get-tuple-element.27.own_ref, bf16[8,216,128]{2,1,0:T(8,128)(2,1)} %copy-done.3, bf16[192,144]{1,0:T(8,128)(2,1)} %constant.32.clone.place_ref), custom_call_target="tpu_custom_call" | custom-call | tf_op jit(solution)/shard_map/unpack_strip/pallas_call | solution.py:130
  173.4 2.8 %copy.35 = bf16[1,2,96,12,192]{4,2,3,1,0:T(8,128)(2,1)} copy(bf16[1,2,96,12,192]{4,3,2,1,0:T(8,128)(2,1)} %unpack_strip.1) | data formatting | bytes 1769472
  176.3 0.1 fusion.4
  176.5 0.6 fusion.6
  177.1 0.8 broadcast_multiply_fusion
  178.0 0.6 slice_multiply_fusion
  179.8 0.7 maximum_multiply_fusion
  (39 shorter events, 0.5 us)
Async XLA Ops:
  0.6 1.3 copy-start
  12.6 8.0 %copy-start.5 = (bf16[2,216,128]{2,1,0:T(8,128)(2,1)S(1)}, bf16[2,216,128]{2,1,0:T(8,128)(2,1)}, u32[]{:S(2)}) copy-start(bf16[2,216,128]{2,1,0:T(8,128)(2,1)} %get-tuple-element.8) | copy-start | bytes 331780
  12.6 10.5 %copy-start.7 = (s32[96]{0:T(128)S(1)}, s32[96]{0:T(128)}, u32[]{:S(2)}) copy-start(s32[96]{0:T(128)} %param.15) | copy-start | bytes 1156
  12.6 10.9 %copy-start.8 = (s32[96]{0:T(128)S(1)}, s32[96]{0:T(128)}, u32[]{:S(2)}) copy-start(s32[96]{0:T(128)} %param.16) | copy-start | bytes 1156
  12.6 23.5 %all-to-all-start = ((bf16[8,2,216,128]{3,2,1,0:T(8,128)(2,1)}), bf16[8,2,216,128]{3,2,1,0:T(8,128)(2,1)S(1)}, u32[]{:S(2)}, u32[]{:S(2)}) async-start(bf16[8,2,216,128]{3,2,1,0:T(8,128)(2,1)} %get-tuple-element.7), calls=%async_computation | async-start | bytes 1769472 | tf_op jit(solution)/shard_map/all_to_all | solution.py:349
  20.6 18.8 %copy-start.6 = (pred[144,144]{1,0:T(8,128)(4,1)S(1)}, pred[144,144]{1,0:T(8,128)(4,1)}, u32[]{:S(2)}) copy-start(pred[144,144]{1,0:T(8,128)(4,1)} %constant.35) | copy-start | bytes 62212
  20.6 19.7 %copy-start.1 = (bf16[192,576]{1,0:T(8,128)(2,1)S(1)}, bf16[192,576]{1,0:T(8,128)(2,1)}, u32[]{:S(2)}) copy-start(bf16[192,576]{1,0:T(8,128)(2,1)} %wqkv_ref.1) | copy-start | bytes 663556
  20.6 23.0 %collective-permute-start.1 = (bf16[216,128]{1,0:T(8,128)(2,1)S(1)}, bf16[216,128]{1,0:T(8,128)(2,1)S(1)}, u32[]{:S(2)}, u32[]{:S(2)}) collective-permute-start(bf16[216,128]{1,0:T(8,128)(2,1)S(1)} %get-tuple-element.37), channel_id=1, source_target_pairs={{0,120},{8,0},{16,8},{24,16},{32,24},{40,32},{48,40},{56,48},{64,5... | collective-permute-start | bytes 165896 | tf_op jit(solution)/shard_map/ppermute | solution.py:348
  23.8 19.1 %copy-start.4 = (bf16[192,192]{1,0:T(8,128)(2,1)S(1)}, bf16[192,192]{1,0:T(8,128)(2,1)}, u32[]{:S(2)}) copy-start(bf16[192,192]{1,0:T(8,128)(2,1)} %wproj_ref.1) | copy-start | bytes 221188
  36.9 8.3 %collective-permute-start = (bf16[8,216,128]{2,1,0:T(8,128)(2,1)S(1)}, bf16[8,216,128]{2,1,0:T(8,128)(2,1)S(1)}, u32[]{:S(2)}, u32[]{:S(2)}) collective-permute-start(bf16[8,216,128]{2,1,0:T(8,128)(2,1)S(1)} %get-tuple-element.28), channel_id=1, source_target_pairs={{0,120},{8,0},{16,8},{24,16},{32,24},{40,32},{48,40},{56,48},{64,5... | collective-permute-start | bytes 1327112 | tf_op jit(solution)/shard_map/ppermute | solution.py:350
  45.2 0.8 copy-start.2
  142.7 1.4 collective-permute-start.3
  144.1 4.6 %collective-permute-start.4 = (f32[160,128]{1,0:T(8,128)S(1)}, f32[160,128]{1,0:T(8,128)S(1)}, u32[]{:S(2)}, u32[]{:S(2)}) collective-permute-start(f32[160,128]{1,0:T(8,128)S(1)} %add.28), channel_id=1, source_target_pairs={{0,16},{8,24},{16,0},{24,8},{32,48},{40,56},{48,32},{56,40},{64,80... | collective-permute-start | bytes 245768 | tf_op jit(solution)/shard_map/ppermute | solution.py:359
  148.7 4.5 %collective-permute-start.5 = (f32[160,128]{1,0:T(8,128)S(1)}, f32[160,128]{1,0:T(8,128)S(1)}, u32[]{:S(2)}, u32[]{:S(2)}) collective-permute-start(f32[160,128]{1,0:T(8,128)S(1)} %add.29), channel_id=1, source_target_pairs={{0,32},{8,40},{16,48},{24,56},{32,0},{40,8},{48,16},{56,24},{64,96... | collective-permute-start | bytes 245768 | tf_op jit(solution)/shard_map/ppermute | solution.py:359
  153.2 6.0 %collective-permute-start.6 = (f32[160,128]{1,0:T(8,128)S(1)}, f32[160,128]{1,0:T(8,128)S(1)}, u32[]{:S(2)}, u32[]{:S(2)}) collective-permute-start(f32[160,128]{1,0:T(8,128)S(1)} %add.30), channel_id=1, source_target_pairs={{0,64},{8,72},{16,80},{24,88},{32,96},{40,104},{48,112},{56,120},{... | collective-permute-start | bytes 245768 | tf_op jit(solution)/shard_map/ppermute | solution.py:359
  156.5 10.1 %collective-permute-start.2 = (bf16[8,216,128]{2,1,0:T(8,128)(2,1)S(1)}, bf16[8,216,128]{2,1,0:T(8,128)(2,1)S(1)}, u32[]{:S(2)}, u32[]{:S(2)}) collective-permute-start(bf16[8,216,128]{2,1,0:T(8,128)(2,1)S(1)} %get-tuple-element.26), channel_id=1, source_target_pairs={{0,8},{8,16},{16,24},{24,32},{32,40},{40,48},{48,56},{56,64},{64,7... | collective-permute-start | bytes 1327112 | tf_op jit(solution)/shard_map/ppermute | solution.py:355
  160.1 16.1 %all-to-all-start.2 = ((bf16[8,176,128]{2,1,0:T(8,128)(2,1)}), bf16[8,176,128]{2,1,0:T(8,128)(2,1)S(1)}, u32[]{:S(2)}, u32[]{:S(2)}) async-start(bf16[8,176,128]{2,1,0:T(8,128)(2,1)} %broadcast_in_dim.39), calls=%async_computation.2 | async-start | bytes 720896 | tf_op jit(solution)/shard_map/all_to_all | solution.py:364
  166.6 0.8 copy-start.3

commit v2 on v1

--- a/solution.py
+++ b/solution.py
@@ -149,13 +149,12 @@
 def main_kernel(
     xo_ref, xb_ref, t_ref, bias_ref, valid_ref, gain_ref, wkv_ref, wqkv_ref, wqkvt_ref, wproj_ref, wprojt_ref,
     out_ref,
-    x_s, t_s, xhat_s, rstd_s, n_s, v_s, qkvt_s, att_s, w_s, mixed_s, sqkv_s, sproj_s, sgain_s,
+    x_s, t_s, xhat_s, rstd_s, n_s, k_s, v_s, qkvt_s, attf_s, att_s, p_s, mixed_s, gat_s, tot_s, ds_s, grad_s,
+    sqkv_s, sproj_s, sgain_s,
 ):
     scale = SIZE ** (-0.5)
     to_exp2 = scale * 1.4426950408889634
-    gain = gain_ref[...]
-    eye_cells = identity(CELLS)
-    eye_c = identity(C)
+    last = 2 * M - 1
 
     for member in range(M):
         own = xo_ref[member].astype(F32)
@@ -169,37 +168,49 @@
     for block in range(2):
         t_s[block] = jnp.concatenate([unpack_half(own, block), unpack_half(beyond, block)], axis=0)
 
-    def forward(window, carry):
-        block = window // M
+
+    def project_qkv(window):
         x = x_s[window]
         centred = x - jnp.mean(x, axis=1, keepdims=True)
         rstd = lax.rsqrt(jnp.mean(centred * centred, axis=1, keepdims=True) + EPS)
         xhat = centred * rstd
         xhat_s[window] = xhat
         rstd_s[window] = rstd
-        normed = (xhat * gain).astype(BF)
+        normed = (xhat * gain_ref[...]).astype(BF)
         n_s[window] = normed
         kv = dot(normed, wkv_ref[...]).astype(BF)
-        keys = kv[:, :C]
+        k_s[window] = kv[:, :C]
         v_s[window] = kv[:, C:]
-        qkvt = dot_t(wqkvt_ref[...], normed).astype(BF)
-        qkvt_s[window] = qkvt
-        qt = qkvt[:C]
-        bias = bias_ref[block]
-        parts = []
-        for head in range(HEADS):
-            scores = dot(head_only(keys, head), qt)
-            expo = jnp.exp2(scores * to_exp2 + bias)
-            weights = expo * (1.0 / jnp.sum(expo, axis=0, keepdims=True))
-            w_s[window, head] = weights
-            vt = qkvt[2 * C + head * SIZE : 2 * C + (head + 1) * SIZE]
-            parts.append(dot(vt, weights.astype(BF)))
-        attended = jnp.concatenate(parts, axis=0).astype(BF)
-        att_s[window] = attended
-        projt = dot(wprojt_ref[...], attended).astype(BF)
-        mixed_s[window] = x + dot_t(eye_cells, projt)
+        qkvt_s[window] = dot_t(wqkvt_ref[...], normed).astype(BF)
+
+    def score_head(window, head):
+        scores = dot(head_only(k_s[window], head), qkvt_s[window, :C])
+        expo = jnp.exp2(scores * to_exp2 + bias_ref[window // M])
+        p_s[window, head] = (expo * (1.0 / jnp.sum(expo, axis=0, keepdims=True))).astype(BF)
+
+    def attend_head(window, head):
+        at = slice(head * SIZE, (head + 1) * SIZE)
+        attended = dot(qkvt_s[window, 2 * C + head * SIZE : 2 * C + (head + 1) * SIZE], p_s[window, head])
+        attf_s[window, at] = attended
+        att_s[window, at] = attended.astype(BF)
+
+    def heads(*stages):
+        for stage, window in stages:
+            for head in range(HEADS):
+                stage(window, head)
+
+    def forward(step, carry):
+        projt = dot(wprojt_ref[...], att_s[step]).astype(BF)
+        heads((attend_head, jnp.minimum(step + 1, last)), (score_head, jnp.minimum(step + 2, last)))
+        project_qkv(jnp.minimum(step + 3, last))
+        mixed_s[step] = x_s[step] + dot_t(identity(CELLS), projt)
         return carry
 
+    project_qkv(0)
+    heads((score_head, 0))
+    project_qkv(1)
+    heads((attend_head, 0), (score_head, 1))
+    project_qkv(2)
     lax.fori_loop(0, 2 * M, forward, 0)
 
     def crps(step, score):
@@ -236,46 +247,60 @@
     sproj_s[...] = jnp.zeros_like(sproj_s)
     sgain_s[...] = jnp.zeros_like(sgain_s)
 
-    def backward(window, carry):
-        grad_mixed = mixed_s[window]
-        grad_rows = grad_mixed.astype(BF)
-        attended = att_s[window]
-        gat = dot_t(wproj_ref[...], grad_rows).astype(BF)
-        sproj_s[...] += dot(attended, grad_rows)
-        values = v_s[window]
-        dq, dk, dv = [], [], []
+    def grad_attended(window):
+        gat = dot_t(wproj_ref[...], mixed_s[window].astype(BF)).astype(BF)
+        gat_s[window] = gat
+        product = gat.astype(F32) * attf_s[window]
         for head in range(HEADS):
-            at = slice(head * SIZE, (head + 1) * SIZE)
-            weights = w_s[window, head]
-            grad_probs = dot(head_only(values, head), gat)
-            total = jnp.sum(weights * grad_probs, axis=0, keepdims=True)
-            grad_scores = (weights * ((grad_probs - total) * scale)).astype(BF)
-            qt = qkvt_s[window, head * SIZE : (head + 1) * SIZE]
-            kt = qkvt_s[window, C + head * SIZE : C + (head + 1) * SIZE]
-            dq.append(dot(kt, grad_scores))
-            dk.append(dot_t(qt, grad_scores))
-            dv.append(dot_t(gat[at], weights.astype(BF)))
-        grad_qkvt = jnp.concatenate(dq + dk + dv, axis=0).astype(BF)
-        sqkv_s[...] += dot(grad_qkvt, n_s[window])
-        gbt = dot(wqkv_ref[...], grad_qkvt).astype(BF)
-        grad_normed = dot_t(eye_cells, gbt)
+            tot_s[window, head] = jnp.sum(product[head * SIZE : (head + 1) * SIZE], axis=0, keepdims=True)
+
+    def grad_score_head(window, head):
+        grad_probs = dot(head_only(v_s[window], head), gat_s[window])
+        ds_s[window % 4, head] = (grad_probs - tot_s[window, head]).astype(BF) * p_s[window, head]
+
+    def grad_qkv_head(window, head):
+        at = slice(head * SIZE, (head + 1) * SIZE)
+        grad_scores = ds_s[window % 4, head]
+        qt = qkvt_s[window, at]
+        kt = qkvt_s[window, C + head * SIZE : C + (head + 1) * SIZE]
+        grad_s[window, at] = (dot(kt, grad_scores) * scale).astype(BF)
+        grad_s[window, C + head * SIZE : C + (head + 1) * SIZE] = (dot_t(qt, grad_scores) * scale).astype(BF)
+        grad_s[window, 2 * C + head * SIZE : 2 * C + (head + 1) * SIZE] = dot_t(
+            gat_s[window, at], p_s[window, head]
+        ).astype(BF)
+
+    def grad_norm(window, gbt):
+        grad_normed = dot_t(identity(CELLS), gbt)
         xhat = xhat_s[window]
         sgain_s[...] += jnp.sum((grad_normed * xhat).reshape(18, 8, C), axis=0)
-        scaled = grad_normed * gain
+        scaled = grad_normed * gain_ref[...]
         first = jnp.mean(scaled, axis=1, keepdims=True)
         second = jnp.mean(scaled * xhat, axis=1, keepdims=True)
-        x_s[window] = grad_mixed + rstd_s[window] * (scaled - first - xhat * second)
+        x_s[window] = mixed_s[window] + rstd_s[window] * (scaled - first - xhat * second)
+
+    def backward(step, carry):
+        gbt = dot(wqkv_ref[...], grad_s[step]).astype(BF)
+        sqkv_s[...] += dot(grad_s[step], n_s[step])
+        sproj_s[...] += dot(att_s[step], mixed_s[step].astype(BF))
+        heads((grad_qkv_head, jnp.minimum(step + 1, last)), (grad_score_head, jnp.minimum(step + 2, last)))
+        grad_attended(jnp.minimum(step + 3, last))
+        grad_norm(step, gbt)
         return carry
 
+    grad_attended(0)
+    heads((grad_score_head, 0))
+    grad_attended(1)
+    heads((grad_qkv_head, 0), (grad_score_head, 1))
+    grad_attended(2)
     lax.fori_loop(0, 2 * M, backward, 0)
 
-    sqkv = dot_t(eye_c, sqkv_s[...].astype(BF))
+    sqkv = dot_t(identity(C), sqkv_s[...].astype(BF))
     sproj = sproj_s[...]
     pad = jnp.zeros((C, 64), F32)
     rest = jnp.concatenate([sqkv[:, 512:], pad], axis=1)
     rest = rest[:96] + pltpu.roll(rest[96:], 64, 1)
-    last = jnp.concatenate([sproj[:, 128:], pad], axis=1)
-    last = last[:96] + pltpu.roll(last[96:], 64, 1)
+    proj_rest = jnp.concatenate([sproj[:, 128:], pad], axis=1)
+    proj_rest = proj_rest[:96] + pltpu.roll(proj_rest[96:], 64, 1)
     sgain = jnp.sum(sgain_s[...], axis=0, keepdims=True)
     total = jnp.sum(jnp.sum(score, axis=0, keepdims=True), axis=1, keepdims=True)
     high = total.astype(BF).astype(F32)
@@ -288,7 +313,7 @@
     extra = extra + jnp.where((row == 2) & (lane == 0), jnp.broadcast_to(high, (128, 128)), 0.0)
     extra = extra + jnp.where((row == 2) & (lane == 1), jnp.broadcast_to(low, (128, 128)), 0.0)
     grads = jnp.concatenate(
-        [sqkv[:, 128 * i : 128 * (i + 1)] for i in range(4)] + [rest, sproj[:, :128], last, extra], axis=0
+        [sqkv[:, 128 * i : 128 * (i + 1)] for i in range(4)] + [rest, sproj[:, :128], proj_rest, extra], axis=0
     )
     for member in range(M):
         halves = []
@@ -311,10 +336,16 @@
             pltpu.VMEM((windows, CELLS, 1), F32),
             pltpu.VMEM((windows, CELLS, C), BF),
             pltpu.VMEM((windows, CELLS, C), BF),
+            pltpu.VMEM((windows, CELLS, C), BF),
             pltpu.VMEM((windows, 3 * C, CELLS), BF),
+            pltpu.VMEM((windows, C, CELLS), F32),
             pltpu.VMEM((windows, C, CELLS), BF),
-            pltpu.VMEM((windows, HEADS, CELLS, CELLS), F32),
+            pltpu.VMEM((windows, HEADS, CELLS, CELLS), BF),
             pltpu.VMEM((windows, CELLS, C), F32),
+            pltpu.VMEM((windows, C, CELLS), BF),
+            pltpu.VMEM((windows, HEADS, 1, CELLS), F32),
+            pltpu.VMEM((4, HEADS, CELLS, CELLS), BF),
+            pltpu.VMEM((windows, 3 * C, CELLS), BF),
             pltpu.VMEM((3 * C, C), F32),
             pltpu.VMEM((C, C), F32),
             pltpu.VMEM((8, C), F32),

time: 183 us -> 142 us (0.78)
  Pallas kernels: 87.6 us -> 47.3 us
    pallas_call x1, Pallas kernels: 74.8 us -> 34.5 us  [main(): pl.pallas_call(main_kernel, out_shape=jax.ShapeDtypeStruct((M, ROWS, 128)...]
  transfers between devices with their start and end apart: 9 -> 9, of which waited for: 7 -> 7; matrix products, arithmetic and copies ran while one was open for 6% -> 8% of each run, Pallas kernels for 3% -> 4%
where the time goes in v2:
time: 142 us; the launch traced here: 141 us
  Pallas kernels  47.3 us (33%)
  waiting for transfers between devices  28.2 us (20%)
  blocking collectives  22 us (15%)
  starting transfers between devices  20 us (14%)
  local copies, waits for them, and re-layouts  16.7 us (12%)
  other arithmetic  3.92 us (3%)
  between operations  3.28 us (2%)
    pallas_call x1, Pallas kernels, main(): pl.pallas_call(main_kernel, out_shape=jax.ShapeDtypeStruct((M, ROWS, 128)...  34.5 us
    all_to_all x1, blocking collectives, body(): back = lax.all_to_all(sent, 'mem', 0, 0, tiled=False)  22 us
    all_to_all x1, waiting for transfers between devices, body(): arrived = lax.all_to_all(packed, 'mem', 0, 0, tiled=False)  12.2 us
    ppermute x4, waiting for transfers between devices, body(): lax.ppermute(part, 'lon', [(i, i ^ bit) for i in range(strips)])  12 us
    unnamed x26, local copies, waits for them, and re-layouts  11.1 us
    all_to_all x1, starting transfers between devices, body(): arrived = lax.all_to_all(packed, 'mem', 0, 0, tiled=False)  8.01 us
    pallas_call x1, Pallas kernels, pack(): pl.pallas_call(pack_kernel, grid=(M,), in_specs=[pl.BlockSpec((1, 2, 12,...  6.72 us
    pallas_call x1, Pallas kernels, unpack(): pl.pallas_call(unpack_kernel, grid=(M,), in_specs=[pl.BlockSpec((1, PIECE...  6.08 us
  transfers between devices with their start and end apart: 9, of which 7 were waited for; matrix products, arithmetic and copies ran while one was open for 8% of the time, Pallas kernels for 4%

profile of v2, /device:TPU:0, one launch (start us, length us, event | category | flops | bytes accessed | tf_op | source)
XLA Modules:
  0.0 141.4 jit_solution(5141173661887092734)
XLA Ops:
  0.7 1.3 copy-done
  2.0 0.7 copy.36.t_ref
  2.7 3.1 %copy.29.x_ref = bf16[1,2,96,12,192]{4,3,2,1,0:T(8,128)(2,1)} copy(bf16[1,2,96,12,192]{4,2,3,1,0:T(8,128)(2,1)} %param.10) | data formatting | bytes 1769472 | tf_op args[0]
  5.8 6.7 %pack_strip.1 = (bf16[8,2,216,128]{3,2,1,0:T(8,128)(2,1)}, bf16[2,216,128]{2,1,0:T(8,128)(2,1)}) custom-call(bf16[1,2,96,12,192]{4,3,2,1,0:T(8,128)(2,1)} %copy.29.x_ref, bf16[2,12,12,192]{3,2,1,0:T(8,128)(2,1)} %copy.36.t_ref, bf16[144,192]{1,0:T(8,128)(2,1)} %constant.30.clone.place_ref), custom_call_target="tpu_custom_call" | custom-call | tf_op jit(solution)/shard_map/pack_strip/pallas_call | solution.py:96
  12.6 8.0 %all-to-all-start = ((bf16[8,2,216,128]{3,2,1,0:T(8,128)(2,1)}), bf16[8,2,216,128]{3,2,1,0:T(8,128)(2,1)S(1)}, u32[]{:S(2)}, u32[]{:S(2)}) async-start(bf16[8,2,216,128]{3,2,1,0:T(8,128)(2,1)} %get-tuple-element.7), calls=%async_computation | async-start | bytes 1769472 | tf_op jit(solution)/shard_map/all_to_all | solution.py:380
  20.6 2.4 %collective-permute-start.1 = (bf16[216,128]{1,0:T(8,128)(2,1)S(1)}, bf16[216,128]{1,0:T(8,128)(2,1)S(1)}, u32[]{:S(2)}, u32[]{:S(2)}) collective-permute-start(bf16[216,128]{1,0:T(8,128)(2,1)S(1)} %get-tuple-element.37), channel_id=1, source_target_pairs={{0,120},{8,0},{16,8},{24,16},{32,24},{40,32},{48,40},{56,48},{64,5... | collective-permute-start | bytes 165896 | tf_op jit(solution)/shard_map/ppermute | solution.py:379
  23.1 0.1 dynamic_slice.10
  23.2 0.1 broadcast_in_dim.32
  23.3 0.1 eq.33
  23.4 0.1 broadcast_compare_fusion
  23.5 0.1 eq.39
  23.6 0.1 broadcast_in_dim.34
  23.7 0.1 eq.40
  23.8 12.2 %all-to-all-done = bf16[8,2,216,128]{3,2,1,0:T(8,128)(2,1)S(1)} async-done(((bf16[8,2,216,128]{3,2,1,0:T(8,128)(2,1)}), bf16[8,2,216,128]{3,2,1,0:T(8,128)(2,1)S(1)}, u32[]{:S(2)}, u32[]{:S(2)}) %all-to-all-start) | async-done | bytes 884768 | tf_op jit(solution)/shard_map/all_to_all | solution.py:380
  36.0 0.8 slice_bitcast_fusion
  36.9 2.5 %collective-permute-start = (bf16[8,216,128]{2,1,0:T(8,128)(2,1)S(1)}, bf16[8,216,128]{2,1,0:T(8,128)(2,1)S(1)}, u32[]{:S(2)}, u32[]{:S(2)}) collective-permute-start(bf16[8,216,128]{2,1,0:T(8,128)(2,1)S(1)} %get-tuple-element.28), channel_id=1, source_target_pairs={{0,120},{8,0},{16,8},{24,16},{32,24},{40,32},{48,40},{56,48},{64,5... | collective-permute-start | bytes 1327112 | tf_op jit(solution)/shard_map/ppermute | solution.py:381
  39.4 0.9 and_select_fusion.bias_ref
  40.2 0.1 dynamic-slice_convert_fusion
  40.3 0.9 copy.32
  41.2 0.8 slice.87.wkv_ref
  41.9 0.1 convert_element_type.31
  42.1 0.8 convert_element_type.37.valid_ref
  42.9 0.7 copy.33
  43.6 0.6 pad_maximum_fusion.t_ref
  44.2 0.9 collective-permute-done.xb_ref
  45.2 0.8 copy-done.2
  45.9 34.5 %window_attention_crps.1 = bf16[8,592,128]{2,1,0:T(8,128)(2,1)} custom-call(bf16[8,216,128]{2,1,0:T(8,128)(2,1)} %get-tuple-element.29.xo_ref, bf16[8,216,128]{2,1,0:T(8,128)(2,1)} %copy-done.2, bf16[2,216,128]{2,1,0:T(8,128)(2,1)} %pad_maximum_fusion.t_ref, f32[2,144,144]{2,1,0:T(8,128)} %and_select_fusion.bias_ref, ...), custom_call_target="tpu_custom_call" | custom-call | tf_op jit(solution)/shard_map/window_attention_crps/pallas_call | solution.py:329
  80.4 22.0 %all_to_all.15 = bf16[8,592,128]{2,1,0:T(8,128)(2,1)S(1)} all-to-all(bf16[8,592,128]{2,1,0:T(8,128)(2,1)} %window_attention_crps.1), channel_id=1, replica_groups=mesh['lon'=16,'mem'=8] {'mem'}, dimensions={0} | all-to-all | bytes 2424832 | tf_op jit(solution)/shard_map/all_to_all | solution.py:385
  102.4 0.1 collective-permute-start.3
  102.5 1.3 collective-permute-done.3
  103.8 0.2 collective-permute-start.4
  104.0 4.4 %collective-permute-done.4 = f32[160,128]{1,0:T(8,128)S(1)} collective-permute-done((f32[160,128]{1,0:T(8,128)S(1)}, f32[160,128]{1,0:T(8,128)S(1)}, u32[]{:S(2)}, u32[]{:S(2)}) %collective-permute-start.4) | collective-permute-done | bytes 81952 | tf_op jit(solution)/shard_map/ppermute | solution.py:390
  108.4 0.9 collective-permute-start.5
  109.3 3.6 %collective-permute-done.5 = f32[160,128]{1,0:T(8,128)S(1)} collective-permute-done((f32[160,128]{1,0:T(8,128)S(1)}, f32[160,128]{1,0:T(8,128)S(1)}, u32[]{:S(2)}, u32[]{:S(2)}) %collective-permute-start.5) | collective-permute-done | bytes 81952 | tf_op jit(solution)/shard_map/ppermute | solution.py:390
  112.9 2.4 %collective-permute-start.6 = (f32[160,128]{1,0:T(8,128)S(1)}, f32[160,128]{1,0:T(8,128)S(1)}, u32[]{:S(2)}, u32[]{:S(2)}) collective-permute-start(f32[160,128]{1,0:T(8,128)S(1)} %add.30), channel_id=1, source_target_pairs={{0,64},{8,72},{16,80},{24,88},{32,96},{40,104},{48,112},{56,120},{... | collective-permute-start | bytes 245768 | tf_op jit(solution)/shard_map/ppermute | solution.py:390
  115.4 0.8 fusion.2
  116.2 2.8 %collective-permute-done.6 = f32[160,128]{1,0:T(8,128)S(1)} collective-permute-done((f32[160,128]{1,0:T(8,128)S(1)}, f32[160,128]{1,0:T(8,128)S(1)}, u32[]{:S(2)}, u32[]{:S(2)}) %collective-permute-start.6) | collective-permute-done | bytes 81952 | tf_op jit(solution)/shard_map/ppermute | solution.py:390
  119.0 0.8 broadcast_in_dim.39
  119.8 3.4 %all-to-all-start.2 = ((bf16[8,176,128]{2,1,0:T(8,128)(2,1)}), bf16[8,176,128]{2,1,0:T(8,128)(2,1)S(1)}, u32[]{:S(2)}, u32[]{:S(2)}) async-start(bf16[8,176,128]{2,1,0:T(8,128)(2,1)} %broadcast_in_dim.39), calls=%async_computation.2 | async-start | bytes 720896 | tf_op jit(solution)/shard_map/all_to_all | solution.py:395
  123.3 3.0 %collective-permute-done.2.beyond_ref = bf16[8,216,128]{2,1,0:T(8,128)(2,1)S(1)} collective-permute-done((bf16[8,216,128]{2,1,0:T(8,128)(2,1)S(1)}, bf16[8,216,128]{2,1,0:T(8,128)(2,1)S(1)}, u32[]{:S(2)}, u32[]{:S(2)}) %collective-permute-start.2) | collective-permute-done | bytes 442400 | tf_op jit(solution)/shard_map/ppermute | solution.py:386
  126.3 0.8 copy-done.3
  127.0 6.1 %unpack_strip.1 = bf16[1,2,96,12,192]{4,3,2,1,0:T(8,128)(2,1)} custom-call(bf16[8,216,128]{2,1,0:T(8,128)(2,1)} %get-tuple-element.27.own_ref, bf16[8,216,128]{2,1,0:T(8,128)(2,1)} %copy-done.3, bf16[192,144]{1,0:T(8,128)(2,1)} %constant.32.clone.place_ref), custom_call_target="tpu_custom_call" | custom-call | tf_op jit(solution)/shard_map/unpack_strip/pallas_call | solution.py:130
  133.1 2.8 %copy.35 = bf16[1,2,96,12,192]{4,2,3,1,0:T(8,128)(2,1)} copy(bf16[1,2,96,12,192]{4,3,2,1,0:T(8,128)(2,1)} %unpack_strip.1) | data formatting | bytes 1769472
  136.0 0.1 fusion.4
  136.2 0.6 fusion.6
  136.8 0.8 broadcast_multiply_fusion
  137.7 0.6 slice_multiply_fusion
  139.5 0.7 maximum_multiply_fusion
  (39 shorter events, 0.5 us)
Async XLA Ops:
  0.6 1.3 copy-start
  12.6 8.0 %copy-start.5 = (bf16[2,216,128]{2,1,0:T(8,128)(2,1)S(1)}, bf16[2,216,128]{2,1,0:T(8,128)(2,1)}, u32[]{:S(2)}) copy-start(bf16[2,216,128]{2,1,0:T(8,128)(2,1)} %get-tuple-element.8) | copy-start | bytes 331780
  12.6 10.5 %copy-start.7 = (s32[96]{0:T(128)S(1)}, s32[96]{0:T(128)}, u32[]{:S(2)}) copy-start(s32[96]{0:T(128)} %param.15) | copy-start | bytes 1156
  12.6 10.9 %copy-start.8 = (s32[96]{0:T(128)S(1)}, s32[96]{0:T(128)}, u32[]{:S(2)}) copy-start(s32[96]{0:T(128)} %param.16) | copy-start | bytes 1156
  12.6 23.5 %all-to-all-start = ((bf16[8,2,216,128]{3,2,1,0:T(8,128)(2,1)}), bf16[8,2,216,128]{3,2,1,0:T(8,128)(2,1)S(1)}, u32[]{:S(2)}, u32[]{:S(2)}) async-start(bf16[8,2,216,128]{3,2,1,0:T(8,128)(2,1)} %get-tuple-element.7), calls=%async_computation | async-start | bytes 1769472 | tf_op jit(solution)/shard_map/all_to_all | solution.py:380
  20.6 18.8 %copy-start.6 = (pred[144,144]{1,0:T(8,128)(4,1)S(1)}, pred[144,144]{1,0:T(8,128)(4,1)}, u32[]{:S(2)}) copy-start(pred[144,144]{1,0:T(8,128)(4,1)} %constant.35) | copy-start | bytes 62212
  20.6 19.7 %copy-start.1 = (bf16[192,576]{1,0:T(8,128)(2,1)S(1)}, bf16[192,576]{1,0:T(8,128)(2,1)}, u32[]{:S(2)}) copy-start(bf16[192,576]{1,0:T(8,128)(2,1)} %wqkv_ref.1) | copy-start | bytes 663556
  20.6 23.0 %collective-permute-start.1 = (bf16[216,128]{1,0:T(8,128)(2,1)S(1)}, bf16[216,128]{1,0:T(8,128)(2,1)S(1)}, u32[]{:S(2)}, u32[]{:S(2)}) collective-permute-start(bf16[216,128]{1,0:T(8,128)(2,1)S(1)} %get-tuple-element.37), channel_id=1, source_target_pairs={{0,120},{8,0},{16,8},{24,16},{32,24},{40,32},{48,40},{56,48},{64,5... | collective-permute-start | bytes 165896 | tf_op jit(solution)/shard_map/ppermute | solution.py:379
  23.8 19.1 %copy-start.4 = (bf16[192,192]{1,0:T(8,128)(2,1)S(1)}, bf16[192,192]{1,0:T(8,128)(2,1)}, u32[]{:S(2)}) copy-start(bf16[192,192]{1,0:T(8,128)(2,1)} %wproj_ref.1) | copy-start | bytes 221188
  36.9 8.3 %collective-permute-start = (bf16[8,216,128]{2,1,0:T(8,128)(2,1)S(1)}, bf16[8,216,128]{2,1,0:T(8,128)(2,1)S(1)}, u32[]{:S(2)}, u32[]{:S(2)}) collective-permute-start(bf16[8,216,128]{2,1,0:T(8,128)(2,1)S(1)} %get-tuple-element.28), channel_id=1, source_target_pairs={{0,120},{8,0},{16,8},{24,16},{32,24},{40,32},{48,40},{56,48},{64,5... | collective-permute-start | bytes 1327112 | tf_op jit(solution)/shard_map/ppermute | solution.py:381
  45.2 0.8 copy-start.2
  102.4 1.4 collective-permute-start.3
  103.8 4.6 %collective-permute-start.4 = (f32[160,128]{1,0:T(8,128)S(1)}, f32[160,128]{1,0:T(8,128)S(1)}, u32[]{:S(2)}, u32[]{:S(2)}) collective-permute-start(f32[160,128]{1,0:T(8,128)S(1)} %add.28), channel_id=1, source_target_pairs={{0,16},{8,24},{16,0},{24,8},{32,48},{40,56},{48,32},{56,40},{64,80... | collective-permute-start | bytes 245768 | tf_op jit(solution)/shard_map/ppermute | solution.py:390
  108.4 4.5 %collective-permute-start.5 = (f32[160,128]{1,0:T(8,128)S(1)}, f32[160,128]{1,0:T(8,128)S(1)}, u32[]{:S(2)}, u32[]{:S(2)}) collective-permute-start(f32[160,128]{1,0:T(8,128)S(1)} %add.29), channel_id=1, source_target_pairs={{0,32},{8,40},{16,48},{24,56},{32,0},{40,8},{48,16},{56,24},{64,96... | collective-permute-start | bytes 245768 | tf_op jit(solution)/shard_map/ppermute | solution.py:390
  112.9 6.0 %collective-permute-start.6 = (f32[160,128]{1,0:T(8,128)S(1)}, f32[160,128]{1,0:T(8,128)S(1)}, u32[]{:S(2)}, u32[]{:S(2)}) collective-permute-start(f32[160,128]{1,0:T(8,128)S(1)} %add.30), channel_id=1, source_target_pairs={{0,64},{8,72},{16,80},{24,88},{32,96},{40,104},{48,112},{56,120},{... | collective-permute-start | bytes 245768 | tf_op jit(solution)/shard_map/ppermute | solution.py:390
  116.2 10.1 %collective-permute-start.2 = (bf16[8,216,128]{2,1,0:T(8,128)(2,1)S(1)}, bf16[8,216,128]{2,1,0:T(8,128)(2,1)S(1)}, u32[]{:S(2)}, u32[]{:S(2)}) collective-permute-start(bf16[8,216,128]{2,1,0:T(8,128)(2,1)S(1)} %get-tuple-element.26), channel_id=1, source_target_pairs={{0,8},{8,16},{16,24},{24,32},{32,40},{40,48},{48,56},{56,64},{64,7... | collective-permute-start | bytes 1327112 | tf_op jit(solution)/shard_map/ppermute | solution.py:386
  119.8 16.1 %all-to-all-start.2 = ((bf16[8,176,128]{2,1,0:T(8,128)(2,1)}), bf16[8,176,128]{2,1,0:T(8,128)(2,1)S(1)}, u32[]{:S(2)}, u32[]{:S(2)}) async-start(bf16[8,176,128]{2,1,0:T(8,128)(2,1)} %broadcast_in_dim.39), calls=%async_computation.2 | async-start | bytes 720896 | tf_op jit(solution)/shard_map/all_to_all | solution.py:395
  126.3 0.8 copy-start.3

commit v3 on v2

v3 whole, which is shorter than its diff:
```python
import functools

import jax
import jax.numpy as jnp
import numpy as np
from jax import lax
from jax.experimental import pallas as pl
from jax.experimental.pallas import tpu as pltpu
from jax.sharding import PartitionSpec as P

HEADS = 6
SIZE = 32
SHIFT = 6
C = 192
CELLS = 144
HALF = 72
M = 8
EPS = 1e-05
DELTA_SQ = 0.0625
PIECE = 112
GRAD_ROWS = 80
LOW_ROWS = 16
BF = jnp.bfloat16
F32 = jnp.float32
VMEM_LIMIT = 40 * 1024 * 1024


def dot(left, right):
    return jnp.dot(left, right, preferred_element_type=F32)


def dot_t(left, right):
    return lax.dot_general(left, right, (((1,), (1,)), ((), ())), preferred_element_type=F32)


def identity(n):
    return (
        lax.broadcasted_iota(jnp.int32, (n, n), 0) == lax.broadcasted_iota(jnp.int32, (n, n), 1)
    ).astype(BF)


def pack_half(cells):
    rest = jnp.concatenate([cells[:, 128:], jnp.zeros((HALF, 64), F32)], axis=1)
    second = jnp.concatenate([rest[40:], jnp.zeros((8, 128), F32)], axis=0)
    return jnp.concatenate([cells[:, :128], rest[:40] + pltpu.roll(second, 64, 1)], axis=0)


def unpack_half(piece):
    rest = piece[HALF:]
    rest = jnp.concatenate([rest[:, :64], pltpu.roll(rest, 64, 1)[:32, :64]], axis=0)
    return jnp.concatenate([piece[:HALF], rest], axis=1)


TILES = ((0,), (0, 1), (0, 1), (1,))
FIRST = (0, 0, 1, 1)


def place_matrices():
    cell = np.arange(288)
    half, block, level, row, column = cell // 144, cell // 72 % 2, cell // 36 % 2, cell // 6 % 6, cell % 6
    out = np.zeros((4, 2, 2, 288, 192), np.float32)
    for i, first in enumerate(FIRST):
        lat = 12 * i + 6 * block + row
        out[i, lat // 16 - first, level, cell, (half * 6 + column) * 16 + lat % 16] = 1.0
    return out


def cell_parts():
    cell = lax.broadcasted_iota(jnp.int32, (CELLS, 1), 0)
    block = (cell >= 72).astype(jnp.int32)
    cell = cell - 72 * block
    level = (cell >= 36).astype(jnp.int32)
    cell = cell - 36 * level
    row = sum((cell >= 6 * k).astype(jnp.int32) for k in range(1, 6))
    return 6 * block + row, level, cell - 6 * row


def place_of(parts, i, first, level, s):
    row, its_level, column = parts
    lat = 12 * i + row - 16 * (first + s)
    return jnp.where((lat >= 0) & (lat < 16) & (its_level == level), column * 16 + lat, -1)


def gather_group(place, steps, tile):
    lane = lax.broadcasted_iota(jnp.int32, (CELLS, 96), 1)
    cells = None
    for s in steps:
        for level in range(2):
            part = dot((place(level, s) == lane).astype(F32).astype(BF), tile(level, s))
            cells = part if cells is None else cells + part
    return cells


def pack_kernel(at_ref, x_hbm, out_ref, x_ref, semaphore):
    copy = pltpu.make_async_copy(x_hbm.at[0, :, pl.ds(at_ref[0] * 6, 6)], x_ref, semaphore)
    copy.start()
    parts = cell_parts()
    copy.wait()
    for quad in range(2):
        for i in range(4):

            def tile(level, s):
                at = 16 * (3 * quad + FIRST[i] + s)
                return x_ref[level, :, at : at + 16, :].reshape(96, C)

            def place(level, s):
                return place_of(parts, i, FIRST[i], level, s)

            cells = gather_group(place, TILES[i], tile)
            for sub in range(2):
                out_ref[8 * quad + 2 * i + sub] = pack_half(cells[sub * HALF : (sub + 1) * HALF]).astype(BF)


def pack(half, inputs):
    return pl.pallas_call(
        pack_kernel,
        in_specs=[SCALARS, pl.BlockSpec(memory_space=pl.ANY)],
        out_specs=WHOLE,
        out_shape=jax.ShapeDtypeStruct((2 * M, PIECE, 128), BF),
        scratch_shapes=[pltpu.VMEM((2, 6, 96, C), BF), pltpu.SemaphoreType.DMA],
        compiler_params=PARAMS,
        name="pack_strip",
    )(half, inputs)


def pack_target_kernel(at_ref, t_ref, even_keep, even_send, odd_keep, odd_send):
    member, odd_strip = at_ref[0], at_ref[1] == 1
    i = member // 2
    first = jnp.where(i >= 2, 1, 0)
    second = member % 2 == 1
    parts = cell_parts()
    pieces = []
    for quad in range(2):
        for half in range(2):

            def tile(level, s):
                at = pl.multiple_of(16 * (3 * quad + first + s), 16)
                return t_ref[level, 6 * half : 6 * half + 6, pl.ds(at, 16), :].reshape(96, C)

            def place(level, s):
                return place_of(parts, i, first, level, s)

            cells = gather_group(place, (0, 1), tile)
            pieces.append(pack_half(jnp.where(second, cells[HALF:], cells[:HALF])))
    low_west, low_east, high_west, high_east = pieces
    even_keep[...] = jnp.where(odd_strip, high_west, low_east).astype(BF)
    even_send[...] = jnp.where(odd_strip, low_west, high_east).astype(BF)
    odd_keep[...] = jnp.where(odd_strip, low_east, high_west).astype(BF)
    odd_send[...] = jnp.where(odd_strip, high_east, low_west).astype(BF)


def pack_target(at, target):
    return pl.pallas_call(
        pack_target_kernel,
        in_specs=[SCALARS, WHOLE],
        out_specs=[WHOLE] * 4,
        out_shape=[jax.ShapeDtypeStruct((PIECE, 128), BF)] * 4,
        compiler_params=PARAMS,
        name="pack_target",
    )(at, target)


WHOLE = pl.BlockSpec(memory_space=pltpu.VMEM)
SCALARS = pl.BlockSpec(memory_space=pltpu.SMEM)
PARAMS = pltpu.CompilerParams(vmem_limit_bytes=VMEM_LIMIT)


def unpack_kernel(at_ref, even_ref, odd_ref, place_ref, out_ref):
    odd_strip = at_ref[1] == 1
    for quad in range(2):
        groups = []
        for i in range(4):
            wests, easts = [], []
            for sub in range(2):
                even = even_ref[8 * quad + 2 * i + sub].astype(F32)
                odd = odd_ref[8 * quad + 2 * i + sub, :PIECE].astype(F32)
                wests.append(unpack_half(jnp.where(odd_strip, even, odd)))
                easts.append(unpack_half(jnp.where(odd_strip, odd, even)))
            groups.append(jnp.concatenate(wests + easts, axis=0).astype(BF))
        for t in range(3):
            at = 16 * (3 * quad + t)
            for level in range(2):
                slab = None
                for i in range(4):
                    if t - FIRST[i] in TILES[i]:
                        part = dot(place_ref[i, t - FIRST[i], level], groups[i])
                        slab = part if slab is None else slab + part
                out_ref[0, level, :, at : at + 16, :] = slab.astype(BF).reshape(12, 16, C)


def unpack(at, even, odd, place_t):
    return pl.pallas_call(
        unpack_kernel,
        in_specs=[SCALARS, WHOLE, WHOLE, WHOLE],
        out_specs=WHOLE,
        out_shape=jax.ShapeDtypeStruct((1, 2, 12, 96, C), BF),
        compiler_params=PARAMS,
        name="unpack_strip",
    )(at, even, odd, place_t)


def split_low(total, copies):
    high = total.astype(BF)
    low = (total - high.astype(F32))[32 : 32 + LOW_ROWS].astype(BF)
    return jnp.broadcast_to(jnp.concatenate([high, low], axis=0)[None], (copies, GRAD_ROWS + LOW_ROWS, 128))


def first_sum_kernel(back_ref, out_ref):
    total = jnp.sum(back_ref[:, PIECE:].astype(F32), axis=0)
    out_ref[...] = split_low(total, out_ref.shape[0])


def second_sum_kernel(parts_ref, out_ref):
    total = jnp.sum(parts_ref[...].astype(F32), axis=0)
    low = jnp.concatenate(
        [jnp.zeros((32, 128), F32), total[GRAD_ROWS:], jnp.zeros((GRAD_ROWS - 32 - LOW_ROWS, 128), F32)], axis=0
    )
    out_ref[...] = split_low(total[:GRAD_ROWS] + low, out_ref.shape[0])


def finish_kernel(scale, per_score, grads_ref, qkv_out, proj_out, gain_out, loss_out):
    rows = grads_ref[:, :GRAD_ROWS].astype(F32).reshape(2 * M * GRAD_ROWS, 128) * scale
    for i in range(4):
        qkv_out[:, 128 * i : 128 * (i + 1)] = rows[i * C : (i + 1) * C]
    rest = rows[768:864]
    qkv_out[:, 512:] = jnp.concatenate([rest[:, :64], pltpu.roll(rest, 64, 1)[:, :64]], axis=0)
    rest = rows[1056:1152]
    proj_out[:, :128] = rows[864:1056]
    proj_out[:, 128:] = jnp.concatenate([rest[:, :64], pltpu.roll(rest, 64, 1)[:, :64]], axis=0)
    piece = 1152 // GRAD_ROWS
    extra = grads_ref[piece, 32 : 32 + LOW_ROWS].astype(F32) + grads_ref[piece, GRAD_ROWS:].astype(F32)
    gain_out[...] = jnp.concatenate([extra[0:1], extra[1:2, :64]], axis=1) * scale
    loss_out[...] = (extra[2:3, 0:1] + extra[2:3, 1:2]) * per_score


def small(kernel, name, out_shape, *args):
    return pl.pallas_call(
        kernel,
        in_specs=[WHOLE] * len(args),
        out_specs=jax.tree.map(lambda _: WHOLE, out_shape),
        out_shape=out_shape,
        compiler_params=PARAMS,
        name=name,
    )(*args)


def head_only(field, head):
    lane = lax.broadcasted_iota(jnp.int32, field.shape, 1)
    return jnp.where((lane >= head * SIZE) & (lane < (head + 1) * SIZE), field, jnp.zeros_like(field))


def main_kernel(
    at_ref, x_ref, tk_ref, tr_ref, bias_ref, valid_ref, gain_ref, wkv_ref, wqkv_ref, wqkvt_ref, wproj_ref, wprojt_ref,
    *refs,
):
    refs = list(refs)
    start = [refs.pop(0) for _ in range(4)] if len(refs) > 21 else None
    out_ref = refs.pop(0)
    (x_s, t_s, xhat_s, rstd_s, n_s, k_s, v_s, qkvt_s, attf_s, att_s, p_s, mixed_s, gat_s, tot_s, ds_s, grad_s) = refs[-16:]
    sqkv_s, sproj_s, sgain_s, score_s = refs[:-16]
    scale = SIZE ** (-0.5)
    to_exp2 = scale * 1.4426950408889634
    last = M - 1

    for member in range(M):
        x_s[member] = jnp.concatenate(
            [unpack_half(x_ref[member].astype(F32)), unpack_half(x_ref[M + member].astype(F32))], axis=0
        )
    kept = unpack_half(tk_ref[...].astype(F32))
    received = unpack_half(tr_ref[...].astype(F32))
    eastern = at_ref[0] == 1
    t_s[...] = jnp.concatenate(
        [jnp.where(eastern, received, kept), jnp.where(eastern, kept, received)], axis=0
    )


    def project_qkv(window):
        x = x_s[window]
        centred = x - jnp.mean(x, axis=1, keepdims=True)
        rstd = lax.rsqrt(jnp.mean(centred * centred, axis=1, keepdims=True) + EPS)
        xhat = centred * rstd
        xhat_s[window] = xhat
        rstd_s[window] = rstd
        normed = (xhat * gain_ref[...]).astype(BF)
        n_s[window] = normed
        kv = dot(normed, wkv_ref[...]).astype(BF)
        k_s[window] = kv[:, :C]
        v_s[window] = kv[:, C:]
        qkvt_s[window] = dot_t(wqkvt_ref[...], normed).astype(BF)

    def score_head(window, head):
        scores = dot(head_only(k_s[window], head), qkvt_s[window, :C])
        expo = jnp.exp2(scores * to_exp2 + bias_ref[...])
        p_s[window, head] = (expo * (1.0 / jnp.sum(expo, axis=0, keepdims=True))).astype(BF)

    def attend_head(window, head):
        at = slice(head * SIZE, (head + 1) * SIZE)
        attended = dot(qkvt_s[window, 2 * C + head * SIZE : 2 * C + (head + 1) * SIZE], p_s[window, head])
        attf_s[window, at] = attended
        att_s[window, at] = attended.astype(BF)

    def heads(*stages):
        for stage, window in stages:
            for head in range(HEADS):
                stage(window, head)

    def forward(step, carry):
        projt = dot(wprojt_ref[...], att_s[step]).astype(BF)
        heads((attend_head, jnp.minimum(step + 1, last)), (score_head, jnp.minimum(step + 2, last)))
        project_qkv(jnp.minimum(step + 3, last))
        mixed_s[step] = x_s[step] + dot_t(identity(CELLS), projt)
        return carry

    project_qkv(0)
    heads((score_head, 0))
    project_qkv(1)
    heads((attend_head, 0), (score_head, 1))
    project_qkv(2)
    lax.fori_loop(0, M, forward, 0)

    def crps(step, score):
        rows = pl.ds(pl.multiple_of(step * 8, 8), 8)
        valid = valid_ref[rows]
        target = t_s[rows]
        mixed = [mixed_s[m, rows] for m in range(M)]
        rounded = [value.astype(BF).astype(F32) for value in mixed]
        slopes = [None] * M
        pairs = None
        for m in range(M):
            for n in range(m + 1, M):
                diff = rounded[m] - rounded[n]
                square = diff * diff + DELTA_SQ
                inverse = lax.rsqrt(square)
                size = square * inverse
                slope = diff * inverse
                pairs = size if pairs is None else pairs + size
                slopes[m] = slope if slopes[m] is None else slopes[m] + slope
                slopes[n] = -slope if slopes[n] is None else slopes[n] - slope
        total = -(2.0 * pairs + M * DELTA_SQ**0.5) / (2.0 * M)
        for m in range(M):
            diff = mixed[m] - target
            square = diff * diff + DELTA_SQ
            inverse = lax.rsqrt(square)
            total = total + square * inverse
            mixed_s[m, rows] = valid * (diff * inverse - slopes[m] / M)
        return score + valid * total

    if start is None:
        sqkv_s[...] = jnp.zeros_like(sqkv_s)
        sproj_s[...] = jnp.zeros_like(sproj_s)
        sgain_s[...] = jnp.zeros_like(sgain_s)
        score_s[...] = jnp.zeros_like(score_s)
    else:
        for ref, begin in zip((sqkv_s, sproj_s, sgain_s, score_s), start):
            ref[...] = begin[...]
    score_s[...] = lax.fori_loop(0, 18, crps, score_s[...])

    def grad_attended(window):
        gat = dot_t(wproj_ref[...], mixed_s[window].astype(BF)).astype(BF)
        gat_s[window] = gat
        product = gat.astype(F32) * attf_s[window]
        for head in range(HEADS):
            tot_s[window, head] = jnp.sum(product[head * SIZE : (head + 1) * SIZE], axis=0, keepdims=True)

    def grad_score_head(window, head):
        grad_probs = dot(head_only(v_s[window], head), gat_s[window])
        ds_s[window % 4, head] = (grad_probs - tot_s[window, head]).astype(BF) * p_s[window, head]

    def grad_qkv_head(window, head):
        at = slice(head * SIZE, (head + 1) * SIZE)
        grad_scores = ds_s[window % 4, head]
        qt = qkvt_s[window, at]
        kt = qkvt_s[window, C + head * SIZE : C + (head + 1) * SIZE]
        grad_s[window, at] = (dot(kt, grad_scores) * scale).astype(BF)
        grad_s[window, C + head * SIZE : C + (head + 1) * SIZE] = (dot_t(qt, grad_scores) * scale).astype(BF)
        grad_s[window, 2 * C + head * SIZE : 2 * C + (head + 1) * SIZE] = dot_t(
            gat_s[window, at], p_s[window, head]
        ).astype(BF)

    def grad_norm(window, gbt):
        grad_normed = dot_t(identity(CELLS), gbt)
        xhat = xhat_s[window]
        sgain_s[...] += jnp.sum((grad_normed * xhat).reshape(18, 8, C), axis=0)
        scaled = grad_normed * gain_ref[...]
        first = jnp.mean(scaled, axis=1, keepdims=True)
        second = jnp.mean(scaled * xhat, axis=1, keepdims=True)
        x_s[window] = mixed_s[window] + rstd_s[window] * (scaled - first - xhat * second)

    def backward(step, carry):
        gbt = dot(wqkv_ref[...], grad_s[step]).astype(BF)
        sqkv_s[...] += dot(grad_s[step], n_s[step])
        sproj_s[...] += dot(att_s[step], mixed_s[step].astype(BF))
        heads((grad_qkv_head, jnp.minimum(step + 1, last)), (grad_score_head, jnp.minimum(step + 2, last)))
        grad_attended(jnp.minimum(step + 3, last))
        grad_norm(step, gbt)
        return carry

    grad_attended(0)
    heads((grad_score_head, 0))
    grad_attended(1)
    heads((grad_qkv_head, 0), (grad_score_head, 1))
    grad_attended(2)
    lax.fori_loop(0, M, backward, 0)

    def pieces(member):
        return [pack_half(x_s[member, half * HALF : (half + 1) * HALF]).astype(BF) for half in range(2)]

    if start is None:
        for member in range(M):
            for half, piece in enumerate(pieces(member)):
                out_ref[half * M + member] = piece
        return

    sqkv = dot_t(identity(C), sqkv_s[...].astype(BF))
    sproj = sproj_s[...]
    pad = jnp.zeros((C, 64), F32)
    rest = jnp.concatenate([sqkv[:, 512:], pad], axis=1)
    rest = rest[:96] + pltpu.roll(rest[96:], 64, 1)
    proj_rest = jnp.concatenate([sproj[:, 128:], pad], axis=1)
    proj_rest = proj_rest[:96] + pltpu.roll(proj_rest[96:], 64, 1)
    sgain = jnp.sum(sgain_s[...], axis=0, keepdims=True)
    total = jnp.sum(jnp.sum(score_s[...], axis=0, keepdims=True), axis=1, keepdims=True)
    high = total.astype(BF).astype(F32)
    low = (total - high).astype(BF).astype(F32)
    row = lax.broadcasted_iota(jnp.int32, (128, 128), 0)
    lane = lax.broadcasted_iota(jnp.int32, (128, 128), 1)
    extra = jnp.where(row == 0, jnp.broadcast_to(sgain[:, :128], (128, 128)), 0.0)
    wide = jnp.concatenate([sgain[:, 128:], jnp.zeros((1, 64), F32)], axis=1)
    extra = extra + jnp.where(row == 1, jnp.broadcast_to(wide, (128, 128)), 0.0)
    extra = extra + jnp.where((row == 2) & (lane == 0), jnp.broadcast_to(high, (128, 128)), 0.0)
    extra = extra + jnp.where((row == 2) & (lane == 1), jnp.broadcast_to(low, (128, 128)), 0.0)
    grads = jnp.concatenate(
        [sqkv[:, 128 * i : 128 * (i + 1)] for i in range(4)] + [rest, sproj[:, :128], proj_rest, extra], axis=0
    ).astype(BF)
    for member in range(M):
        for half, piece in enumerate(pieces(member)):
            to = half * M + member
            out_ref[to] = jnp.concatenate([piece, grads[to * GRAD_ROWS : (to + 1) * GRAD_ROWS]], axis=0)


SUMS = [(3 * C, C), (C, C), (8, C), (8, C)]


def main(at, pieces, target_kept, target_received, bias, valid, gain, w_qkv, w_proj, sums=()):
    total = [jax.ShapeDtypeStruct(shape, F32) for shape in SUMS]
    rows = PIECE + GRAD_ROWS if sums else PIECE
    out = jax.ShapeDtypeStruct((2 * M, rows, 128), BF)
    scratch = [
        pltpu.VMEM((M, CELLS, C), F32),
        pltpu.VMEM((CELLS, C), F32),
        pltpu.VMEM((M, CELLS, C), F32),
        pltpu.VMEM((M, CELLS, 1), F32),
        pltpu.VMEM((M, CELLS, C), BF),
        pltpu.VMEM((M, CELLS, C), BF),
        pltpu.VMEM((M, CELLS, C), BF),
        pltpu.VMEM((M, 3 * C, CELLS), BF),
        pltpu.VMEM((M, C, CELLS), F32),
        pltpu.VMEM((M, C, CELLS), BF),
        pltpu.VMEM((M, HEADS, CELLS, CELLS), BF),
        pltpu.VMEM((M, CELLS, C), F32),
        pltpu.VMEM((M, C, CELLS), BF),
        pltpu.VMEM((M, HEADS, 1, CELLS), F32),
        pltpu.VMEM((4, HEADS, CELLS, CELLS), BF),
        pltpu.VMEM((M, 3 * C, CELLS), BF),
    ]
    if sums:
        scratch = [pltpu.VMEM(shape, F32) for shape in SUMS] + scratch
    args = (at, pieces, target_kept, target_received, bias, valid, gain[None], w_qkv[:, C:], w_qkv, w_qkv.T, w_proj, w_proj.T) + tuple(sums)
    return pl.pallas_call(
        main_kernel,
        in_specs=[SCALARS] + [WHOLE] * (len(args) - 1),
        out_specs=WHOLE if sums else [WHOLE] * 5,
        out_shape=out if sums else [out] + total,
        scratch_shapes=scratch,
        compiler_params=PARAMS,
        name="window_attention_crps",
    )(*args)


def body(inputs, target, norm_gain_vector, w_qkv, w_proj, lat_region, lat_valid):
    strips = lax.axis_size("lon")
    strip, member = lax.axis_index("lon"), lax.axis_index("mem")
    both = ("lon", "mem")

    def group(*members_of):
        return [strip * M + m for strip in members_of for m in range(M)]

    even_groups = [group(p, p + 1) for p in range(0, strips, 2)]
    odd_groups = [group(p + 1, (p + 2) % strips) for p in range(0, strips, 2)]
    alike_groups = [[(p + side) * M + m for p in range(0, strips, 2)] for side in range(2) for m in range(M)]
    even_swap = [(i, i ^ 1) for i in range(strips)]
    odd_swap = [(i, (i + 1 if i % 2 else i - 1) % strips) for i in range(strips)]

    def exchange(array, groups):
        return lax.all_to_all(array, both, 0, 0, axis_index_groups=groups)

    parity = strip % 2
    at = jnp.stack([member, parity]).astype(jnp.int32)
    side = parity.astype(jnp.int32)
    by_column = inputs.transpose(0, 1, 3, 2, 4)
    even = pack((1 - side)[None], by_column)
    odd = pack(side[None], by_column)
    even_keep, even_send, odd_keep, odd_send = pack_target(at, target.transpose(0, 2, 1, 3))
    even = exchange(even, even_groups)
    odd = exchange(odd, odd_groups)
    even_received = lax.ppermute(even_send, "lon", even_swap)
    odd_received = lax.ppermute(odd_send, "lon", odd_swap)
    even, even_received, odd_received = lax.optimization_barrier((even, even_received, odd_received))

    def of_block(side):
        first = (side * M + member) * 6
        region, valid = (
            jnp.broadcast_to(lax.dynamic_slice_in_dim(rows, first, 6).reshape(1, 6, 1), (4, 6, 6)).reshape(CELLS)
            for rows in (lat_region, lat_valid)
        )
        allowed = (region[:, None] == region[None, :]) & ((valid[:, None] == 1) | np.eye(CELLS, dtype=bool))
        return jnp.where(allowed, 0.0, -1e30).astype(F32), valid.astype(F32)[:, None]

    weights = (norm_gain_vector, w_qkv, w_proj)
    even_back, *sums = main(side[None], even, even_keep, even_received, *of_block(side), *weights)
    odd_back = main((1 - side)[None], odd, odd_keep, odd_received, *of_block(1 - side), *weights, sums=tuple(sums))
    even_back, odd_back = lax.optimization_barrier((exchange(even_back, even_groups), odd_back))
    odd_back = exchange(odd_back, odd_groups)

    count = M * 2 * 96 * 12 * strips
    rows = GRAD_ROWS + LOW_ROWS
    part = small(first_sum_kernel, "sum_group", jax.ShapeDtypeStruct((strips // 2, rows, 128), BF), odd_back)
    part = exchange(part, alike_groups)
    part = small(second_sum_kernel, "sum_all", jax.ShapeDtypeStruct((2 * M, rows, 128), BF), part)
    part = exchange(part, odd_groups)
    grad_inputs = unpack(at, even_back, odd_back, jnp.asarray(place_matrices().swapaxes(3, 4), BF)).transpose(0, 1, 3, 2, 4)
    grad_qkv, grad_proj, grad_gain, loss = small(
        functools.partial(finish_kernel, count ** (-0.5), 1.0 / (count * C)),
        "finish",
        [jax.ShapeDtypeStruct(shape, F32) for shape in ((C, 3 * C), (C, C), (1, C), (1, 1))],
        part,
    )
    return (grad_inputs, grad_qkv, grad_proj, grad_gain[0], loss[0, 0])


def solution(mesh):
    in_specs = (
        P("mem", None, None, "lon", None),
        P(None, None, "lon", None),
        P(),
        P(),
        P(),
        P(),
        P(),
    )
    out_specs = (P("mem", None, None, "lon", None), P(), P(), P(), P())
    return jax.shard_map(body, mesh=mesh, in_specs=in_specs, out_specs=out_specs, check_vma=False)
```

time: 142 us -> 122 us (0.86)
  waiting for transfers between devices: 28.2 us -> 9.61 us
  local copies, waits for them, and re-layouts: 16.7 us -> 6.14 us
  starting transfers between devices: 20 us -> 29.7 us
  blocking collectives: 22 us -> 31.1 us
  Pallas kernels: 47.3 us -> 42.9 us
  other arithmetic: 3.92 us -> 0.39 us
  between operations: 3.28 us -> 0.93 us
    ppermute x7 -> x2, waiting for transfers between devices: 16 us -> 0.01 us  [the longest x1 0.01 us: body(): odd_received = lax.ppermute(odd_send, 'lon', odd_swap)]
    all_to_all x2 -> x4, starting transfers between devices: 11.4 us -> 26.3 us  [exchange(): return lax.all_to_all(array, both, 0, 0, axis_index_groups=groups)]
    all_to_all x1 -> x2, blocking collectives: 22 us -> 31.1 us  [exchange(): return lax.all_to_all(array, both, 0, 0, axis_index_groups=groups)]
    unnamed x26 -> x32, local copies, waits for them, and re-layouts: 11.1 us -> 5.02 us
    ppermute x7 -> x2, starting transfers between devices: 8.59 us -> 3.41 us  [the longest x1 2.92 us: body(): odd_received = lax.ppermute(odd_send, 'lon', odd_swap)]
    pallas_call x3 -> x9, Pallas kernels: 47.3 us -> 42.9 us  [the longest x2 34.6 us: main(): pl.pallas_call(main_kernel, in_specs=[SCALARS] + [WHOLE] * (len(args) - 1...]
    all_to_all x2 -> x4, waiting for transfers between devices: 12.2 us -> 9.6 us  [exchange(): return lax.all_to_all(array, both, 0, 0, axis_index_groups=groups)]
    mul x3 -> x0, other arithmetic: 2.09 us -> none  [the longest x1 0.82 us: body(): qkv_sum * scale]
  transfers between devices with their start and end apart: 9 -> 6, of which waited for: 7 -> 2; matrix products, arithmetic and copies ran while one was open for 8% -> 1% of each run, Pallas kernels for 4% -> 33%
where the time goes in v3:
time: 122 us; the launch traced here: 121 us
  Pallas kernels  42.9 us (35%)
  blocking collectives  31.1 us (25%)
  starting transfers between devices  29.7 us (24%)
  waiting for transfers between devices  9.61 us (8%)
  local copies, waits for them, and re-layouts  6.14 us (5%)
    pallas_call x2, Pallas kernels, main(): pl.pallas_call(main_kernel, in_specs=[SCALARS] + [WHOLE] * (len(args) - 1...  34.6 us
    all_to_all x2, blocking collectives, exchange(): return lax.all_to_all(array, both, 0, 0, axis_index_groups=groups)  31.1 us
    all_to_all x4, starting transfers between devices, exchange(): return lax.all_to_all(array, both, 0, 0, axis_index_groups=groups)  26.3 us
    all_to_all x4, waiting for transfers between devices, exchange(): return lax.all_to_all(array, both, 0, 0, axis_index_groups=groups)  9.6 us
    unnamed x32, local copies, waits for them, and re-layouts  5.02 us
    pallas_call x2, Pallas kernels, pack(): pl.pallas_call(pack_kernel, in_specs=[SCALARS, pl.BlockSpec(memory_space=...  3.14 us
    pallas_call x1, Pallas kernels, unpack(): pl.pallas_call(unpack_kernel, in_specs=[SCALARS, WHOLE, WHOLE, WHOLE], ou...  3.02 us
    ppermute x1, starting transfers between devices, body(): odd_received = lax.ppermute(odd_send, 'lon', odd_swap)  2.92 us
  transfers between devices with their start and end apart: 6, of which 2 were waited for; matrix products, arithmetic and copies ran while one was open for 1% of the time, Pallas kernels for 33%

profile of v3, /device:TPU:0, one launch (start us, length us, event | category | flops | bytes accessed | tf_op | source)
XLA Modules:
  0.0 120.8 jit_solution(1793883742951466860)
XLA Ops:
  0.6 0.0 copy-start
  0.7 1.3 %copy-done = bf16[1,2,96,12,192]{4,2,3,1,0:T(8,128)(2,1)S(1)} copy-done((bf16[1,2,96,12,192]{4,2,3,1,0:T(8,128)(2,1)S(1)}, bf16[1,2,96,12,192]{4,2,3,1,0:T(8,128)(2,1)}, u32[]{:S(2)}) %copy-start) | copy-done | bytes 884760
  1.9 1.6 %pack_strip.2 = bf16[16,112,128]{2,1,0:T(8,128)(2,1)} custom-call(s32[1]{0:T(128)} %bitcast.2.at_ref, bf16[1,2,12,96,192]{4,3,2,1,0:T(8,128)(2,1)S(1)} %bitcast.11), custom_call_target="tpu_custom_call" | custom-call | tf_op jit(solution)/shard_map/pack_strip/pallas_call | solution.py:115
  3.5 0.0 copy-start.1
  3.5 8.1 %all-to-all-start = ((bf16[16,112,128]{2,1,0:T(8,128)(2,1)}), bf16[16,112,128]{2,1,0:T(8,128)(2,1)S(1)}, u32[]{:S(2)}, u32[]{:S(2)}) async-start(bf16[16,112,128]{2,1,0:T(8,128)(2,1)} %pack_strip.2), calls=%async_computation | async-start | bytes 917504 | tf_op jit(solution)/shard_map/all_to_all | solution.py:495
  11.6 0.1 pad_add_fusion.at_ref
  11.7 1.1 pack_target.1
  12.8 0.5 collective-permute-start
  13.3 2.9 %collective-permute-start.1 = (bf16[112,128]{1,0:T(8,128)(2,1)S(1)}, bf16[112,128]{1,0:T(8,128)(2,1)S(1)}, u32[]{:S(2)}, u32[]{:S(2)}) collective-permute-start(bf16[112,128]{1,0:T(8,128)(2,1)S(1)} %get-tuple-element.24), channel_id=1, source_target_pairs={{0,120},{8,16},{16,8},{24,32},{32,24},{40,48},{48,40},{56,64},{64,... | collective-permute-start | bytes 86024 | tf_op jit(solution)/shard_map/ppermute | solution.py:507
  16.2 0.0 copy-start.2
  16.2 1.6 %pack_strip.3 = bf16[16,112,128]{2,1,0:T(8,128)(2,1)} custom-call(s32[1]{0:T(128)} %bitcast.1.at_ref, bf16[1,2,12,96,192]{4,3,2,1,0:T(8,128)(2,1)S(1)} %bitcast.12), custom_call_target="tpu_custom_call" | custom-call | tf_op jit(solution)/shard_map/pack_strip/pallas_call | solution.py:115
  17.8 0.0 copy-start.8
  17.8 0.0 copy-start.11
  17.8 5.3 %all-to-all-done.x_ref = bf16[16,112,128]{2,1,0:T(8,128)(2,1)S(1)} async-done(((bf16[16,112,128]{2,1,0:T(8,128)(2,1)}), bf16[16,112,128]{2,1,0:T(8,128)(2,1)S(1)}, u32[]{:S(2)}, u32[]{:S(2)}) %all-to-all-start) | async-done | bytes 458784 | tf_op jit(solution)/shard_map/all_to_all | solution.py:495
  23.1 6.5 %all-to-all-start.2 = ((bf16[16,112,128]{2,1,0:T(8,128)(2,1)}), bf16[16,112,128]{2,1,0:T(8,128)(2,1)S(1)}, u32[]{:S(2)}, u32[]{:S(2)}) async-start(bf16[16,112,128]{2,1,0:T(8,128)(2,1)} %pack_strip.3), calls=%async_computation.2 | async-start | bytes 917504 | tf_op jit(solution)/shard_map/all_to_all | solution.py:495
  29.7 0.1 dynamic-slice_convert_fusion
  29.8 0.1 broadcast_in_dim.53
  29.8 0.1 eq.62
  29.9 0.1 broadcast_compare_fusion
  30.0 0.1 broadcast_in_dim.54
  30.1 0.1 eq.67
  30.2 0.1 broadcast_in_dim.48
  30.3 0.1 eq.61
  30.4 0.1 broadcast_in_dim.47
  30.5 0.1 eq.56
  30.6 0.1 and_select_fusion
  30.7 0.1 slice.4.wkv_ref
  30.8 0.2 copy.17
  31.0 0.1 broadcast_in_dim.51
  31.1 0.1 convert_element_type.32.valid_ref
  31.2 0.1 copy.18
  31.3 17.6 %window_attention_crps.2 = (bf16[16,112,128]{2,1,0:T(8,128)(2,1)}, f32[576,192]{1,0:T(8,128)S(1)}, f32[192,192]{1,0:T(8,128)S(1)}, f32[8,192]{1,0:T(8,128)S(1)}, f32[8,192]{1,0:T(8,128)S(1)}) custom-call(s32[1]{0:T(128)} %bitcast.1.at_ref, bf16[16,112,128]{2,1,0:T(8,128)(2,1)S(1)} %all-to-all-done.x_ref, bf16[112,128]{1,0:T(8,128)(2,1)S(1)} %get-tuple-element.26.tk_ref, ...), custom_call_target="tpu_custom_call" | custom-call | tf_op jit(solution)/shard_map/window_attention_crps/pallas_call | solution.py:469
  48.9 5.9 %all-to-all-start.1 = ((bf16[16,112,128]{2,1,0:T(8,128)(2,1)}), bf16[16,112,128]{2,1,0:T(8,128)(2,1)S(1)}, u32[]{:S(2)}, u32[]{:S(2)}) async-start(bf16[16,112,128]{2,1,0:T(8,128)(2,1)} %get-tuple-element.28), calls=%async_computation.1 | async-start | bytes 917504 | tf_op jit(solution)/shard_map/all_to_all | solution.py:495
  54.8 0.1 broadcast_in_dim.55
  54.9 0.1 convert_element_type.33.valid_ref
  55.0 0.9 copy-done.10
  55.9 17.0 %window_attention_crps.3 = bf16[16,192,128]{2,1,0:T(8,128)(2,1)S(1)} custom-call(s32[1]{0:T(128)} %bitcast.2.at_ref, bf16[16,112,128]{2,1,0:T(8,128)(2,1)S(1)} %all-to-all-done.2.x_ref, bf16[112,128]{1,0:T(8,128)(2,1)S(1)} %get-tuple-element.29.tk_ref, bf16[112,128]{1,0:T(8,128)(2,1)S(1)} %collective-permute-done.1.tr_ref, ...), custom_call_target="tpu_custom_call" | custom-call | tf_op jit(solution)/shard_map/window_attention_crps/pallas_call | solution.py:469
  73.0 0.8 copy-done.4
  73.7 20.2 %all_to_all.30.odd_ref.back_ref = bf16[16,192,128]{2,1,0:T(8,128)(2,1)S(1)} all-to-all(bf16[16,192,128]{2,1,0:T(8,128)(2,1)S(1)} %window_attention_crps.3), channel_id=1, replica_groups={{8,9,10,11,12,13,14,15,16,17,18,19,20,21,22,23},{24,25,26,27,28,29,30,3..., dimensions={0} | all-to-all | bytes 1572864 | tf_op jit(solution)/shard_map/all_to_all | solution.py:495
  93.9 0.1 sum_group.1
  94.0 10.9 %all_to_all.31.parts_ref = bf16[8,96,128]{2,1,0:T(8,128)(2,1)S(1)} all-to-all(bf16[8,96,128]{2,1,0:T(8,128)(2,1)S(1)} %sum_group.1), channel_id=1, replica_groups={{0,16,32,48,64,80,96,112},{1,17,33,49,65,81,97,113},{2,18,34,50,66,82,9..., dimensions={0} | all-to-all | bytes 393216 | tf_op jit(solution)/shard_map/all_to_all | solution.py:495
  104.9 0.8 copy-done.6
  105.6 5.8 %all-to-all-start.5 = ((bf16[16,96,128]{2,1,0:T(8,128)(2,1)}), bf16[16,96,128]{2,1,0:T(8,128)(2,1)S(1)}, u32[]{:S(2)}, u32[]{:S(2)}) async-start(bf16[16,96,128]{2,1,0:T(8,128)(2,1)} %copy-done.6), calls=%async_computation.5 | async-start | bytes 786432 | tf_op jit(solution)/shard_map/all_to_all | solution.py:495
  111.5 0.0 copy-start.5
  111.5 1.0 copy-done.5
  112.5 3.0 %unpack_strip.1 = bf16[1,2,12,96,192]{4,3,2,1,0:T(8,128)(2,1)} custom-call(s32[2]{0:T(128)S(1)} %pad_add_fusion.at_ref, bf16[16,112,128]{2,1,0:T(8,128)(2,1)S(1)} %copy-done.5, bf16[16,192,128]{2,1,0:T(8,128)(2,1)S(1)} %all_to_all.30.odd_ref.back_ref, bf16[4,2,2,192,288]{4,3,2,1,0:T(8,128)(2,1)S(1)} %copy-done.3), custom_call_target="tpu_custom_call" | custom-call | tf_op jit(solution)/shard_map/unpack_strip/pallas_call | solution.py:192
  115.5 4.3 %all-to-all-done.5.grads_ref = bf16[16,96,128]{2,1,0:T(8,128)(2,1)S(1)} async-done(((bf16[16,96,128]{2,1,0:T(8,128)(2,1)}), bf16[16,96,128]{2,1,0:T(8,128)(2,1)S(1)}, u32[]{:S(2)}, u32[]{:S(2)}) %all-to-all-start.5) | async-done | bytes 393248 | tf_op jit(solution)/shard_map/all_to_all | solution.py:495
  119.8 0.9 finish.1
  (24 shorter events, 0.1 us)
Async XLA Ops:
  0.6 1.3 %copy-start = (bf16[1,2,96,12,192]{4,2,3,1,0:T(8,128)(2,1)S(1)}, bf16[1,2,96,12,192]{4,2,3,1,0:T(8,128)(2,1)}, u32[]{:S(2)}) copy-start(bf16[1,2,96,12,192]{4,2,3,1,0:T(8,128)(2,1)} %param.10) | copy-start | bytes 2654212
  1.9 9.8 %copy-start.7 = (bf16[2,96,12,192]{3,1,2,0:T(8,128)(2,1)S(1)}, bf16[2,96,12,192]{3,1,2,0:T(8,128)(2,1)}, u32[]{:S(2)}) copy-start(bf16[2,96,12,192]{3,1,2,0:T(8,128)(2,1)} %param.11) | copy-start | bytes 2654212
  3.5 12.7 %copy-start.1 = (bf16[1,2,96,12,192]{4,2,3,1,0:T(8,128)(2,1)S(1)}, bf16[1,2,96,12,192]{4,2,3,1,0:T(8,128)(2,1)}, u32[]{:S(2)}) copy-start(bf16[1,2,96,12,192]{4,2,3,1,0:T(8,128)(2,1)} %param.10) | copy-start | bytes 2654212
  3.5 19.6 %all-to-all-start = ((bf16[16,112,128]{2,1,0:T(8,128)(2,1)}), bf16[16,112,128]{2,1,0:T(8,128)(2,1)S(1)}, u32[]{:S(2)}, u32[]{:S(2)}) async-start(bf16[16,112,128]{2,1,0:T(8,128)(2,1)} %pack_strip.2), calls=%async_computation | async-start | bytes 917504 | tf_op jit(solution)/shard_map/all_to_all | solution.py:495
  12.8 18.5 %collective-permute-start = (bf16[112,128]{1,0:T(8,128)(2,1)S(1)}, bf16[112,128]{1,0:T(8,128)(2,1)S(1)}, u32[]{:S(2)}, u32[]{:S(2)}) collective-permute-start(bf16[112,128]{1,0:T(8,128)(2,1)S(1)} %get-tuple-element.23), channel_id=1, source_target_pairs={{0,8},{8,0},{16,24},{24,16},{32,40},{40,32},{48,56},{56,48},{64,72... | collective-permute-start | bytes 86024 | tf_op jit(solution)/shard_map/ppermute | solution.py:506
  13.3 18.0 %collective-permute-start.1 = (bf16[112,128]{1,0:T(8,128)(2,1)S(1)}, bf16[112,128]{1,0:T(8,128)(2,1)S(1)}, u32[]{:S(2)}, u32[]{:S(2)}) collective-permute-start(bf16[112,128]{1,0:T(8,128)(2,1)S(1)} %get-tuple-element.24), channel_id=1, source_target_pairs={{0,120},{8,16},{16,8},{24,32},{32,24},{40,48},{48,40},{56,64},{64,... | collective-permute-start | bytes 86024 | tf_op jit(solution)/shard_map/ppermute | solution.py:507
  16.2 13.5 %copy-start.13 = (s32[96]{0:T(128)S(1)}, s32[96]{0:T(128)}, u32[]{:S(2)}) copy-start(s32[96]{0:T(128)} %param.16) | copy-start | bytes 1156
  16.2 13.5 %copy-start.14 = (s32[96]{0:T(128)S(1)}, s32[96]{0:T(128)}, u32[]{:S(2)}) copy-start(s32[96]{0:T(128)} %param.15) | copy-start | bytes 1156
  16.2 14.3 %copy-start.12 = (pred[144,144]{1,0:T(8,128)(4,1)S(1)}, pred[144,144]{1,0:T(8,128)(4,1)}, u32[]{:S(2)}) copy-start(pred[144,144]{1,0:T(8,128)(4,1)} %constant.39.clone) | copy-start | bytes 62212
  16.2 14.5 %copy-start.2 = (bf16[192,576]{1,0:T(8,128)(2,1)S(1)}, bf16[192,576]{1,0:T(8,128)(2,1)}, u32[]{:S(2)}) copy-start(bf16[192,576]{1,0:T(8,128)(2,1)} %wqkv_ref.3) | copy-start | bytes 663556
  17.8 13.4 %copy-start.8 = (bf16[192,192]{1,0:T(8,128)(2,1)S(1)}, bf16[192,192]{1,0:T(8,128)(2,1)}, u32[]{:S(2)}) copy-start(bf16[192,192]{1,0:T(8,128)(2,1)} %wproj_ref.3) | copy-start | bytes 221188
  17.8 13.5 %copy-start.11 = (f32[192]{0:T(256)S(1)}, f32[192]{0:T(256)}, u32[]{:S(2)}) copy-start(f32[192]{0:T(256)} %param.12) | copy-start | bytes 2308
  23.1 25.8 %all-to-all-start.2 = ((bf16[16,112,128]{2,1,0:T(8,128)(2,1)}), bf16[16,112,128]{2,1,0:T(8,128)(2,1)S(1)}, u32[]{:S(2)}, u32[]{:S(2)}) async-start(bf16[16,112,128]{2,1,0:T(8,128)(2,1)} %pack_strip.3), calls=%async_computation.2 | async-start | bytes 917504 | tf_op jit(solution)/shard_map/all_to_all | solution.py:495
  48.9 6.1 %copy-start.9 = (f32[192,192]{1,0:T(8,128)}, f32[192,192]{1,0:T(8,128)S(1)}, u32[]{:S(2)}) copy-start(f32[192,192]{1,0:T(8,128)S(1)} %get-tuple-element.32.refs_1_) | copy-start | bytes 442372
  48.9 24.0 %all-to-all-start.1 = ((bf16[16,112,128]{2,1,0:T(8,128)(2,1)}), bf16[16,112,128]{2,1,0:T(8,128)(2,1)S(1)}, u32[]{:S(2)}, u32[]{:S(2)}) async-start(bf16[16,112,128]{2,1,0:T(8,128)(2,1)} %get-tuple-element.28), calls=%async_computation.1 | async-start | bytes 917504 | tf_op jit(solution)/shard_map/all_to_all | solution.py:495
  55.0 0.9 copy-start.10
  73.0 0.8 copy-start.4
  93.9 17.6 %copy-start.3 = (bf16[4,2,2,192,288]{4,3,2,1,0:T(8,128)(2,1)S(1)}, bf16[4,2,2,192,288]{4,3,2,1,0:T(8,128)(2,1)}, u32[]{:S(2)}) copy-start(bf16[4,2,2,192,288]{4,3,2,1,0:T(8,128)(2,1)} %constant.40.clone.place_ref) | copy-start | bytes 5308420
  104.9 0.8 copy-start.6
  105.6 14.2 %all-to-all-start.5 = ((bf16[16,96,128]{2,1,0:T(8,128)(2,1)}), bf16[16,96,128]{2,1,0:T(8,128)(2,1)S(1)}, u32[]{:S(2)}, u32[]{:S(2)}) async-start(bf16[16,96,128]{2,1,0:T(8,128)(2,1)} %copy-done.6), calls=%async_computation.5 | async-start | bytes 786432 | tf_op jit(solution)/shard_map/all_to_all | solution.py:495
  111.5 1.0 copy-start.5

commit v4 on v3

--- a/solution.py
+++ b/solution.py
@@ -55,18 +55,8 @@
 FIRST = (0, 0, 1, 1)
 
 
-def place_matrices():
-    cell = np.arange(288)
-    half, block, level, row, column = cell // 144, cell // 72 % 2, cell // 36 % 2, cell // 6 % 6, cell % 6
-    out = np.zeros((4, 2, 2, 288, 192), np.float32)
-    for i, first in enumerate(FIRST):
-        lat = 12 * i + 6 * block + row
-        out[i, lat // 16 - first, level, cell, (half * 6 + column) * 16 + lat % 16] = 1.0
-    return out
-
-
-def cell_parts():
-    cell = lax.broadcasted_iota(jnp.int32, (CELLS, 1), 0)
+def cell_parts(axis):
+    cell = lax.broadcasted_iota(jnp.int32, (CELLS, 1) if axis == 0 else (1, CELLS), axis)
     block = (cell >= 72).astype(jnp.int32)
     cell = cell - 72 * block
     level = (cell >= 36).astype(jnp.int32)
@@ -94,7 +84,7 @@
 def pack_kernel(at_ref, x_hbm, out_ref, x_ref, semaphore):
     copy = pltpu.make_async_copy(x_hbm.at[0, :, pl.ds(at_ref[0] * 6, 6)], x_ref, semaphore)
     copy.start()
-    parts = cell_parts()
+    parts = cell_parts(0)
     copy.wait()
     for quad in range(2):
         for i in range(4):
@@ -114,7 +104,7 @@
 def pack(half, inputs):
     return pl.pallas_call(
         pack_kernel,
-        in_specs=[SCALARS, pl.BlockSpec(memory_space=pl.ANY)],
+        in_specs=[SCALARS, HBM],
         out_specs=WHOLE,
         out_shape=jax.ShapeDtypeStruct((2 * M, PIECE, 128), BF),
         scratch_shapes=[pltpu.VMEM((2, 6, 96, C), BF), pltpu.SemaphoreType.DMA],
@@ -128,7 +118,7 @@
     i = member // 2
     first = jnp.where(i >= 2, 1, 0)
     second = member % 2 == 1
-    parts = cell_parts()
+    parts = cell_parts(0)
     pieces = []
     for quad in range(2):
         for half in range(2):
@@ -162,41 +152,54 @@
 
 WHOLE = pl.BlockSpec(memory_space=pltpu.VMEM)
 SCALARS = pl.BlockSpec(memory_space=pltpu.SMEM)
+HBM = pl.BlockSpec(memory_space=pltpu.HBM)
 PARAMS = pltpu.CompilerParams(vmem_limit_bytes=VMEM_LIMIT)
 
 
-def unpack_kernel(at_ref, even_ref, odd_ref, place_ref, out_ref):
-    odd_strip = at_ref[1] == 1
+def unpack_half_strip(half, back_ref, out_hbm, cells_s, slabs_s, semaphore):
+    parts = cell_parts(1)
+    slot = lax.broadcasted_iota(jnp.int32, (96, CELLS), 0)
+    for block in range(2 * M):
+        cells_s[block // 2, block % 2 * HALF : (block % 2 + 1) * HALF] = unpack_half(back_ref[block, :PIECE].astype(F32))
     for quad in range(2):
-        groups = []
-        for i in range(4):
-            wests, easts = [], []
-            for sub in range(2):
-                even = even_ref[8 * quad + 2 * i + sub].astype(F32)
-                odd = odd_ref[8 * quad + 2 * i + sub, :PIECE].astype(F32)
-                wests.append(unpack_half(jnp.where(odd_strip, even, odd)))
-                easts.append(unpack_half(jnp.where(odd_strip, odd, even)))
-            groups.append(jnp.concatenate(wests + easts, axis=0).astype(BF))
+        groups = [cells_s[4 * quad + i].astype(BF) for i in range(4)]
         for t in range(3):
             at = 16 * (3 * quad + t)
             for level in range(2):
                 slab = None
                 for i in range(4):
                     if t - FIRST[i] in TILES[i]:
-                        part = dot(place_ref[i, t - FIRST[i], level], groups[i])
+                        place = (place_of(parts, i, t, level, 0) == slot).astype(F32).astype(BF)
+                        part = dot(place, groups[i])
                         slab = part if slab is None else slab + part
-                out_ref[0, level, :, at : at + 16, :] = slab.astype(BF).reshape(12, 16, C)
-
-
-def unpack(at, even, odd, place_t):
+                slabs_s[level, :, at : at + 16, :] = slab.astype(BF).reshape(6, 16, C)
+    copy = pltpu.make_async_copy(slabs_s, out_hbm.at[0, :, pl.ds(half * 6, 6)], semaphore)
+    copy.start()
+    return copy
+
+
+UNPACK_SCRATCH = [
+    pltpu.VMEM((M, CELLS, C), F32),
+    pltpu.VMEM((2, 6, 96, C), BF),
+    pltpu.SemaphoreType.DMA,
+]
+STRIP = jax.ShapeDtypeStruct((1, 2, 12, 96, C), BF)
+
+
+def unpack_kernel(half_ref, back_ref, out_hbm, *scratch):
+    unpack_half_strip(half_ref[0], back_ref, out_hbm, *scratch).wait()
+
+
+def unpack(half, back):
     return pl.pallas_call(
         unpack_kernel,
-        in_specs=[SCALARS, WHOLE, WHOLE, WHOLE],
-        out_specs=WHOLE,
-        out_shape=jax.ShapeDtypeStruct((1, 2, 12, 96, C), BF),
+        in_specs=[SCALARS, WHOLE],
+        out_specs=HBM,
+        out_shape=STRIP,
+        scratch_shapes=UNPACK_SCRATCH,
         compiler_params=PARAMS,
         name="unpack_strip",
-    )(at, even, odd, place_t)
+    )(half, back)
 
 
 def split_low(total, copies):
@@ -210,16 +213,22 @@
     out_ref[...] = split_low(total, out_ref.shape[0])
 
 
-def second_sum_kernel(parts_ref, out_ref):
+def second_sum_kernel(parts_ref, back_ref, out_ref):
     total = jnp.sum(parts_ref[...].astype(F32), axis=0)
     low = jnp.concatenate(
         [jnp.zeros((32, 128), F32), total[GRAD_ROWS:], jnp.zeros((GRAD_ROWS - 32 - LOW_ROWS, 128), F32)], axis=0
     )
-    out_ref[...] = split_low(total[:GRAD_ROWS] + low, out_ref.shape[0])
-
-
-def finish_kernel(scale, per_score, grads_ref, qkv_out, proj_out, gain_out, loss_out):
-    rows = grads_ref[:, :GRAD_ROWS].astype(F32).reshape(2 * M * GRAD_ROWS, 128) * scale
+    out_ref[:, :PIECE] = back_ref[...]
+    out_ref[:, PIECE:] = split_low(total[:GRAD_ROWS] + low, out_ref.shape[0])
+
+
+def finish_kernel(
+    scale, per_score, half_ref, back_ref, half_done, out_hbm, qkv_out, proj_out, gain_out, loss_out, *scratch
+):
+    del half_done
+    copy = unpack_half_strip(half_ref[0], back_ref, out_hbm, *scratch)
+    pieces = [back_ref[(i + M) % (2 * M), PIECE : PIECE + GRAD_ROWS] for i in range(2 * M)]
+    rows = jnp.concatenate(pieces, axis=0).astype(F32) * scale
     for i in range(4):
         qkv_out[:, 128 * i : 128 * (i + 1)] = rows[i * C : (i + 1) * C]
     rest = rows[768:864]
@@ -227,10 +236,25 @@
     rest = rows[1056:1152]
     proj_out[:, :128] = rows[864:1056]
     proj_out[:, 128:] = jnp.concatenate([rest[:, :64], pltpu.roll(rest, 64, 1)[:, :64]], axis=0)
-    piece = 1152 // GRAD_ROWS
-    extra = grads_ref[piece, 32 : 32 + LOW_ROWS].astype(F32) + grads_ref[piece, GRAD_ROWS:].astype(F32)
+    piece = (1152 // GRAD_ROWS + M) % (2 * M)
+    at = PIECE + 32
+    extra = back_ref[piece, at : at + LOW_ROWS].astype(F32) + back_ref[piece, PIECE + GRAD_ROWS :].astype(F32)
     gain_out[...] = jnp.concatenate([extra[0:1], extra[1:2, :64]], axis=1) * scale
     loss_out[...] = (extra[2:3, 0:1] + extra[2:3, 1:2]) * per_score
+    copy.wait()
+
+
+def finish(half, back, half_done, count):
+    return pl.pallas_call(
+        functools.partial(finish_kernel, count ** (-0.5), 1.0 / (count * C)),
+        in_specs=[SCALARS, WHOLE, HBM],
+        out_specs=[HBM] + [WHOLE] * 4,
+        out_shape=[STRIP] + [jax.ShapeDtypeStruct(shape, F32) for shape in ((C, 3 * C), (C, C), (1, C), (1, 1))],
+        scratch_shapes=UNPACK_SCRATCH,
+        input_output_aliases={2: 0},
+        compiler_params=PARAMS,
+        name="finish",
+    )(half, back, half_done)
 
 
 def small(kernel, name, out_shape, *args):
@@ -250,14 +274,16 @@
 
 
 def main_kernel(
-    at_ref, x_ref, tk_ref, tr_ref, bias_ref, valid_ref, gain_ref, wkv_ref, wqkv_ref, wqkvt_ref, wproj_ref, wprojt_ref,
-    *refs,
+    at_ref, x_ref, t_ref, aux_ref, bias_ref, wkv_ref, wqkv_ref, wqkvt_ref, wproj_ref, wprojt_ref, *refs
 ):
     refs = list(refs)
-    start = [refs.pop(0) for _ in range(4)] if len(refs) > 21 else None
-    out_ref = refs.pop(0)
-    (x_s, t_s, xhat_s, rstd_s, n_s, k_s, v_s, qkvt_s, attf_s, att_s, p_s, mixed_s, gat_s, tot_s, ds_s, grad_s) = refs[-16:]
-    sqkv_s, sproj_s, sgain_s, score_s = refs[:-16]
+    before_ref = refs.pop(0) if len(refs) > 18 else None
+    out_ref, sums_s = refs[:2]
+    (x_s, t_s, xhat_s, rstd_s, n_s, k_s, v_s, qkvt_s, attf_s, att_s, p_s, mixed_s, gat_s, tot_s, ds_s, grad_s) = refs[2:]
+    sqkv_s, sproj_s, sgain_s, score_s = (
+        sums_s.at[start : start + rows] for start, rows in ((0, 3 * C), (3 * C, C), (4 * C, 8), (4 * C + 8, 8))
+    )
+    gain_ref, valid_ref = aux_ref.at[CELLS : CELLS + 1], aux_ref.at[:CELLS]
     scale = SIZE ** (-0.5)
     to_exp2 = scale * 1.4426950408889634
     last = M - 1
@@ -266,8 +292,8 @@
         x_s[member] = jnp.concatenate(
             [unpack_half(x_ref[member].astype(F32)), unpack_half(x_ref[M + member].astype(F32))], axis=0
         )
-    kept = unpack_half(tk_ref[...].astype(F32))
-    received = unpack_half(tr_ref[...].astype(F32))
+    kept = unpack_half(t_ref[0].astype(F32))
+    received = unpack_half(t_ref[1].astype(F32))
     eastern = at_ref[0] == 1
     t_s[...] = jnp.concatenate(
         [jnp.where(eastern, received, kept), jnp.where(eastern, kept, received)], axis=0
@@ -308,7 +334,7 @@
         projt = dot(wprojt_ref[...], att_s[step]).astype(BF)
         heads((attend_head, jnp.minimum(step + 1, last)), (score_head, jnp.minimum(step + 2, last)))
         project_qkv(jnp.minimum(step + 3, last))
-        mixed_s[step] = x_s[step] + dot_t(identity(CELLS), projt)
+        mixed_s[step] = x_s[step] + projt.T.astype(F32)
         return carry
 
     project_qkv(0)
@@ -345,14 +371,7 @@
             mixed_s[m, rows] = valid * (diff * inverse - slopes[m] / M)
         return score + valid * total
 
-    if start is None:
-        sqkv_s[...] = jnp.zeros_like(sqkv_s)
-        sproj_s[...] = jnp.zeros_like(sproj_s)
-        sgain_s[...] = jnp.zeros_like(sgain_s)
-        score_s[...] = jnp.zeros_like(score_s)
-    else:
-        for ref, begin in zip((sqkv_s, sproj_s, sgain_s, score_s), start):
-            ref[...] = begin[...]
+    sums_s[...] = jnp.zeros_like(sums_s) if before_ref is None else before_ref[...]
     score_s[...] = lax.fori_loop(0, 18, crps, score_s[...])
 
     def grad_attended(window):
@@ -378,7 +397,7 @@
         ).astype(BF)
 
     def grad_norm(window, gbt):
-        grad_normed = dot_t(identity(CELLS), gbt)
+        grad_normed = gbt.T.astype(F32)
         xhat = xhat_s[window]
         sgain_s[...] += jnp.sum((grad_normed * xhat).reshape(18, 8, C), axis=0)
         scaled = grad_normed * gain_ref[...]
@@ -400,12 +419,12 @@
     grad_attended(1)
     heads((grad_qkv_head, 0), (grad_score_head, 1))
     grad_attended(2)
-    lax.fori_loop(0, M, backward, 0)
+    lax.fori_loop(0, M, backward, 0, unroll=2)
 
     def pieces(member):
         return [pack_half(x_s[member, half * HALF : (half + 1) * HALF]).astype(BF) for half in range(2)]
 
-    if start is None:
+    if before_ref is None:
         for member in range(M):
             for half, piece in enumerate(pieces(member)):
                 out_ref[half * M + member] = piece
@@ -438,13 +457,12 @@
             out_ref[to] = jnp.concatenate([piece, grads[to * GRAD_ROWS : (to + 1) * GRAD_ROWS]], axis=0)
 
 
-SUMS = [(3 * C, C), (C, C), (8, C), (8, C)]
-
-
-def main(at, pieces, target_kept, target_received, bias, valid, gain, w_qkv, w_proj, sums=()):
-    total = [jax.ShapeDtypeStruct(shape, F32) for shape in SUMS]
-    rows = PIECE + GRAD_ROWS if sums else PIECE
-    out = jax.ShapeDtypeStruct((2 * M, rows, 128), BF)
+SUMS = (4 * C + 16, C)
+
+
+def main(at, pieces, target, aux, bias, weights, before=None):
+    sums = jax.ShapeDtypeStruct(SUMS, F32)
+    out = jax.ShapeDtypeStruct((2 * M, PIECE if before is None else PIECE + GRAD_ROWS, 128), BF)
     scratch = [
         pltpu.VMEM((M, CELLS, C), F32),
         pltpu.VMEM((CELLS, C), F32),
@@ -463,14 +481,15 @@
         pltpu.VMEM((4, HEADS, CELLS, CELLS), BF),
         pltpu.VMEM((M, 3 * C, CELLS), BF),
     ]
-    if sums:
-        scratch = [pltpu.VMEM(shape, F32) for shape in SUMS] + scratch
-    args = (at, pieces, target_kept, target_received, bias, valid, gain[None], w_qkv[:, C:], w_qkv, w_qkv.T, w_proj, w_proj.T) + tuple(sums)
+    args = (at, pieces, target, aux, bias) + tuple(weights)
+    if before is not None:
+        scratch = [pltpu.VMEM(SUMS, F32)] + scratch
+        args += (before,)
     return pl.pallas_call(
         main_kernel,
         in_specs=[SCALARS] + [WHOLE] * (len(args) - 1),
-        out_specs=WHOLE if sums else [WHOLE] * 5,
-        out_shape=out if sums else [out] + total,
+        out_specs=[WHOLE] * 2 if before is None else WHOLE,
+        out_shape=[out, sums] if before is None else out,
         scratch_shapes=scratch,
         compiler_params=PARAMS,
         name="window_attention_crps",
@@ -499,13 +518,12 @@
     side = parity.astype(jnp.int32)
     by_column = inputs.transpose(0, 1, 3, 2, 4)
     even = pack((1 - side)[None], by_column)
+    even, target, by_column = lax.optimization_barrier((even, target, by_column))
     odd = pack(side[None], by_column)
     even_keep, even_send, odd_keep, odd_send = pack_target(at, target.transpose(0, 2, 1, 3))
     even = exchange(even, even_groups)
-    odd = exchange(odd, odd_groups)
-    even_received = lax.ppermute(even_send, "lon", even_swap)
-    odd_received = lax.ppermute(odd_send, "lon", odd_swap)
-    even, even_received, odd_received = lax.optimization_barrier((even, even_received, odd_received))
+    even_target = jnp.stack([even_keep, lax.ppermute(even_send, "lon", even_swap)])
+    odd_target = jnp.stack([odd_keep, lax.ppermute(odd_send, "lon", odd_swap)])
 
     def of_block(side):
         first = (side * M + member) * 6
@@ -514,27 +532,28 @@
             for rows in (lat_region, lat_valid)
         )
         allowed = (region[:, None] == region[None, :]) & ((valid[:, None] == 1) | np.eye(CELLS, dtype=bool))
-        return jnp.where(allowed, 0.0, -1e30).astype(F32), valid.astype(F32)[:, None]
-
-    weights = (norm_gain_vector, w_qkv, w_proj)
-    even_back, *sums = main(side[None], even, even_keep, even_received, *of_block(side), *weights)
-    odd_back = main((1 - side)[None], odd, odd_keep, odd_received, *of_block(1 - side), *weights, sums=tuple(sums))
-    even_back, odd_back = lax.optimization_barrier((exchange(even_back, even_groups), odd_back))
+        aux = jnp.concatenate(
+            [jnp.broadcast_to(valid.astype(F32)[:, None], (CELLS, C)), jnp.broadcast_to(norm_gain_vector[None], (8, C))]
+        )
+        return aux, jnp.where(allowed, 0.0, -1e30).astype(F32)
+
+    even_extra, odd_extra = (even_target, *of_block(side)), (odd_target, *of_block(1 - side))
+    weights = (w_qkv[:, C:], w_qkv, w_qkv.T, w_proj, w_proj.T)
+    odd, even_extra, odd_extra, weights = lax.optimization_barrier((odd, even_extra, odd_extra, weights))
+    odd = exchange(odd, odd_groups)
+    even_back, sums = main(side[None], even, *even_extra, weights)
+    odd_back = main((1 - side)[None], odd, *odd_extra, weights, sums)
     odd_back = exchange(odd_back, odd_groups)
 
     count = M * 2 * 96 * 12 * strips
     rows = GRAD_ROWS + LOW_ROWS
     part = small(first_sum_kernel, "sum_group", jax.ShapeDtypeStruct((strips // 2, rows, 128), BF), odd_back)
     part = exchange(part, alike_groups)
-    part = small(second_sum_kernel, "sum_all", jax.ShapeDtypeStruct((2 * M, rows, 128), BF), part)
-    part = exchange(part, odd_groups)
-    grad_inputs = unpack(at, even_back, odd_back, jnp.asarray(place_matrices().swapaxes(3, 4), BF)).transpose(0, 1, 3, 2, 4)
-    grad_qkv, grad_proj, grad_gain, loss = small(
-        functools.partial(finish_kernel, count ** (-0.5), 1.0 / (count * C)),
-        "finish",
-        [jax.ShapeDtypeStruct(shape, F32) for shape in ((C, 3 * C), (C, C), (1, C), (1, 1))],
-        part,
-    )
+    last = jax.ShapeDtypeStruct((2 * M, PIECE + rows, 128), BF)
+    back = exchange(small(second_sum_kernel, "sum_all", last, part, even_back), even_groups)
+    half_done = unpack(side[None], odd_back)
+    by_column, grad_qkv, grad_proj, grad_gain, loss = finish((1 - side)[None], back, half_done, count)
+    grad_inputs = by_column.transpose(0, 1, 3, 2, 4)
     return (grad_inputs, grad_qkv, grad_proj, grad_gain[0], loss[0, 0])
 
 

time: 122 us -> 115 us (0.943)
  waiting for transfers between devices: 9.61 us -> 16.3 us
  starting transfers between devices: 29.7 us -> 23.3 us
  Pallas kernels: 42.9 us -> 39.1 us
  local copies, waits for them, and re-layouts: 6.14 us -> 3.51 us
  blocking collectives: 31.1 us -> 28.6 us
  other arithmetic: 0.39 us -> 1.87 us
    all_to_all x4 -> x3, waiting for transfers between devices: 9.6 us -> 16.3 us  [exchange(): return lax.all_to_all(array, both, 0, 0, axis_index_groups=groups)]
    all_to_all x4 -> x3, starting transfers between devices: 26.3 us -> 19.8 us  [exchange(): return lax.all_to_all(array, both, 0, 0, axis_index_groups=groups)]
    pallas_call x2, Pallas kernels: 34.6 us -> 30.2 us  [main(): pl.pallas_call(main_kernel, in_specs=[SCALARS] + [WHOLE] * (len(args) - 1...]
    unnamed x32 -> x30, local copies, waits for them, and re-layouts: 5.02 us -> 2.35 us
    all_to_all x2, blocking collectives: 31.1 us -> 28.6 us  [exchange(): return lax.all_to_all(array, both, 0, 0, axis_index_groups=groups)]
    pallas_call x3 -> x4, Pallas kernels: 6.16 us -> 6.72 us  [the longest x2 3.14 us: pack(): pl.pallas_call(pack_kernel, in_specs=[SCALARS, HBM], out_specs=WHOLE, out...]
  transfers between devices with their start and end apart: 6 -> 5, of which waited for: 2 -> 2; matrix products, arithmetic and copies ran while one was open for 1% -> 3% of each run, Pallas kernels for 33% -> 17%
where the time goes in v4:
time: 115 us; the launch traced here: 114 us
  Pallas kernels  39.1 us (34%)
  blocking collectives  28.6 us (25%)
  starting transfers between devices  23.3 us (20%)
  waiting for transfers between devices  16.3 us (14%)
  local copies, waits for them, and re-layouts  3.51 us (3%)
  other arithmetic  1.87 us (2%)
    pallas_call x2, Pallas kernels, main(): pl.pallas_call(main_kernel, in_specs=[SCALARS] + [WHOLE] * (len(args) - 1...  30.2 us
    all_to_all x2, blocking collectives, exchange(): return lax.all_to_all(array, both, 0, 0, axis_index_groups=groups)  28.6 us
    all_to_all x3, starting transfers between devices, exchange(): return lax.all_to_all(array, both, 0, 0, axis_index_groups=groups)  19.8 us
    all_to_all x3, waiting for transfers between devices, exchange(): return lax.all_to_all(array, both, 0, 0, axis_index_groups=groups)  16.3 us
    pallas_call x2, Pallas kernels, pack(): pl.pallas_call(pack_kernel, in_specs=[SCALARS, HBM], out_specs=WHOLE, out...  3.14 us
    ppermute x1, starting transfers between devices, body(): odd_target = jnp.stack([odd_keep, lax.ppermute(odd_send, 'lon', odd_swap)])  2.92 us
    unnamed x30, local copies, waits for them, and re-layouts  2.35 us
  transfers between devices with their start and end apart: 5, of which 2 were waited for; matrix products, arithmetic and copies ran while one was open for 3% of the time, Pallas kernels for 17%

profile of v4, /device:TPU:0, one launch (start us, length us, event | category | flops | bytes accessed | tf_op | source)
XLA Modules:
  0.0 113.6 jit_solution(4933875921003916459)
XLA Ops:
  0.6 0.0 copy-start
  0.7 1.3 %copy-done = bf16[1,2,96,12,192]{4,2,3,1,0:T(8,128)(2,1)S(1)} copy-done((bf16[1,2,96,12,192]{4,2,3,1,0:T(8,128)(2,1)S(1)}, bf16[1,2,96,12,192]{4,2,3,1,0:T(8,128)(2,1)}, u32[]{:S(2)}) %copy-start) | copy-done | bytes 884760
  1.9 1.6 %pack_strip.2 = bf16[16,112,128]{2,1,0:T(8,128)(2,1)} custom-call(s32[1]{0:T(128)} %bitcast.at_ref.half_ref, bf16[1,2,12,96,192]{4,3,2,1,0:T(8,128)(2,1)S(1)} %bitcast.14), custom_call_target="tpu_custom_call" | custom-call | tf_op jit(solution)/shard_map/pack_strip/pallas_call | solution.py:105
  3.5 0.0 copy-start.11
  3.5 0.0 copy-start.12
  3.5 0.0 copy-start.10
  3.5 0.0 copy-start.13
  3.5 8.1 %all-to-all-start.1 = ((bf16[16,112,128]{2,1,0:T(8,128)(2,1)}), bf16[16,112,128]{2,1,0:T(8,128)(2,1)S(1)}, u32[]{:S(2)}, u32[]{:S(2)}) async-start(bf16[16,112,128]{2,1,0:T(8,128)(2,1)} %pack_strip.2), calls=%async_computation.1 | async-start | bytes 917504 | tf_op jit(solution)/shard_map/all_to_all | solution.py:514
  11.7 0.1 pad_add_fusion.at_ref
  11.8 1.1 pack_target.1
  12.8 0.0 copy-start.1
  12.9 0.5 collective-permute-start
  13.3 2.9 %collective-permute-start.1 = (bf16[112,128]{1,0:T(8,128)(2,1)S(1)}, bf16[112,128]{1,0:T(8,128)(2,1)S(1)}, u32[]{:S(2)}, u32[]{:S(2)}) collective-permute-start(bf16[112,128]{1,0:T(8,128)(2,1)S(1)} %get-tuple-element.36), channel_id=1, source_target_pairs={{0,120},{8,16},{16,8},{24,32},{32,24},{40,48},{48,40},{56,64},{64,... | collective-permute-start | bytes 86024 | tf_op jit(solution)/shard_map/ppermute | solution.py:526
  16.3 0.1 broadcast_compare_fusion
  16.4 0.1 dynamic-slice_convert_fusion
  16.4 0.1 broadcast_in_dim.78
  16.5 0.1 eq.67
  16.6 0.1 broadcast_in_dim.72
  16.7 0.1 eq.61
  16.8 0.1 broadcast_in_dim.75
  16.9 0.1 reshape.56
  17.0 0.1 broadcast_in_dim.34
  17.0 0.1 reshape.55
  17.2 0.1 broadcast_in_dim.37
  17.2 0.1 eq.56
  17.3 0.1 broadcast_in_dim.77
  17.4 0.1 eq.62
  17.5 0.9 and_select_fusion
  18.4 0.8 pad_maximum_fusion
  19.1 0.1 slice.3.wkv_ref
  19.3 0.2 copy.17
  19.4 0.1 copy.18
  19.6 1.6 %pack_strip.3 = bf16[16,112,128]{2,1,0:T(8,128)(2,1)} custom-call(s32[1]{0:T(128)} %bitcast.1.at_ref.half_ref, bf16[1,2,12,96,192]{4,3,2,1,0:T(8,128)(2,1)S(1)} %bitcast.15), custom_call_target="tpu_custom_call" | custom-call | tf_op jit(solution)/shard_map/pack_strip/pallas_call | solution.py:105
  21.2 2.0 %all-to-all-done.1.x_ref = bf16[16,112,128]{2,1,0:T(8,128)(2,1)S(1)} async-done(((bf16[16,112,128]{2,1,0:T(8,128)(2,1)}), bf16[16,112,128]{2,1,0:T(8,128)(2,1)S(1)}, u32[]{:S(2)}, u32[]{:S(2)}) %all-to-all-start.1) | async-done | bytes 458784 | tf_op jit(solution)/shard_map/all_to_all | solution.py:514
  23.2 7.7 %all-to-all-start = ((bf16[16,112,128]{2,1,0:T(8,128)(2,1)}), bf16[16,112,128]{2,1,0:T(8,128)(2,1)S(1)}, u32[]{:S(2)}, u32[]{:S(2)}) async-start(bf16[16,112,128]{2,1,0:T(8,128)(2,1)} %pack_strip.3), calls=%async_computation | async-start | bytes 917504 | tf_op jit(solution)/shard_map/all_to_all | solution.py:514
  30.9 15.1 %window_attention_crps.2 = (bf16[16,112,128]{2,1,0:T(8,128)(2,1)S(1)}, f32[784,192]{1,0:T(8,128)S(1)}) custom-call(s32[1]{0:T(128)} %bitcast.1.at_ref.half_ref, bf16[16,112,128]{2,1,0:T(8,128)(2,1)S(1)} %all-to-all-done.1.x_ref, bf16[2,112,128]{2,1,0:T(8,128)(2,1)S(1)} %pad_maximum_fusion.2.t_ref, f32[152,192]{1,0:T(8,128)S(1)} %copy-done.5, ...), custom_call_target="tpu_custom_call" | custom-call | tf_op jit(solution)/shard_map/window_attention_crps/pallas_call | solution.py:488
  46.0 0.0 copy-start.8
  46.0 0.8 copy-done.8
  46.8 15.2 %window_attention_crps.3 = bf16[16,192,128]{2,1,0:T(8,128)(2,1)S(1)} custom-call(s32[1]{0:T(128)} %bitcast.at_ref.half_ref, bf16[16,112,128]{2,1,0:T(8,128)(2,1)S(1)} %all-to-all-done.x_ref, bf16[2,112,128]{2,1,0:T(8,128)(2,1)S(1)} %pad_maximum_fusion.3.t_ref, f32[152,192]{1,0:T(8,128)S(1)} %get-tuple-element.39.aux_ref, f32[144,144]{1,0:T(8,128)S(1)} %copy-done.6, ...), custom_call_target="tpu_custom_call" | custom-call | tf_op jit(solution)/shard_map/window_attention_crps/pallas_call | solution.py:488
  61.9 0.0 copy-start.9
  62.0 18.6 %all_to_all.25.back_ref = bf16[16,192,128]{2,1,0:T(8,128)(2,1)S(1)} all-to-all(bf16[16,192,128]{2,1,0:T(8,128)(2,1)S(1)} %window_attention_crps.3), channel_id=1, replica_groups={{8,9,10,11,12,13,14,15,16,17,18,19,20,21,22,23},{24,25,26,27,28,29,30,3..., dimensions={0} | all-to-all | bytes 1572864 | tf_op jit(solution)/shard_map/all_to_all | solution.py:514
  80.5 0.1 sum_group.1
  80.6 10.0 %all_to_all.26.parts_ref = bf16[8,96,128]{2,1,0:T(8,128)(2,1)S(1)} all-to-all(bf16[8,96,128]{2,1,0:T(8,128)(2,1)S(1)} %sum_group.1), channel_id=1, replica_groups={{0,16,32,48,64,80,96,112},{1,17,33,49,65,81,97,113},{2,18,34,50,66,82,9..., dimensions={0} | all-to-all | bytes 393216 | tf_op jit(solution)/shard_map/all_to_all | solution.py:514
  90.6 1.0 sum_all.1
  91.6 4.0 %all-to-all-start.4 = ((bf16[16,208,128]{2,1,0:T(8,128)(2,1)}), bf16[16,208,128]{2,1,0:T(8,128)(2,1)S(1)}, u32[]{:S(2)}, u32[]{:S(2)}) async-start(bf16[16,208,128]{2,1,0:T(8,128)(2,1)} %sum_all.1), calls=%async_computation.4 | async-start | bytes 1703936 | tf_op jit(solution)/shard_map/all_to_all | solution.py:514
  95.6 1.4 %unpack_strip.1.half_done = bf16[1,2,12,96,192]{4,3,2,1,0:T(8,128)(2,1)} custom-call(s32[1]{0:T(128)} %bitcast.1.at_ref.half_ref, bf16[16,192,128]{2,1,0:T(8,128)(2,1)S(1)} %all_to_all.25.back_ref), custom_call_target="tpu_custom_call" | custom-call | tf_op jit(solution)/shard_map/unpack_strip/pallas_call | solution.py:194
  97.0 14.4 %all-to-all-done.4.back_ref = bf16[16,208,128]{2,1,0:T(8,128)(2,1)S(1)} async-done(((bf16[16,208,128]{2,1,0:T(8,128)(2,1)}), bf16[16,208,128]{2,1,0:T(8,128)(2,1)S(1)}, u32[]{:S(2)}, u32[]{:S(2)}) %all-to-all-start.4) | async-done | bytes 852000 | tf_op jit(solution)/shard_map/all_to_all | solution.py:514
  111.3 2.2 %finish.1 = (bf16[1,2,12,96,192]{4,3,2,1,0:T(8,128)(2,1)}, f32[192,576]{1,0:T(8,128)}, f32[192,192]{1,0:T(8,128)}, f32[1,192]{1,0:T(1,128)}, f32[1,1]{1,0:T(1,128)}) custom-call(s32[1]{0:T(128)} %bitcast.at_ref.half_ref, bf16[16,208,128]{2,1,0:T(8,128)(2,1)S(1)} %all-to-all-done.4.back_ref, ...), custom_call_target="tpu_custom_call", output_to_operand_aliasing={{0}: (2, {})} | custom-call | tf_op jit(solution)/shard_map/finish/pallas_call | solution.py:248
  (26 shorter events, 0.1 us)
Async XLA Ops:
  0.6 1.3 %copy-start = (bf16[1,2,96,12,192]{4,2,3,1,0:T(8,128)(2,1)S(1)}, bf16[1,2,96,12,192]{4,2,3,1,0:T(8,128)(2,1)}, u32[]{:S(2)}) copy-start(bf16[1,2,96,12,192]{4,2,3,1,0:T(8,128)(2,1)} %param.9) | copy-start | bytes 2654212
  1.9 9.8 %copy-start.3 = (bf16[2,96,12,192]{3,1,2,0:T(8,128)(2,1)S(1)}, bf16[2,96,12,192]{3,1,2,0:T(8,128)(2,1)}, u32[]{:S(2)}) copy-start(bf16[2,96,12,192]{3,1,2,0:T(8,128)(2,1)} %param.10) | copy-start | bytes 2654212
  3.5 12.8 %copy-start.11 = (s32[96]{0:T(128)S(1)}, s32[96]{0:T(128)}, u32[]{:S(2)}) copy-start(s32[96]{0:T(128)} %param.15) | copy-start | bytes 1156
  3.5 12.8 %copy-start.12 = (s32[96]{0:T(128)S(1)}, s32[96]{0:T(128)}, u32[]{:S(2)}) copy-start(s32[96]{0:T(128)} %param.14) | copy-start | bytes 1156
  3.5 14.0 %copy-start.10 = (pred[144,144]{1,0:T(8,128)(4,1)S(1)}, pred[144,144]{1,0:T(8,128)(4,1)}, u32[]{:S(2)}) copy-start(pred[144,144]{1,0:T(8,128)(4,1)} %constant.37.clone) | copy-start | bytes 62212
  3.5 14.9 %copy-start.13 = (f32[192]{0:T(256)S(1)}, f32[192]{0:T(256)}, u32[]{:S(2)}) copy-start(f32[192]{0:T(256)} %param.11) | copy-start | bytes 2308
  3.5 19.6 %all-to-all-start.1 = ((bf16[16,112,128]{2,1,0:T(8,128)(2,1)}), bf16[16,112,128]{2,1,0:T(8,128)(2,1)S(1)}, u32[]{:S(2)}, u32[]{:S(2)}) async-start(bf16[16,112,128]{2,1,0:T(8,128)(2,1)} %pack_strip.2), calls=%async_computation.1 | async-start | bytes 917504 | tf_op jit(solution)/shard_map/all_to_all | solution.py:514
  11.7 7.5 %copy-start.2 = (bf16[192,576]{1,0:T(8,128)(2,1)S(1)}, bf16[192,576]{1,0:T(8,128)(2,1)}, u32[]{:S(2)}) copy-start(bf16[192,576]{1,0:T(8,128)(2,1)} %wqkv_ref.1) | copy-start | bytes 663556
  11.8 7.7 %copy-start.4 = (bf16[192,192]{1,0:T(8,128)(2,1)S(1)}, bf16[192,192]{1,0:T(8,128)(2,1)}, u32[]{:S(2)}) copy-start(bf16[192,192]{1,0:T(8,128)(2,1)} %wproj_ref.1) | copy-start | bytes 221188
  12.8 6.7 %copy-start.1 = (bf16[1,2,96,12,192]{4,2,3,1,0:T(8,128)(2,1)S(1)}, bf16[1,2,96,12,192]{4,2,3,1,0:T(8,128)(2,1)}, u32[]{:S(2)}) copy-start(bf16[1,2,96,12,192]{4,2,3,1,0:T(8,128)(2,1)} %param.9) | copy-start | bytes 2654212
  12.9 8.3 %collective-permute-start = (bf16[112,128]{1,0:T(8,128)(2,1)S(1)}, bf16[112,128]{1,0:T(8,128)(2,1)S(1)}, u32[]{:S(2)}, u32[]{:S(2)}) collective-permute-start(bf16[112,128]{1,0:T(8,128)(2,1)S(1)} %get-tuple-element.34), channel_id=1, source_target_pairs={{0,8},{8,0},{16,24},{24,16},{32,40},{40,32},{48,56},{56,48},{64,72... | collective-permute-start | bytes 86024 | tf_op jit(solution)/shard_map/ppermute | solution.py:525
  13.3 7.8 %collective-permute-start.1 = (bf16[112,128]{1,0:T(8,128)(2,1)S(1)}, bf16[112,128]{1,0:T(8,128)(2,1)S(1)}, u32[]{:S(2)}, u32[]{:S(2)}) collective-permute-start(bf16[112,128]{1,0:T(8,128)(2,1)S(1)} %get-tuple-element.36), channel_id=1, source_target_pairs={{0,120},{8,16},{16,8},{24,32},{32,24},{40,48},{48,40},{56,64},{64,... | collective-permute-start | bytes 86024 | tf_op jit(solution)/shard_map/ppermute | solution.py:526
  21.1 9.8 %copy-start.5 = (f32[152,192]{1,0:T(8,128)S(1)}, f32[152,192]{1,0:T(8,128)}, u32[]{:S(2)}) copy-start(f32[152,192]{1,0:T(8,128)} %get-tuple-element.48.aux_ref) | copy-start | bytes 350212
  21.1 9.8 %copy-start.7 = (f32[144,144]{1,0:T(8,128)S(1)}, f32[144,144]{1,0:T(8,128)}, u32[]{:S(2)}) copy-start(f32[144,144]{1,0:T(8,128)} %get-tuple-element.49.bias_ref) | copy-start | bytes 248836
  21.2 25.5 %copy-start.6 = (f32[144,144]{1,0:T(8,128)S(1)}, f32[144,144]{1,0:T(8,128)}, u32[]{:S(2)}) copy-start(f32[144,144]{1,0:T(8,128)} %get-tuple-element.40.bias_ref) | copy-start | bytes 248836
  23.2 23.6 %all-to-all-start = ((bf16[16,112,128]{2,1,0:T(8,128)(2,1)}), bf16[16,112,128]{2,1,0:T(8,128)(2,1)S(1)}, u32[]{:S(2)}, u32[]{:S(2)}) async-start(bf16[16,112,128]{2,1,0:T(8,128)(2,1)} %pack_strip.3), calls=%async_computation | async-start | bytes 917504 | tf_op jit(solution)/shard_map/all_to_all | solution.py:514
  46.0 0.8 copy-start.8
  61.9 28.7 %copy-start.9 = (bf16[16,112,128]{2,1,0:T(8,128)(2,1)S(1)}, bf16[16,112,128]{2,1,0:T(8,128)(2,1)}, u32[]{:S(2)}) copy-start(bf16[16,112,128]{2,1,0:T(8,128)(2,1)} %copy-done.8) | copy-start | bytes 1376260
  91.6 19.8 %all-to-all-start.4 = ((bf16[16,208,128]{2,1,0:T(8,128)(2,1)}), bf16[16,208,128]{2,1,0:T(8,128)(2,1)S(1)}, u32[]{:S(2)}, u32[]{:S(2)}) async-start(bf16[16,208,128]{2,1,0:T(8,128)(2,1)} %sum_all.1), calls=%async_computation.4 | async-start | bytes 1703936 | tf_op jit(solution)/shard_map/all_to_all | solution.py:514

commit v5 on v4

--- a/solution.py
+++ b/solution.py
@@ -299,6 +299,17 @@
         [jnp.where(eastern, received, kept), jnp.where(eastern, kept, received)], axis=0
     )
 
+    def steps(body, unroll):
+        def group(first, carry):
+            for step in range(unroll):
+                body(first * unroll + step)
+            return carry
+
+        whole = (M - 3) // unroll
+        lax.fori_loop(0, whole, group, 0)
+        for step in range(whole * unroll, M):
+            body(step, min(3, last - step))
+
 
     def project_qkv(window):
         x = x_s[window]
@@ -330,25 +341,31 @@
             for head in range(HEADS):
                 stage(window, head)
 
-    def forward(step, carry):
+    def forward(step, left=3):
         projt = dot(wprojt_ref[...], att_s[step]).astype(BF)
-        heads((attend_head, jnp.minimum(step + 1, last)), (score_head, jnp.minimum(step + 2, last)))
-        project_qkv(jnp.minimum(step + 3, last))
+        heads(*[(stage, step + ahead) for stage, ahead in ((attend_head, 1), (score_head, 2)) if ahead <= left])
+        if left >= 3:
+            project_qkv(step + 3)
         mixed_s[step] = x_s[step] + projt.T.astype(F32)
-        return carry
 
     project_qkv(0)
     heads((score_head, 0))
     project_qkv(1)
     heads((attend_head, 0), (score_head, 1))
     project_qkv(2)
-    lax.fori_loop(0, M, forward, 0)
+    steps(forward, 5)
 
     def crps(step, score):
-        rows = pl.ds(pl.multiple_of(step * 8, 8), 8)
-        valid = valid_ref[rows]
-        target = t_s[rows]
-        mixed = [mixed_s[m, rows] for m in range(M)]
+        rows = pl.ds(pl.multiple_of(step * 16, 16), 16)
+
+        def load(ref):
+            value = ref[rows]
+            rest = jnp.concatenate([value[:, 128:], jnp.zeros((16, 64), F32)], axis=1)
+            return jnp.concatenate([value[:, :128], rest[:8] + pltpu.roll(rest[8:], 64, 1)], axis=0)
+
+        valid = load(valid_ref)
+        target = load(t_s)
+        mixed = [load(mixed_s.at[m]) for m in range(M)]
         rounded = [value.astype(BF).astype(F32) for value in mixed]
         slopes = [None] * M
         pairs = None
@@ -368,11 +385,16 @@
             square = diff * diff + DELTA_SQ
             inverse = lax.rsqrt(square)
             total = total + square * inverse
-            mixed_s[m, rows] = valid * (diff * inverse - slopes[m] / M)
-        return score + valid * total
+            grad = valid * (diff * inverse - slopes[m] / M)
+            rest = grad[16:]
+            mixed_s[m, rows] = jnp.concatenate(
+                [grad[:16], jnp.concatenate([rest[:, :64], pltpu.roll(rest, 64, 1)[:, :64]], axis=0)], axis=1
+            )
+        total = valid * total
+        return score + (total[:8] + total[8:16] + total[16:])
 
     sums_s[...] = jnp.zeros_like(sums_s) if before_ref is None else before_ref[...]
-    score_s[...] = lax.fori_loop(0, 18, crps, score_s[...])
+    score_s[:, :128] += lax.fori_loop(0, 9, crps, jnp.zeros((8, 128), F32), unroll=9)
 
     def grad_attended(window):
         gat = dot_t(wproj_ref[...], mixed_s[window].astype(BF)).astype(BF)
@@ -405,21 +427,21 @@
         second = jnp.mean(scaled * xhat, axis=1, keepdims=True)
         x_s[window] = mixed_s[window] + rstd_s[window] * (scaled - first - xhat * second)
 
-    def backward(step, carry):
+    def backward(step, left=3):
         gbt = dot(wqkv_ref[...], grad_s[step]).astype(BF)
         sqkv_s[...] += dot(grad_s[step], n_s[step])
         sproj_s[...] += dot(att_s[step], mixed_s[step].astype(BF))
-        heads((grad_qkv_head, jnp.minimum(step + 1, last)), (grad_score_head, jnp.minimum(step + 2, last)))
-        grad_attended(jnp.minimum(step + 3, last))
+        heads(*[(stage, step + ahead) for stage, ahead in ((grad_qkv_head, 1), (grad_score_head, 2)) if ahead <= left])
+        if left >= 3:
+            grad_attended(step + 3)
         grad_norm(step, gbt)
-        return carry
 
     grad_attended(0)
     heads((grad_score_head, 0))
     grad_attended(1)
     heads((grad_qkv_head, 0), (grad_score_head, 1))
     grad_attended(2)
-    lax.fori_loop(0, M, backward, 0, unroll=2)
+    steps(backward, 5)
 
     def pieces(member):
         return [pack_half(x_s[member, half * HALF : (half + 1) * HALF]).astype(BF) for half in range(2)]

time: 115 us -> 108 us (0.939)
  Pallas kernels: 39.1 us -> 31.8 us
    pallas_call x2, Pallas kernels: 30.2 us -> 22.9 us  [main(): pl.pallas_call(main_kernel, in_specs=[SCALARS] + [WHOLE] * (len(args) - 1...]
  transfers between devices with their start and end apart: 5 -> 5, of which waited for: 2 -> 2; matrix products, arithmetic and copies ran while one was open for 3% -> 3% of each run, Pallas kernels for 17% -> 14%
where the time goes in v5:
time: 108 us; the launch traced here: 106 us
  Pallas kernels  31.8 us (29%)
  blocking collectives  28.6 us (26%)
  starting transfers between devices  23.2 us (21%)
  waiting for transfers between devices  16.3 us (15%)
  local copies, waits for them, and re-layouts  3.51 us (3%)
  other arithmetic  1.87 us (2%)
  between operations  1.09 us (1%)
    all_to_all x2, blocking collectives, exchange(): return lax.all_to_all(array, both, 0, 0, axis_index_groups=groups)  28.6 us
    pallas_call x2, Pallas kernels, main(): pl.pallas_call(main_kernel, in_specs=[SCALARS] + [WHOLE] * (len(args) - 1...  22.9 us
    all_to_all x3, starting transfers between devices, exchange(): return lax.all_to_all(array, both, 0, 0, axis_index_groups=groups)  19.8 us
    all_to_all x3, waiting for transfers between devices, exchange(): return lax.all_to_all(array, both, 0, 0, axis_index_groups=groups)  16.3 us
    pallas_call x2, Pallas kernels, pack(): pl.pallas_call(pack_kernel, in_specs=[SCALARS, HBM], out_specs=WHOLE, out...  3.14 us
    ppermute x1, starting transfers between devices, body(): odd_target = jnp.stack([odd_keep, lax.ppermute(odd_send, 'lon', odd_swap)])  2.92 us
    unnamed x30, local copies, waits for them, and re-layouts  2.36 us
    pallas_call x1, Pallas kernels, finish(): pl.pallas_call(functools.partial(finish_kernel, count ** (-0.5), 1.0 / (c...  2.21 us
  transfers between devices with their start and end apart: 5, of which 2 were waited for; matrix products, arithmetic and copies ran while one was open for 3% of the time, Pallas kernels for 14%

profile of v5, /device:TPU:0, one launch (start us, length us, event | category | flops | bytes accessed | tf_op | source)
XLA Modules:
  0.0 106.4 jit_solution(14096512359635113255)
XLA Ops:
  0.6 0.0 copy-start
  0.7 1.3 %copy-done = bf16[1,2,96,12,192]{4,2,3,1,0:T(8,128)(2,1)S(1)} copy-done((bf16[1,2,96,12,192]{4,2,3,1,0:T(8,128)(2,1)S(1)}, bf16[1,2,96,12,192]{4,2,3,1,0:T(8,128)(2,1)}, u32[]{:S(2)}) %copy-start) | copy-done | bytes 884760
  1.9 1.6 %pack_strip.2 = bf16[16,112,128]{2,1,0:T(8,128)(2,1)} custom-call(s32[1]{0:T(128)} %bitcast.at_ref.half_ref, bf16[1,2,12,96,192]{4,3,2,1,0:T(8,128)(2,1)S(1)} %bitcast.14), custom_call_target="tpu_custom_call" | custom-call | tf_op jit(solution)/shard_map/pack_strip/pallas_call | solution.py:105
  3.5 0.0 copy-start.11
  3.5 0.0 copy-start.12
  3.5 0.0 copy-start.10
  3.5 0.0 copy-start.13
  3.5 8.1 %all-to-all-start.1 = ((bf16[16,112,128]{2,1,0:T(8,128)(2,1)}), bf16[16,112,128]{2,1,0:T(8,128)(2,1)S(1)}, u32[]{:S(2)}, u32[]{:S(2)}) async-start(bf16[16,112,128]{2,1,0:T(8,128)(2,1)} %pack_strip.2), calls=%async_computation.1 | async-start | bytes 917504 | tf_op jit(solution)/shard_map/all_to_all | solution.py:536
  11.7 0.0 copy-start.2
  11.7 0.1 pad_add_fusion.at_ref
  11.8 1.1 %pack_target.1 = (bf16[112,128]{1,0:T(8,128)(2,1)S(1)}, bf16[112,128]{1,0:T(8,128)(2,1)S(1)}, bf16[112,128]{1,0:T(8,128)(2,1)S(1)}, bf16[112,128]{1,0:T(8,128)(2,1)S(1)}) custom-call(s32[2]{0:T(128)S(1)} %pad_add_fusion.at_ref, bf16[2,12,96,192]{3,2,1,0:T(8,128)(2,1)S(1)} %bitcast.18), custom_call_target="tpu_custom_call" | custom-call | tf_op jit(solution)/shard_map/pack_target/pallas_call | solution.py:143
  12.8 0.0 copy-start.1
  12.9 0.5 collective-permute-start
  13.3 2.9 %collective-permute-start.1 = (bf16[112,128]{1,0:T(8,128)(2,1)S(1)}, bf16[112,128]{1,0:T(8,128)(2,1)S(1)}, u32[]{:S(2)}, u32[]{:S(2)}) collective-permute-start(bf16[112,128]{1,0:T(8,128)(2,1)S(1)} %get-tuple-element.36), channel_id=1, source_target_pairs={{0,120},{8,16},{16,8},{24,32},{32,24},{40,48},{48,40},{56,64},{64,... | collective-permute-start | bytes 86024 | tf_op jit(solution)/shard_map/ppermute | solution.py:548
  16.3 0.1 broadcast_compare_fusion
  16.4 0.1 dynamic-slice_convert_fusion
  16.4 0.1 broadcast_in_dim.78
  16.5 0.1 eq.67
  16.6 0.1 broadcast_in_dim.72
  16.7 0.1 eq.61
  16.8 0.1 broadcast_in_dim.75
  16.9 0.1 reshape.56
  17.0 0.1 broadcast_in_dim.34
  17.0 0.1 reshape.55
  17.2 0.1 broadcast_in_dim.37
  17.2 0.1 eq.56
  17.3 0.1 broadcast_in_dim.77
  17.4 0.1 eq.62
  17.5 0.9 and_select_fusion
  18.4 0.8 pad_maximum_fusion
  19.2 0.1 slice.3.wkv_ref
  19.3 0.2 copy.17
  19.4 0.1 copy.18
  19.6 1.6 %pack_strip.3 = bf16[16,112,128]{2,1,0:T(8,128)(2,1)} custom-call(s32[1]{0:T(128)} %bitcast.1.at_ref.half_ref, bf16[1,2,12,96,192]{4,3,2,1,0:T(8,128)(2,1)S(1)} %bitcast.15), custom_call_target="tpu_custom_call" | custom-call | tf_op jit(solution)/shard_map/pack_strip/pallas_call | solution.py:105
  21.1 0.0 copy-start.5
  21.2 2.0 %all-to-all-done.1.x_ref = bf16[16,112,128]{2,1,0:T(8,128)(2,1)S(1)} async-done(((bf16[16,112,128]{2,1,0:T(8,128)(2,1)}), bf16[16,112,128]{2,1,0:T(8,128)(2,1)S(1)}, u32[]{:S(2)}, u32[]{:S(2)}) %all-to-all-start.1) | async-done | bytes 458784 | tf_op jit(solution)/shard_map/all_to_all | solution.py:536
  23.2 7.7 %all-to-all-start = ((bf16[16,112,128]{2,1,0:T(8,128)(2,1)}), bf16[16,112,128]{2,1,0:T(8,128)(2,1)S(1)}, u32[]{:S(2)}, u32[]{:S(2)}) async-start(bf16[16,112,128]{2,1,0:T(8,128)(2,1)} %pack_strip.3), calls=%async_computation | async-start | bytes 917504 | tf_op jit(solution)/shard_map/all_to_all | solution.py:536
  30.9 11.3 %window_attention_crps.2 = (bf16[16,112,128]{2,1,0:T(8,128)(2,1)S(1)}, f32[784,192]{1,0:T(8,128)S(1)}) custom-call(s32[1]{0:T(128)} %bitcast.1.at_ref.half_ref, bf16[16,112,128]{2,1,0:T(8,128)(2,1)S(1)} %all-to-all-done.1.x_ref, bf16[2,112,128]{2,1,0:T(8,128)(2,1)S(1)} %pad_maximum_fusion.2.t_ref, f32[152,192]{1,0:T(8,128)S(1)} %copy-done.5, ...), custom_call_target="tpu_custom_call" | custom-call | tf_op jit(solution)/shard_map/window_attention_crps/pallas_call | solution.py:510
  42.3 0.8 copy-done.8
  43.0 11.6 %window_attention_crps.3 = bf16[16,192,128]{2,1,0:T(8,128)(2,1)S(1)} custom-call(s32[1]{0:T(128)} %bitcast.at_ref.half_ref, bf16[16,112,128]{2,1,0:T(8,128)(2,1)S(1)} %all-to-all-done.x_ref, bf16[2,112,128]{2,1,0:T(8,128)(2,1)S(1)} %pad_maximum_fusion.3.t_ref, f32[152,192]{1,0:T(8,128)S(1)} %get-tuple-element.39.aux_ref, f32[144,144]{1,0:T(8,128)S(1)} %copy-done.6, ...), custom_call_target="tpu_custom_call" | custom-call | tf_op jit(solution)/shard_map/window_attention_crps/pallas_call | solution.py:510
  54.6 18.6 %all_to_all.25.back_ref = bf16[16,192,128]{2,1,0:T(8,128)(2,1)S(1)} all-to-all(bf16[16,192,128]{2,1,0:T(8,128)(2,1)S(1)} %window_attention_crps.3), channel_id=1, replica_groups={{8,9,10,11,12,13,14,15,16,17,18,19,20,21,22,23},{24,25,26,27,28,29,30,3..., dimensions={0} | all-to-all | bytes 1572864 | tf_op jit(solution)/shard_map/all_to_all | solution.py:536
  73.2 0.1 sum_group.1
  73.3 10.0 %all_to_all.26.parts_ref = bf16[8,96,128]{2,1,0:T(8,128)(2,1)S(1)} all-to-all(bf16[8,96,128]{2,1,0:T(8,128)(2,1)S(1)} %sum_group.1), channel_id=1, replica_groups={{0,16,32,48,64,80,96,112},{1,17,33,49,65,81,97,113},{2,18,34,50,66,82,9..., dimensions={0} | all-to-all | bytes 393216 | tf_op jit(solution)/shard_map/all_to_all | solution.py:536
  83.3 1.0 sum_all.1
  84.3 4.0 %all-to-all-start.4 = ((bf16[16,208,128]{2,1,0:T(8,128)(2,1)}), bf16[16,208,128]{2,1,0:T(8,128)(2,1)S(1)}, u32[]{:S(2)}, u32[]{:S(2)}) async-start(bf16[16,208,128]{2,1,0:T(8,128)(2,1)} %sum_all.1), calls=%async_computation.4 | async-start | bytes 1703936 | tf_op jit(solution)/shard_map/all_to_all | solution.py:536
  88.3 1.4 %unpack_strip.1.half_done = bf16[1,2,12,96,192]{4,3,2,1,0:T(8,128)(2,1)} custom-call(s32[1]{0:T(128)} %bitcast.1.at_ref.half_ref, bf16[16,192,128]{2,1,0:T(8,128)(2,1)S(1)} %all_to_all.25.back_ref), custom_call_target="tpu_custom_call" | custom-call | tf_op jit(solution)/shard_map/unpack_strip/pallas_call | solution.py:194
  89.7 14.4 %all-to-all-done.4.back_ref = bf16[16,208,128]{2,1,0:T(8,128)(2,1)S(1)} async-done(((bf16[16,208,128]{2,1,0:T(8,128)(2,1)}), bf16[16,208,128]{2,1,0:T(8,128)(2,1)S(1)}, u32[]{:S(2)}, u32[]{:S(2)}) %all-to-all-start.4) | async-done | bytes 852000 | tf_op jit(solution)/shard_map/all_to_all | solution.py:536
  104.0 2.2 %finish.1 = (bf16[1,2,12,96,192]{4,3,2,1,0:T(8,128)(2,1)}, f32[192,576]{1,0:T(8,128)}, f32[192,192]{1,0:T(8,128)}, f32[1,192]{1,0:T(1,128)}, f32[1,1]{1,0:T(1,128)}) custom-call(s32[1]{0:T(128)} %bitcast.at_ref.half_ref, bf16[16,208,128]{2,1,0:T(8,128)(2,1)S(1)} %all-to-all-done.4.back_ref, ...), custom_call_target="tpu_custom_call", output_to_operand_aliasing={{0}: (2, {})} | custom-call | tf_op jit(solution)/shard_map/finish/pallas_call | solution.py:248
  (26 shorter events, 0.1 us)
Async XLA Ops:
  0.6 1.3 %copy-start = (bf16[1,2,96,12,192]{4,2,3,1,0:T(8,128)(2,1)S(1)}, bf16[1,2,96,12,192]{4,2,3,1,0:T(8,128)(2,1)}, u32[]{:S(2)}) copy-start(bf16[1,2,96,12,192]{4,2,3,1,0:T(8,128)(2,1)} %param.9) | copy-start | bytes 2654212
  1.9 9.8 %copy-start.3 = (bf16[2,96,12,192]{3,1,2,0:T(8,128)(2,1)S(1)}, bf16[2,96,12,192]{3,1,2,0:T(8,128)(2,1)}, u32[]{:S(2)}) copy-start(bf16[2,96,12,192]{3,1,2,0:T(8,128)(2,1)} %param.10) | copy-start | bytes 2654212
  3.5 12.8 %copy-start.11 = (s32[96]{0:T(128)S(1)}, s32[96]{0:T(128)}, u32[]{:S(2)}) copy-start(s32[96]{0:T(128)} %param.15) | copy-start | bytes 1156
  3.5 12.8 %copy-start.12 = (s32[96]{0:T(128)S(1)}, s32[96]{0:T(128)}, u32[]{:S(2)}) copy-start(s32[96]{0:T(128)} %param.14) | copy-start | bytes 1156
  3.5 14.0 %copy-start.10 = (pred[144,144]{1,0:T(8,128)(4,1)S(1)}, pred[144,144]{1,0:T(8,128)(4,1)}, u32[]{:S(2)}) copy-start(pred[144,144]{1,0:T(8,128)(4,1)} %constant.37.clone) | copy-start | bytes 62212
  3.5 14.9 %copy-start.13 = (f32[192]{0:T(256)S(1)}, f32[192]{0:T(256)}, u32[]{:S(2)}) copy-start(f32[192]{0:T(256)} %param.11) | copy-start | bytes 2308
  3.5 19.6 %all-to-all-start.1 = ((bf16[16,112,128]{2,1,0:T(8,128)(2,1)}), bf16[16,112,128]{2,1,0:T(8,128)(2,1)S(1)}, u32[]{:S(2)}, u32[]{:S(2)}) async-start(bf16[16,112,128]{2,1,0:T(8,128)(2,1)} %pack_strip.2), calls=%async_computation.1 | async-start | bytes 917504 | tf_op jit(solution)/shard_map/all_to_all | solution.py:536
  11.7 7.5 %copy-start.2 = (bf16[192,576]{1,0:T(8,128)(2,1)S(1)}, bf16[192,576]{1,0:T(8,128)(2,1)}, u32[]{:S(2)}) copy-start(bf16[192,576]{1,0:T(8,128)(2,1)} %wqkv_ref.1) | copy-start | bytes 663556
  11.8 7.7 %copy-start.4 = (bf16[192,192]{1,0:T(8,128)(2,1)S(1)}, bf16[192,192]{1,0:T(8,128)(2,1)}, u32[]{:S(2)}) copy-start(bf16[192,192]{1,0:T(8,128)(2,1)} %wproj_ref.1) | copy-start | bytes 221188
  12.8 6.7 %copy-start.1 = (bf16[1,2,96,12,192]{4,2,3,1,0:T(8,128)(2,1)S(1)}, bf16[1,2,96,12,192]{4,2,3,1,0:T(8,128)(2,1)}, u32[]{:S(2)}) copy-start(bf16[1,2,96,12,192]{4,2,3,1,0:T(8,128)(2,1)} %param.9) | copy-start | bytes 2654212
  12.9 8.3 %collective-permute-start = (bf16[112,128]{1,0:T(8,128)(2,1)S(1)}, bf16[112,128]{1,0:T(8,128)(2,1)S(1)}, u32[]{:S(2)}, u32[]{:S(2)}) collective-permute-start(bf16[112,128]{1,0:T(8,128)(2,1)S(1)} %get-tuple-element.34), channel_id=1, source_target_pairs={{0,8},{8,0},{16,24},{24,16},{32,40},{40,32},{48,56},{56,48},{64,72... | collective-permute-start | bytes 86024 | tf_op jit(solution)/shard_map/ppermute | solution.py:547
  13.3 7.8 %collective-permute-start.1 = (bf16[112,128]{1,0:T(8,128)(2,1)S(1)}, bf16[112,128]{1,0:T(8,128)(2,1)S(1)}, u32[]{:S(2)}, u32[]{:S(2)}) collective-permute-start(bf16[112,128]{1,0:T(8,128)(2,1)S(1)} %get-tuple-element.36), channel_id=1, source_target_pairs={{0,120},{8,16},{16,8},{24,32},{32,24},{40,48},{48,40},{56,64},{64,... | collective-permute-start | bytes 86024 | tf_op jit(solution)/shard_map/ppermute | solution.py:548
  21.1 9.8 %copy-start.5 = (f32[152,192]{1,0:T(8,128)S(1)}, f32[152,192]{1,0:T(8,128)}, u32[]{:S(2)}) copy-start(f32[152,192]{1,0:T(8,128)} %get-tuple-element.48.aux_ref) | copy-start | bytes 350212
  21.2 9.8 %copy-start.7 = (f32[144,144]{1,0:T(8,128)S(1)}, f32[144,144]{1,0:T(8,128)}, u32[]{:S(2)}) copy-start(f32[144,144]{1,0:T(8,128)} %get-tuple-element.49.bias_ref) | copy-start | bytes 248836
  21.2 21.8 %copy-start.6 = (f32[144,144]{1,0:T(8,128)S(1)}, f32[144,144]{1,0:T(8,128)}, u32[]{:S(2)}) copy-start(f32[144,144]{1,0:T(8,128)} %get-tuple-element.40.bias_ref) | copy-start | bytes 248836
  23.2 19.8 %all-to-all-start = ((bf16[16,112,128]{2,1,0:T(8,128)(2,1)}), bf16[16,112,128]{2,1,0:T(8,128)(2,1)S(1)}, u32[]{:S(2)}, u32[]{:S(2)}) async-start(bf16[16,112,128]{2,1,0:T(8,128)(2,1)} %pack_strip.3), calls=%async_computation | async-start | bytes 917504 | tf_op jit(solution)/shard_map/all_to_all | solution.py:536
  42.2 0.8 copy-start.8
  54.6 28.7 %copy-start.9 = (bf16[16,112,128]{2,1,0:T(8,128)(2,1)S(1)}, bf16[16,112,128]{2,1,0:T(8,128)(2,1)}, u32[]{:S(2)}) copy-start(bf16[16,112,128]{2,1,0:T(8,128)(2,1)} %copy-done.8) | copy-start | bytes 1376260
  84.3 19.7 %all-to-all-start.4 = ((bf16[16,208,128]{2,1,0:T(8,128)(2,1)}), bf16[16,208,128]{2,1,0:T(8,128)(2,1)S(1)}, u32[]{:S(2)}, u32[]{:S(2)}) async-start(bf16[16,208,128]{2,1,0:T(8,128)(2,1)} %sum_all.1), calls=%async_computation.4 | async-start | bytes 1703936 | tf_op jit(solution)/shard_map/all_to_all | solution.py:536

commit v6 on v5

--- a/solution.py
+++ b/solution.py
@@ -81,17 +81,14 @@
     return cells
 
 
-def pack_kernel(at_ref, x_hbm, out_ref, x_ref, semaphore):
-    copy = pltpu.make_async_copy(x_hbm.at[0, :, pl.ds(at_ref[0] * 6, 6)], x_ref, semaphore)
-    copy.start()
+def pack_kernel(x_ref, out_ref):
     parts = cell_parts(0)
-    copy.wait()
     for quad in range(2):
         for i in range(4):
 
             def tile(level, s):
                 at = 16 * (3 * quad + FIRST[i] + s)
-                return x_ref[level, :, at : at + 16, :].reshape(96, C)
+                return x_ref[0, level, :, at : at + 16, :].reshape(96, C)
 
             def place(level, s):
                 return place_of(parts, i, FIRST[i], level, s)
@@ -104,13 +101,12 @@
 def pack(half, inputs):
     return pl.pallas_call(
         pack_kernel,
-        in_specs=[SCALARS, HBM],
+        in_specs=[WHOLE],
         out_specs=WHOLE,
         out_shape=jax.ShapeDtypeStruct((2 * M, PIECE, 128), BF),
-        scratch_shapes=[pltpu.VMEM((2, 6, 96, C), BF), pltpu.SemaphoreType.DMA],
         compiler_params=PARAMS,
         name="pack_strip",
-    )(half, inputs)
+    )(lax.dynamic_slice_in_dim(inputs, half * 6, 6, axis=2))
 
 
 def pack_target_kernel(at_ref, t_ref, even_keep, even_send, odd_keep, odd_send):
@@ -539,9 +535,9 @@
     at = jnp.stack([member, parity]).astype(jnp.int32)
     side = parity.astype(jnp.int32)
     by_column = inputs.transpose(0, 1, 3, 2, 4)
-    even = pack((1 - side)[None], by_column)
+    even = pack(1 - side, by_column)
     even, target, by_column = lax.optimization_barrier((even, target, by_column))
-    odd = pack(side[None], by_column)
+    odd = pack(side, by_column)
     even_keep, even_send, odd_keep, odd_send = pack_target(at, target.transpose(0, 2, 1, 3))
     even = exchange(even, even_groups)
     even_target = jnp.stack([even_keep, lax.ppermute(even_send, "lon", even_swap)])

time: 108 us -> 114 us (1.056)
  local copies, waits for them, and re-layouts: 3.51 us -> 10 us
  starting transfers between devices: 23.2 us -> 25.1 us
  waiting for transfers between devices: 16.3 us -> 14.4 us
  Pallas kernels: 31.8 us -> 30.5 us
    unnamed x30 -> x32, local copies, waits for them, and re-layouts: 2.36 us -> 8.76 us
    all_to_all x3, waiting for transfers between devices: 16.3 us -> 14.4 us  [exchange(): return lax.all_to_all(array, both, 0, 0, axis_index_groups=groups)]
    all_to_all x3, starting transfers between devices: 19.8 us -> 21.7 us  [exchange(): return lax.all_to_all(array, both, 0, 0, axis_index_groups=groups)]
  transfers between devices with their start and end apart: 5 -> 5, of which waited for: 2 -> 1; matrix products, arithmetic and copies ran while one was open for 3% -> 4% of each run, Pallas kernels for 14% -> 13%
where the time goes in v6:
time: 114 us; the launch traced here: 112 us
  Pallas kernels  30.5 us (27%)
  blocking collectives  28.6 us (25%)
  starting transfers between devices  25.1 us (22%)
  waiting for transfers between devices  14.4 us (13%)
  local copies, waits for them, and re-layouts  10 us (9%)
  other arithmetic  2.71 us (2%)
    all_to_all x2, blocking collectives, exchange(): return lax.all_to_all(array, both, 0, 0, axis_index_groups=groups)  28.6 us
    pallas_call x2, Pallas kernels, main(): pl.pallas_call(main_kernel, in_specs=[SCALARS] + [WHOLE] * (len(args) - 1...  22.8 us
    all_to_all x3, starting transfers between devices, exchange(): return lax.all_to_all(array, both, 0, 0, axis_index_groups=groups)  21.7 us
    all_to_all x3, waiting for transfers between devices, exchange(): return lax.all_to_all(array, both, 0, 0, axis_index_groups=groups)  14.4 us
    unnamed x32, local copies, waits for them, and re-layouts  8.76 us
    ppermute x1, starting transfers between devices, body(): odd_target = jnp.stack([odd_keep, lax.ppermute(odd_send, 'lon', odd_swap)])  2.93 us
    pallas_call x2, Pallas kernels, pack(): pl.pallas_call(pack_kernel, in_specs=[WHOLE], out_specs=WHOLE, out_shape=...  2.92 us
  transfers between devices with their start and end apart: 5, of which 1 were waited for; matrix products, arithmetic and copies ran while one was open for 4% of the time, Pallas kernels for 13%

profile of v6, /device:TPU:0, one launch (start us, length us, event | category | flops | bytes accessed | tf_op | source)
XLA Modules:
  0.0 112.2 jit_solution(6957507690883888899)
XLA Ops:
  0.7 1.2 %copy-done = bf16[1,2,96,12,192]{4,2,3,1,0:T(8,128)(2,1)S(1)} copy-done((bf16[1,2,96,12,192]{4,2,3,1,0:T(8,128)(2,1)S(1)}, bf16[1,2,96,12,192]{4,2,3,1,0:T(8,128)(2,1)}, u32[]{:S(2)}) %copy-start) | copy-done | bytes 884760
  2.0 1.5 %pack_strip.2 = bf16[16,112,128]{2,1,0:T(8,128)(2,1)} custom-call(bf16[1,2,6,96,192]{4,3,2,1,0:T(8,128)(2,1)S(1)} %dynamic-slice_bitcast_fusion.x_ref), custom_call_target="tpu_custom_call" | custom-call | tf_op jit(solution)/shard_map/pack_strip/pallas_call | solution.py:102
  3.4 8.1 %all-to-all-start.1 = ((bf16[16,112,128]{2,1,0:T(8,128)(2,1)}), bf16[16,112,128]{2,1,0:T(8,128)(2,1)S(1)}, u32[]{:S(2)}, u32[]{:S(2)}) async-start(bf16[16,112,128]{2,1,0:T(8,128)(2,1)} %pack_strip.2), calls=%async_computation.1 | async-start | bytes 917504 | tf_op jit(solution)/shard_map/all_to_all | solution.py:532
  11.5 0.1 pad_add_fusion.at_ref
  11.6 1.3 %copy-done.3 = bf16[2,96,12,192]{3,1,2,0:T(8,128)(2,1)S(1)} copy-done((bf16[2,96,12,192]{3,1,2,0:T(8,128)(2,1)S(1)}, bf16[2,96,12,192]{3,1,2,0:T(8,128)(2,1)}, u32[]{:S(2)}) %copy-start.3) | copy-done | bytes 884760
  12.9 1.1 pack_target.1
  14.0 0.5 collective-permute-start
  14.5 2.9 %collective-permute-start.1 = (bf16[112,128]{1,0:T(8,128)(2,1)S(1)}, bf16[112,128]{1,0:T(8,128)(2,1)}, u32[]{:S(2)}, u32[]{:S(2)}) collective-permute-start(bf16[112,128]{1,0:T(8,128)(2,1)S(1)} %get-tuple-element.36), channel_id=1, source_target_pairs={{0,120},{8,16},{16,8},{24,32},{32,24},{40,48},{48,40},{56,64},{64,... | collective-permute-start | bytes 86024 | tf_op jit(solution)/shard_map/ppermute | solution.py:544
  17.4 0.1 broadcast_compare_fusion
  17.5 0.1 dynamic-slice_convert_fusion
  17.6 0.1 broadcast_in_dim.73
  17.6 0.1 eq.67
  17.7 0.1 broadcast_in_dim.35
  17.8 0.1 eq.61
  17.9 0.1 broadcast_in_dim.70
  18.0 0.1 reshape.56
  18.1 0.1 broadcast_in_dim.31
  18.2 0.1 reshape.55
  18.3 0.1 broadcast_in_dim.34
  18.4 0.1 eq.56
  18.5 0.1 broadcast_in_dim.72
  18.5 0.1 eq.62
  18.6 0.9 and_select_fusion
  19.5 0.1 pad_maximum_fusion
  19.7 0.1 slice.3.wkv_ref
  19.8 0.2 copy.17
  20.0 0.4 copy-done.4
  20.4 0.1 copy.18
  20.5 1.5 %pack_strip.3 = bf16[16,112,128]{2,1,0:T(8,128)(2,1)} custom-call(bf16[1,2,6,96,192]{4,3,2,1,0:T(8,128)(2,1)S(1)} %constant_dynamic-slice_fusion.x_ref), custom_call_target="tpu_custom_call" | custom-call | tf_op jit(solution)/shard_map/pack_strip/pallas_call | solution.py:102
  22.0 0.8 pad_maximum_fusion.2.t_ref
  22.7 0.8 pad_maximum_fusion.3.t_ref
  23.5 9.5 %all-to-all-start = ((bf16[16,112,128]{2,1,0:T(8,128)(2,1)}), bf16[16,112,128]{2,1,0:T(8,128)(2,1)S(1)}, u32[]{:S(2)}, u32[]{:S(2)}) async-start(bf16[16,112,128]{2,1,0:T(8,128)(2,1)} %pack_strip.3), calls=%async_computation | async-start | bytes 917504 | tf_op jit(solution)/shard_map/all_to_all | solution.py:532
  33.0 0.9 copy-done.8
  33.9 11.2 %window_attention_crps.2 = (bf16[16,112,128]{2,1,0:T(8,128)(2,1)S(1)}, f32[784,192]{1,0:T(8,128)S(1)}) custom-call(s32[1]{0:T(128)} %bitcast.4.at_ref.half_ref, bf16[16,112,128]{2,1,0:T(8,128)(2,1)S(1)} %all-to-all-done.1.x_ref, bf16[2,112,128]{2,1,0:T(8,128)(2,1)S(1)} %pad_maximum_fusion.2.t_ref, f32[152,192]{1,0:T(8,128)S(1)} %get-tuple-element.48.aux_ref, ...), custom_call_target="tpu_custom_call" | custom-call | tf_op jit(solution)/shard_map/window_attention_crps/pallas_call | solution.py:506
  45.2 0.9 copy-done.5
  46.0 0.8 copy-done.9
  46.8 1.1 %copy-done.6 = f32[784,192]{1,0:T(8,128)S(1)} copy-done((f32[784,192]{1,0:T(8,128)S(1)}, f32[784,192]{1,0:T(8,128)}, u32[]{:S(2)}) %copy-start.6) | copy-done | bytes 602136
  48.0 0.9 copy-done.7
  48.9 11.5 %window_attention_crps.3 = bf16[16,192,128]{2,1,0:T(8,128)(2,1)S(1)} custom-call(s32[1]{0:T(128)} %bitcast.at_ref.half_ref, bf16[16,112,128]{2,1,0:T(8,128)(2,1)S(1)} %all-to-all-done.x_ref, bf16[2,112,128]{2,1,0:T(8,128)(2,1)S(1)} %pad_maximum_fusion.3.t_ref, f32[152,192]{1,0:T(8,128)S(1)} %get-tuple-element.39.aux_ref, f32[144,144]{1,0:T(8,128)S(1)} %copy-done.7, ...), custom_call_target="tpu_custom_call" | custom-call | tf_op jit(solution)/shard_map/window_attention_crps/pallas_call | solution.py:506
  60.4 18.3 %all_to_all.25.back_ref = bf16[16,192,128]{2,1,0:T(8,128)(2,1)S(1)} all-to-all(bf16[16,192,128]{2,1,0:T(8,128)(2,1)S(1)} %window_attention_crps.3), channel_id=1, replica_groups={{8,9,10,11,12,13,14,15,16,17,18,19,20,21,22,23},{24,25,26,27,28,29,30,3..., dimensions={0} | all-to-all | bytes 1572864 | tf_op jit(solution)/shard_map/all_to_all | solution.py:532
  78.7 0.1 sum_group.1
  78.8 10.3 %all_to_all.26.parts_ref = bf16[8,96,128]{2,1,0:T(8,128)(2,1)S(1)} all-to-all(bf16[8,96,128]{2,1,0:T(8,128)(2,1)S(1)} %sum_group.1), channel_id=1, replica_groups={{0,16,32,48,64,80,96,112},{1,17,33,49,65,81,97,113},{2,18,34,50,66,82,9..., dimensions={0} | all-to-all | bytes 393216 | tf_op jit(solution)/shard_map/all_to_all | solution.py:532
  89.0 0.1 sum_all.1
  89.1 0.9 copy-done.1
  90.0 4.0 %all-to-all-start.4 = ((bf16[16,208,128]{2,1,0:T(8,128)(2,1)}), bf16[16,208,128]{2,1,0:T(8,128)(2,1)S(1)}, u32[]{:S(2)}, u32[]{:S(2)}) async-start(bf16[16,208,128]{2,1,0:T(8,128)(2,1)} %copy-done.1), calls=%async_computation.4 | async-start | bytes 1703936 | tf_op jit(solution)/shard_map/all_to_all | solution.py:532
  94.1 1.4 %unpack_strip.1.half_done = bf16[1,2,12,96,192]{4,3,2,1,0:T(8,128)(2,1)} custom-call(s32[1]{0:T(128)} %bitcast.4.at_ref.half_ref, bf16[16,192,128]{2,1,0:T(8,128)(2,1)S(1)} %all_to_all.25.back_ref), custom_call_target="tpu_custom_call" | custom-call | tf_op jit(solution)/shard_map/unpack_strip/pallas_call | solution.py:190
  95.5 14.4 %all-to-all-done.4.back_ref = bf16[16,208,128]{2,1,0:T(8,128)(2,1)S(1)} async-done(((bf16[16,208,128]{2,1,0:T(8,128)(2,1)}), bf16[16,208,128]{2,1,0:T(8,128)(2,1)S(1)}, u32[]{:S(2)}, u32[]{:S(2)}) %all-to-all-start.4) | async-done | bytes 852000 | tf_op jit(solution)/shard_map/all_to_all | solution.py:532
  109.8 2.2 %finish.1 = (bf16[1,2,12,96,192]{4,3,2,1,0:T(8,128)(2,1)}, f32[192,576]{1,0:T(8,128)}, f32[192,192]{1,0:T(8,128)}, f32[1,192]{1,0:T(1,128)}, f32[1,1]{1,0:T(1,128)}) custom-call(s32[1]{0:T(128)} %bitcast.at_ref.half_ref, bf16[16,208,128]{2,1,0:T(8,128)(2,1)S(1)} %all-to-all-done.4.back_ref, ...), custom_call_target="tpu_custom_call", output_to_operand_aliasing={{0}: (2, {})} | custom-call | tf_op jit(solution)/shard_map/finish/pallas_call | solution.py:244
  (30 shorter events, 0.2 us)
Async XLA Ops:
  0.6 1.3 %copy-start = (bf16[1,2,96,12,192]{4,2,3,1,0:T(8,128)(2,1)S(1)}, bf16[1,2,96,12,192]{4,2,3,1,0:T(8,128)(2,1)}, u32[]{:S(2)}) copy-start(bf16[1,2,96,12,192]{4,2,3,1,0:T(8,128)(2,1)} %param.9) | copy-start | bytes 2654212
  3.4 14.0 %copy-start.12 = (s32[96]{0:T(128)S(1)}, s32[96]{0:T(128)}, u32[]{:S(2)}) copy-start(s32[96]{0:T(128)} %param.15) | copy-start | bytes 1156
  3.4 14.1 %copy-start.13 = (s32[96]{0:T(128)S(1)}, s32[96]{0:T(128)}, u32[]{:S(2)}) copy-start(s32[96]{0:T(128)} %param.14) | copy-start | bytes 1156
  3.4 15.2 %copy-start.11 = (pred[144,144]{1,0:T(8,128)(4,1)S(1)}, pred[144,144]{1,0:T(8,128)(4,1)}, u32[]{:S(2)}) copy-start(pred[144,144]{1,0:T(8,128)(4,1)} %constant.39.clone) | copy-start | bytes 62212
  3.4 16.1 %copy-start.14 = (f32[192]{0:T(256)S(1)}, f32[192]{0:T(256)}, u32[]{:S(2)}) copy-start(f32[192]{0:T(256)} %param.11) | copy-start | bytes 2308
  3.4 20.1 %all-to-all-start.1 = ((bf16[16,112,128]{2,1,0:T(8,128)(2,1)}), bf16[16,112,128]{2,1,0:T(8,128)(2,1)S(1)}, u32[]{:S(2)}, u32[]{:S(2)}) async-start(bf16[16,112,128]{2,1,0:T(8,128)(2,1)} %pack_strip.2), calls=%async_computation.1 | async-start | bytes 917504 | tf_op jit(solution)/shard_map/all_to_all | solution.py:532
  11.6 1.3 %copy-start.3 = (bf16[2,96,12,192]{3,1,2,0:T(8,128)(2,1)S(1)}, bf16[2,96,12,192]{3,1,2,0:T(8,128)(2,1)}, u32[]{:S(2)}) copy-start(bf16[2,96,12,192]{3,1,2,0:T(8,128)(2,1)} %param.10) | copy-start | bytes 2654212
  14.0 5.7 %copy-start.2 = (bf16[192,576]{1,0:T(8,128)(2,1)S(1)}, bf16[192,576]{1,0:T(8,128)(2,1)}, u32[]{:S(2)}) copy-start(bf16[192,576]{1,0:T(8,128)(2,1)} %wqkv_ref.1) | copy-start | bytes 663556
  14.0 8.0 %collective-permute-start = (bf16[112,128]{1,0:T(8,128)(2,1)S(1)}, bf16[112,128]{1,0:T(8,128)(2,1)}, u32[]{:S(2)}, u32[]{:S(2)}) collective-permute-start(bf16[112,128]{1,0:T(8,128)(2,1)S(1)} %get-tuple-element.34), channel_id=1, source_target_pairs={{0,8},{8,0},{16,24},{24,16},{32,40},{40,32},{48,56},{56,48},{64,72... | collective-permute-start | bytes 86024 | tf_op jit(solution)/shard_map/ppermute | solution.py:543
  14.5 8.3 %collective-permute-start.1 = (bf16[112,128]{1,0:T(8,128)(2,1)S(1)}, bf16[112,128]{1,0:T(8,128)(2,1)}, u32[]{:S(2)}, u32[]{:S(2)}) collective-permute-start(bf16[112,128]{1,0:T(8,128)(2,1)S(1)} %get-tuple-element.36), channel_id=1, source_target_pairs={{0,120},{8,16},{16,8},{24,32},{32,24},{40,48},{48,40},{56,64},{64,... | collective-permute-start | bytes 86024 | tf_op jit(solution)/shard_map/ppermute | solution.py:544
  19.5 0.9 copy-start.4
  23.5 23.3 %all-to-all-start = ((bf16[16,112,128]{2,1,0:T(8,128)(2,1)}), bf16[16,112,128]{2,1,0:T(8,128)(2,1)S(1)}, u32[]{:S(2)}, u32[]{:S(2)}) async-start(bf16[16,112,128]{2,1,0:T(8,128)(2,1)} %pack_strip.3), calls=%async_computation | async-start | bytes 917504 | tf_op jit(solution)/shard_map/all_to_all | solution.py:532
  33.0 0.9 copy-start.8
  45.2 0.9 copy-start.5
  46.0 0.8 copy-start.9
  46.8 1.1 %copy-start.6 = (f32[784,192]{1,0:T(8,128)S(1)}, f32[784,192]{1,0:T(8,128)}, u32[]{:S(2)}) copy-start(f32[784,192]{1,0:T(8,128)} %copy-done.5) | copy-start | bytes 1806340
  48.0 0.9 copy-start.7
  60.4 28.6 %copy-start.10 = (bf16[16,112,128]{2,1,0:T(8,128)(2,1)S(1)}, bf16[16,112,128]{2,1,0:T(8,128)(2,1)}, u32[]{:S(2)}) copy-start(bf16[16,112,128]{2,1,0:T(8,128)(2,1)} %copy-done.9) | copy-start | bytes 1376260
  89.1 0.9 copy-start.1
  90.0 19.8 %all-to-all-start.4 = ((bf16[16,208,128]{2,1,0:T(8,128)(2,1)}), bf16[16,208,128]{2,1,0:T(8,128)(2,1)S(1)}, u32[]{:S(2)}, u32[]{:S(2)}) async-start(bf16[16,208,128]{2,1,0:T(8,128)(2,1)} %copy-done.1), calls=%async_computation.4 | async-start | bytes 1703936 | tf_op jit(solution)/shard_map/all_to_all | solution.py:532
